TPU v7x, 32 devices: a whole 2x2x4 slice. The times are simulated.
32 devices in a mesh: ep: 8 (over z, y), dp: 4 (over x, core).
Axes of the slice: x: 2, y: 2, z: 4, core: 2. Of those that a mesh axis runs over, the one named last changes fastest.
Arguments:
- layer_input: bfloat16 [4096, 2048], P(('ep', 'dp')), may hold values from -6 to 6
- grad_out: bfloat16 [4096, 2048], P(('ep', 'dp')), may hold values from -6 to 6
- attn_gain: bfloat16 [2048], P(('ep', 'dp')), may hold values from 0.5 to 1.5
- w_q: bfloat16 [2048, 2048], P(('ep', 'dp')), may hold values from -0.125 to 0.125
- w_k: bfloat16 [2048, 2048], P(('ep', 'dp')), may hold values from -0.125 to 0.125
- w_v: bfloat16 [2048, 2048], P(('ep', 'dp')), may hold values from -0.125 to 0.125
- q_gain: bfloat16 [2048], P(('ep', 'dp')), may hold values from 0.5 to 1.5
- k_gain: bfloat16 [2048], P(('ep', 'dp')), may hold values from 0.5 to 1.5
- w_o: bfloat16 [2048, 2048], P(('ep', 'dp')), may hold values from -0.5 to 0.5
- ffn_gain: bfloat16 [2048], P(('ep', 'dp')), may hold values from 0.5 to 1.5
- router: bfloat16 [2048, 64], P(('ep', 'dp')), may hold values from -0.0625 to 0.0625
- w_gate: bfloat16 [64, 2048, 1024], P('ep', None, 'dp'), may hold values from -0.125 to 0.125
- w_up: bfloat16 [64, 2048, 1024], P('ep', None, 'dp'), may hold values from -0.125 to 0.125
- w_down: bfloat16 [64, 1024, 2048], P('ep', 'dp'), may hold values from -0.75 to 0.75
- routes: int32 [4096, 8], P(('ep', 'dp')), may hold values from 0 to 63, all different within a row; in each aligned block of 128 rows (0 to 127, 128 to 255, ...) at most 32 rows name the same one
Outputs:
- output: bfloat16 [4096, 2048], P(('ep', 'dp'))
- grad_input: float32 [4096, 2048], P(('ep', 'dp'))
- grad_attn_gain: float32 [2048], P(('ep', 'dp'))
- grad_w_q: float32 [2048, 2048], P(('ep', 'dp'))
- grad_w_k: float32 [2048, 2048], P(('ep', 'dp'))
- grad_w_v: float32 [2048, 2048], P(('ep', 'dp'))
- grad_q_gain: float32 [2048], P(('ep', 'dp'))
- grad_k_gain: float32 [2048], P(('ep', 'dp'))
- grad_w_o: float32 [2048, 2048], P(('ep', 'dp'))
- grad_ffn_gain: float32 [2048], P(('ep', 'dp'))
- grad_router: float32 [2048, 64], P(('ep', 'dp'))
- grad_w_gate: float32 [64, 2048, 1024], P('ep', None, 'dp')
- grad_w_up: float32 [64, 2048, 1024], P('ep', None, 'dp')
- grad_w_down: float32 [64, 1024, 2048], P('ep', 'dp')
Inputs may be any that keep to these rules, and one draw needn't show every extreme that they name: `routes`: each row names 8 different experts; in each aligned block of 128 rows (the rows of one device) no expert is named by more than 32 rows.
All inputs are finite; a program needn't handle non-finite values.
Results may differ from a plain program's by a relative error of at most 0.02.
Values may be sent and summed in bfloat16 or wider, within the bound.
A program may use at most 448 MiB of HBM per device.

v0:
```python
import jax
import jax.numpy as jnp
from jax import lax
from jax.sharding import PartitionSpec as P

HEADS = 16
HEAD_DIM = 128


EPSILON = 1e-05


def rms_scale(value, gain):
    return value * lax.rsqrt(jnp.mean(value * value, axis=-1, keepdims=True) + EPSILON) * gain


def rotate(value, positions):
    half_dim = value.shape[-1] // 2
    frequency = 10000.0 ** (-jnp.arange(half_dim, dtype=jnp.float32) * 2.0 / value.shape[-1])
    angle_table = positions.astype(jnp.float32)[:, None] * frequency[None, :]
    cosine = jnp.concatenate([jnp.cos(angle_table), jnp.cos(angle_table)], axis=-1)[:, None, :]
    sine_part = jnp.concatenate([jnp.sin(angle_table), jnp.sin(angle_table)], axis=-1)[:, None, :]
    first_half = value[..., :half_dim]
    second_half = value[..., half_dim:]
    turned = jnp.concatenate([-second_half, first_half], axis=-1)
    return value * cosine + turned * sine_part


def swiglu(gate_part, up_part):
    return jax.nn.silu(gate_part) * up_part


def masked_scores(queries, keys, query_pos, score_scale):
    key_pos = jnp.arange(keys.shape[0], dtype=jnp.int32)
    raw_scores = jnp.einsum("qhd,khd->hqk", queries, keys, preferred_element_type=jnp.float32)
    return jnp.where(
        (query_pos[:, None] >= key_pos[None, :])[None], raw_scores * score_scale, -1e30
    )


def attend_forward(queries, keys, values, query_pos, score_scale):
    scores = masked_scores(queries, keys, query_pos, score_scale)
    row_peak = jnp.max(scores, axis=-1, keepdims=True)
    exp_scores = jnp.exp(scores - row_peak)
    row_total = jnp.sum(exp_scores, axis=-1, keepdims=True)
    log_total = row_peak + jnp.log(row_total)
    prob_low = (exp_scores / row_total).astype(jnp.bfloat16)
    attended = jnp.einsum("hqk,khd->qhd", prob_low, values, preferred_element_type=jnp.float32)
    return (attended, log_total)


def attend_backward(queries, keys, values, query_pos, score_scale, log_total, grad_mixed):
    prob_full = jnp.exp(masked_scores(queries, keys, query_pos, score_scale) - log_total)
    prob_again = prob_full.astype(jnp.bfloat16)
    grad_values_part = jnp.einsum(
        "hqk,qhd->khd", prob_again, grad_mixed, preferred_element_type=jnp.float32
    )
    grad_probs = jnp.einsum("qhd,khd->hqk", grad_mixed, values, preferred_element_type=jnp.float32)
    row_delta = jnp.sum(prob_full * grad_probs, axis=-1, keepdims=True)
    grad_scores = (prob_full * (grad_probs - row_delta)).astype(jnp.bfloat16)
    grad_q_rot = (
        jnp.einsum("hqk,khd->qhd", grad_scores, keys, preferred_element_type=jnp.float32)
        * score_scale
    )
    grad_keys_part = (
        jnp.einsum("hqk,qhd->khd", grad_scores, queries, preferred_element_type=jnp.float32)
        * score_scale
    )
    return (grad_q_rot, grad_keys_part, grad_values_part)


def shards(
    layer_input,
    grad_out,
    attn_gain,
    w_q,
    w_k,
    w_v,
    q_gain,
    k_gain,
    w_o,
    ffn_gain,
    router,
    w_gate,
    w_up,
    w_down,
    routes,
):
    tok_rows, feat_width = layer_input.shape
    score_scale = HEAD_DIM ** (-0.5)
    shared = (
        lax.all_gather(attn_gain, ("ep", "dp"), axis=0, tiled=True),
        lax.all_gather(w_q, ("ep", "dp"), axis=0, tiled=True),
        lax.all_gather(w_k, ("ep", "dp"), axis=0, tiled=True),
        lax.all_gather(w_v, ("ep", "dp"), axis=0, tiled=True),
        lax.all_gather(q_gain, ("ep", "dp"), axis=0, tiled=True),
        lax.all_gather(k_gain, ("ep", "dp"), axis=0, tiled=True),
        lax.all_gather(w_o, ("ep", "dp"), axis=0, tiled=True),
        lax.all_gather(ffn_gain, ("ep", "dp"), axis=0, tiled=True),
        lax.all_gather(router, ("ep", "dp"), axis=0, tiled=True),
    )
    (
        full_attn_gain,
        full_q,
        full_k,
        full_v,
        full_q_gain,
        full_k_gain,
        full_o,
        full_ffn_gain,
        full_router,
    ) = shared
    expert_full = (
        lax.all_gather(w_gate, "dp", axis=2, tiled=True),
        lax.all_gather(w_up, "dp", axis=2, tiled=True),
        lax.all_gather(w_down, "dp", axis=1, tiled=True),
    )
    gate_full, up_full, down_full = expert_full
    inputs = layer_input.astype(jnp.float32)
    normed_f, norm_back = jax.vjp(rms_scale, inputs, full_attn_gain.astype(jnp.float32))
    normed = normed_f.astype(jnp.bfloat16)
    q_raw = jnp.dot(normed, full_q, preferred_element_type=jnp.float32)
    k_raw = jnp.dot(normed, full_k, preferred_element_type=jnp.float32)
    v_low = jnp.dot(normed, full_v, preferred_element_type=jnp.float32).astype(jnp.bfloat16)
    positions = lax.axis_index("dp") * tok_rows + jnp.arange(tok_rows, dtype=jnp.int32)

    def norm_rope(value, gain):
        return rotate(rms_scale(value, gain).reshape(tok_rows, HEADS, HEAD_DIM), positions)

    q_rot_f, query_back = jax.vjp(norm_rope, q_raw, full_q_gain.astype(jnp.float32))
    k_rot_f, key_back = jax.vjp(norm_rope, k_raw, full_k_gain.astype(jnp.float32))
    queries = q_rot_f.astype(jnp.bfloat16)
    key_rot = k_rot_f.astype(jnp.bfloat16)
    all_keys, all_values = (
        lax.all_gather(key_rot, "dp", axis=0, tiled=True),
        lax.all_gather(v_low.reshape(tok_rows, HEADS, HEAD_DIM), "dp", axis=0, tiled=True),
    )
    attended, log_total = attend_forward(queries, all_keys, all_values, positions, score_scale)
    mixed_low = attended.reshape(tok_rows, feat_width).astype(jnp.bfloat16)
    attn_out = jnp.dot(mixed_low, full_o, preferred_element_type=jnp.float32)
    residual = inputs + attn_out
    normed2_f, ffn_back = jax.vjp(rms_scale, residual, full_ffn_gain.astype(jnp.float32))
    normed2 = normed2_f.astype(jnp.bfloat16)
    logits = jnp.dot(normed2, full_router, preferred_element_type=jnp.float32)
    experts = logits.shape[1]
    top_count = routes.shape[1]
    picked_mask = routes[:, :, None] == jnp.arange(experts, dtype=jnp.int32)[None, None, :]

    def gate_softmax(logit_values):
        chosen = jnp.sum(jnp.where(picked_mask, logit_values[:, None, :], 0.0), axis=-1)
        return jax.nn.softmax(chosen, axis=-1)

    gate_values, gate_back = jax.vjp(gate_softmax, logits)
    expert_hits = jnp.sum(picked_mask.astype(jnp.int32), axis=1)
    hits_before = jnp.cumsum(expert_hits, axis=0) - expert_hits
    slot_index = jnp.sum(jnp.where(picked_mask, hits_before[:, None, :], 0), axis=-1)
    capacity = 2 * tok_rows * top_count // experts
    slot_target = routes * capacity + slot_index
    slot_count = experts * capacity
    slot_table = jnp.sum(
        (slot_target[None, :, :] == jnp.arange(slot_count, dtype=jnp.int32)[:, None, None]).astype(
            jnp.bfloat16
        ),
        axis=2,
    )
    dispatch = jnp.dot(slot_table, normed2, preferred_element_type=jnp.float32).astype(jnp.bfloat16)
    received = lax.all_to_all(
        dispatch.reshape(experts, capacity, feat_width),
        "ep",
        split_axis=0,
        concat_axis=1,
        tiled=True,
    )
    gate_part = jnp.einsum("erd,edf->erf", received, gate_full, preferred_element_type=jnp.float32)
    up_part = jnp.einsum("erd,edf->erf", received, up_full, preferred_element_type=jnp.float32)
    hidden, swiglu_back = jax.vjp(swiglu, gate_part, up_part)
    hidden_low = hidden.astype(jnp.bfloat16)
    expert_out = jnp.einsum(
        "erf,efd->erd", hidden_low, down_full, preferred_element_type=jnp.float32
    ).astype(jnp.bfloat16)
    returned = lax.all_to_all(expert_out, "ep", split_axis=1, concat_axis=0, tiled=True)
    picked_rows = jnp.take(returned.reshape(slot_count, feat_width), slot_target, axis=0).astype(
        jnp.float32
    )
    expert_sum = jnp.sum(gate_values[:, :, None] * picked_rows, axis=1)
    output = (residual + expert_sum).astype(jnp.bfloat16)
    grad_y = grad_out.astype(jnp.float32)
    grad_gates = jnp.sum(grad_y[:, None, :] * picked_rows, axis=-1)
    grad_logits = gate_back(grad_gates)[0].astype(jnp.bfloat16)
    slot_grads = (gate_values[:, :, None] * grad_y[:, None, :]).reshape(-1, feat_width)
    grad_buffer = (
        jnp.zeros((slot_count, feat_width), jnp.float32).at[slot_target.reshape(-1)].set(slot_grads)
    )
    grad_eout = lax.all_to_all(
        grad_buffer.astype(jnp.bfloat16).reshape(experts, capacity, feat_width),
        "ep",
        split_axis=0,
        concat_axis=1,
        tiled=True,
    )
    grad_hidden = jnp.einsum(
        "erd,efd->erf", grad_eout, down_full, preferred_element_type=jnp.float32
    )
    grad_down = jnp.einsum(
        "erf,erd->efd", hidden_low, grad_eout, preferred_element_type=jnp.float32
    )
    grad_gpart, grad_upart = swiglu_back(grad_hidden)
    gpart_low = grad_gpart.astype(jnp.bfloat16)
    upart_low = grad_upart.astype(jnp.bfloat16)
    grad_gate_w = jnp.einsum(
        "erd,erf->edf", received, gpart_low, preferred_element_type=jnp.float32
    )
    grad_up_w = jnp.einsum("erd,erf->edf", received, upart_low, preferred_element_type=jnp.float32)
    grad_copy = jnp.einsum(
        "erf,edf->erd", gpart_low, gate_full, preferred_element_type=jnp.float32
    ) + jnp.einsum("erf,edf->erd", upart_low, up_full, preferred_element_type=jnp.float32)
    grad_back = lax.all_to_all(
        grad_copy.astype(jnp.bfloat16), "ep", split_axis=1, concat_axis=0, tiled=True
    )
    grad_rows = jnp.take(grad_back.reshape(slot_count, feat_width), slot_target, axis=0).astype(
        jnp.float32
    )
    grad_normed2 = jnp.sum(grad_rows, axis=1) + jnp.einsum(
        "te,de->td", grad_logits, full_router, preferred_element_type=jnp.float32
    )
    grad_router = jnp.einsum("td,te->de", normed2, grad_logits, preferred_element_type=jnp.float32)
    grad_resid_norm, grad_ffn_gain = ffn_back(grad_normed2)
    grad_residual = grad_y + grad_resid_norm
    grad_attn_out = grad_residual.astype(jnp.bfloat16)
    expert_grads = (
        lax.psum_scatter(
            grad_gate_w.astype(jnp.bfloat16), "dp", scatter_dimension=2, tiled=True
        ).astype(jnp.float32),
        lax.psum_scatter(
            grad_up_w.astype(jnp.bfloat16), "dp", scatter_dimension=2, tiled=True
        ).astype(jnp.float32),
        lax.psum_scatter(
            grad_down.astype(jnp.bfloat16), "dp", scatter_dimension=1, tiled=True
        ).astype(jnp.float32),
    )
    grad_w_o = jnp.einsum("td,te->de", mixed_low, grad_attn_out, preferred_element_type=jnp.float32)
    grad_mixed = jnp.einsum("te,de->td", grad_attn_out, full_o, preferred_element_type=jnp.float32)
    grad_mixed = grad_mixed.astype(jnp.bfloat16).reshape(tok_rows, HEADS, HEAD_DIM)
    grad_q_rot, grad_keys_part, grad_values_part = attend_backward(
        queries, all_keys, all_values, positions, score_scale, log_total, grad_mixed
    )
    grad_k_rot, grad_values = (
        lax.psum_scatter(
            grad_keys_part.astype(jnp.bfloat16), "dp", scatter_dimension=0, tiled=True
        ).astype(jnp.float32),
        lax.psum_scatter(
            grad_values_part.astype(jnp.bfloat16), "dp", scatter_dimension=0, tiled=True
        ).astype(jnp.float32),
    )
    grad_q_raw, grad_q_gain = query_back(grad_q_rot)
    grad_k_raw, grad_k_gain = key_back(grad_k_rot)
    q_grad_low = grad_q_raw.astype(jnp.bfloat16)
    k_grad_low = grad_k_raw.astype(jnp.bfloat16)
    v_grad_low = grad_values.reshape(tok_rows, feat_width).astype(jnp.bfloat16)
    grad_w_q = jnp.einsum("td,te->de", normed, q_grad_low, preferred_element_type=jnp.float32)
    grad_w_k = jnp.einsum("td,te->de", normed, k_grad_low, preferred_element_type=jnp.float32)
    grad_w_v = jnp.einsum("td,te->de", normed, v_grad_low, preferred_element_type=jnp.float32)
    grad_normed = (
        jnp.einsum("te,de->td", q_grad_low, full_q, preferred_element_type=jnp.float32)
        + jnp.einsum("te,de->td", k_grad_low, full_k, preferred_element_type=jnp.float32)
        + jnp.einsum("te,de->td", v_grad_low, full_v, preferred_element_type=jnp.float32)
    )
    grad_input_norm, grad_attn_gain = norm_back(grad_normed)
    grad_input = grad_residual + grad_input_norm
    summed = (
        lax.psum_scatter(grad_attn_gain, ("ep", "dp"), scatter_dimension=0, tiled=True),
        lax.psum_scatter(grad_w_q, ("ep", "dp"), scatter_dimension=0, tiled=True),
        lax.psum_scatter(grad_w_k, ("ep", "dp"), scatter_dimension=0, tiled=True),
        lax.psum_scatter(grad_w_v, ("ep", "dp"), scatter_dimension=0, tiled=True),
        lax.psum_scatter(grad_q_gain, ("ep", "dp"), scatter_dimension=0, tiled=True),
        lax.psum_scatter(grad_k_gain, ("ep", "dp"), scatter_dimension=0, tiled=True),
        lax.psum_scatter(grad_w_o, ("ep", "dp"), scatter_dimension=0, tiled=True),
        lax.psum_scatter(grad_ffn_gain, ("ep", "dp"), scatter_dimension=0, tiled=True),
        lax.psum_scatter(grad_router, ("ep", "dp"), scatter_dimension=0, tiled=True),
    )
    return (
        output,
        grad_input,
        summed[0],
        summed[1],
        summed[2],
        summed[3],
        summed[4],
        summed[5],
        summed[6],
        summed[7],
        summed[8],
        expert_grads[0],
        expert_grads[1],
        expert_grads[2],
    )


def solution(mesh):
    in_specs = (
        P(("ep", "dp"), None),
        P(("ep", "dp"), None),
        P(("ep", "dp")),
        P(("ep", "dp"), None),
        P(("ep", "dp"), None),
        P(("ep", "dp"), None),
        P(("ep", "dp")),
        P(("ep", "dp")),
        P(("ep", "dp"), None),
        P(("ep", "dp")),
        P(("ep", "dp"), None),
        P("ep", None, "dp"),
        P("ep", None, "dp"),
        P("ep", "dp", None),
        P(("ep", "dp"), None),
    )
    out_specs = (
        P(("ep", "dp"), None),
        P(("ep", "dp"), None),
        P(("ep", "dp")),
        P(("ep", "dp"), None),
        P(("ep", "dp"), None),
        P(("ep", "dp"), None),
        P(("ep", "dp")),
        P(("ep", "dp")),
        P(("ep", "dp"), None),
        P(("ep", "dp")),
        P(("ep", "dp"), None),
        P("ep", None, "dp"),
        P("ep", None, "dp"),
        P("ep", "dp", None),
    )
    return jax.shard_map(shards, mesh=mesh, in_specs=in_specs, out_specs=out_specs, check_vma=False)
```

profile of v0, /device:TPU:0, one launch (start us, length us, event | category | flops | bytes accessed | tf_op | source)
XLA Modules:
  0.0 3166.8 jit_solution(15129586549102910537)
XLA Ops:
  12.9 42.6 %all-reduce.13 = (bf16[2048]{0:T(1024)(128)(2,1)S(1)}, bf16[2048]{0:T(1024)(128)(2,1)S(1)}, bf16[2048]{0:T(1024)(128)(2,1)S(1)}, bf16[2048]{0:T(1024)(128)(2,1)S(1)}) all-reduce(bf16[2048]{0:T(1024)(128)(2,1)S(1)} %dynamic-update-slice, bf16[2048]{0:T(1024)(128)(2,1)S(1)} %dynamic-update-slice.1, ...), channel_id=1, replica_groups=mesh['ep'=8,'dp'=4] {'ep','dp'}, use_global_device_ids=true, to_apply=%add.4 | all-reduce | flops 8192 | bytes 32768
  57.9 33.4 %all-gather.16.cloned.1.call-done = bf16[2048,2048]{1,0:T(8,128)(2,1)} async-done(((bf16[64,2048]{1,0:T(8,128)(2,1)}), bf16[2048,2048]{1,0:T(8,128)(2,1)}) %all-gather.16.cloned.1.call-update) | async-done | bytes 8388624 | tf_op jit(solution)/shard_map/all_gather | solution.py:94
  96.4 73.9 %all-gather.14.cloned.1.call-done = bf16[2048,2048]{1,0:T(8,128)(2,1)} async-done(((bf16[64,2048]{1,0:T(8,128)(2,1)}), bf16[2048,2048]{1,0:T(8,128)(2,1)}) %all-gather.14.cloned.1.call-update) | async-done | bytes 8388624 | tf_op jit(solution)/shard_map/all_gather | solution.py:93
  178.3 70.9 %all-gather.10.cloned.1.call-done = bf16[2048,2048]{1,0:T(8,128)(2,1)} async-done(((bf16[64,2048]{1,0:T(8,128)(2,1)}), bf16[2048,2048]{1,0:T(8,128)(2,1)}) %all-gather.10.cloned.1.call-update) | async-done | bytes 8388624 | tf_op jit(solution)/shard_map/all_gather | solution.py:95
  301.1 76.4 %all-gather.20.cloned.1.call-done = bf16[2048,2048]{1,0:T(8,128)(2,1)} async-done(((bf16[64,2048]{1,0:T(8,128)(2,1)}), bf16[2048,2048]{1,0:T(8,128)(2,1)}) %all-gather.20.cloned.1.call-update) | async-done | bytes 8388624 | tf_op jit(solution)/shard_map/all_gather | solution.py:98
  396.9 196.9 %all_gather.52 = bf16[2048,64]{1,0:T(8,128)(2,1)S(1)} all-gather(bf16[64,64]{1,0:T(8,128)(2,1)S(1)} %copy-done.54), channel_id=1, replica_groups=mesh['ep'=8,'dp'=4] {'ep','dp'}, dimensions={0}, use_global_device_ids=true | all-gather | bytes 270336 | tf_op jit(solution)/shard_map/all_gather | solution.py:100
  645.9 176.5 %all-to-all-done.2 = bf16[64,32,2048]{2,1,0:T(8,128)(2,1)} async-done(((bf16[64,32,2048]{2,1,0:T(8,128)(2,1)}), bf16[64,32,2048]{2,1,0:T(8,128)(2,1)}, u32[]{:S(2)}, u32[]{:S(2)}) %all-to-all-start.2) | async-done | bytes 8388640 | tf_op jit(solution)/shard_map/all_to_all | solution.py:194
  831.5 23.3 fusion.67
  854.8 23.3 fusion.68
  878.0 121.3 %all-gather.26.cloned.1.call-done = bf16[8,1024,2048]{2,1,0:T(8,128)(2,1)} async-done(((bf16[8,256,2048]{2,1,0:T(8,128)(2,1)}), bf16[8,1024,2048]{2,1,0:T(8,128)(2,1)}) %all-gather.26.cloned.1.call-update) | async-done | bytes 33554448 | tf_op jit(solution)/shard_map/all_gather | solution.py:116
  999.4 25.8 multiply_convert_fusion
  1060.5 20.3 fusion.69
  1080.7 22.4 add_convert_fusion
  1114.5 129.6 %all-to-all-done.1 = bf16[8,256,2048]{2,0,1:T(8,128)(2,1)} async-done(((bf16[8,256,2048]{2,0,1:T(8,128)(2,1)}), bf16[8,256,2048]{2,0,1:T(8,128)(2,1)}, u32[]{:S(2)}, u32[]{:S(2)}) %all-to-all-start.1) | async-done | bytes 8388640 | tf_op jit(solution)/shard_map/all_to_all | solution.py:181
  1262.2 169.5 %all-to-all-done.3 = bf16[8,256,2048]{2,0,1:T(8,128)(2,1)} async-done(((bf16[8,256,2048]{2,0,1:T(8,128)(2,1)}), bf16[8,256,2048]{2,0,1:T(8,128)(2,1)}, u32[]{:S(2)}, u32[]{:S(2)}) %all-to-all-start.3) | async-done | bytes 8388640 | tf_op jit(solution)/shard_map/all_to_all | solution.py:217
  1643.3 39.2 %all-reduce.12 = (f32[2048]{0:T(1024)S(1)}, f32[2048]{0:T(1024)S(1)}, f32[2048]{0:T(1024)S(1)}, f32[2048]{0:T(1024)S(1)}) all-reduce(f32[2048]{0:T(1024)S(1)} %get-tuple-element.23, f32[2048]{0:T(1024)S(1)} %get-tuple-element.21, f32[2048]{0:T(1024)S(1)} %get-tuple-element.19, ...), channel_id=4, replica_groups=mesh['ep'=8,'dp'=4] {'ep','dp'}, use_global_device_ids=true, to_apply=%region_27.29.clone | all-reduce | flops 8192 | bytes 65536
  1686.2 117.8 %reduce-scatter.25.cloned.1.call-done = bf16[8,2048,256]{2,1,0:T(8,128)(2,1)} async-done(((bf16[8,2048,1024]{2,1,0:T(8,128)(2,1)}), bf16[8,2048,256]{2,1,0:T(8,128)(2,1)}) %reduce-scatter.25.cloned.1.call-update) | async-done | bytes 8388624 | tf_op jit(solution)/shard_map/reduce_scatter | solution.py:231
  1816.5 224.9 %reduce-scatter.27.cloned.1.call-done = bf16[8,2048,256]{2,1,0:T(8,128)(2,1)} async-done(((bf16[8,2048,1024]{2,1,0:T(8,128)(2,1)}), bf16[8,2048,256]{2,1,0:T(8,128)(2,1)}) %reduce-scatter.27.cloned.1.call-update) | async-done | bytes 8388624 | tf_op jit(solution)/shard_map/reduce_scatter | solution.py:234
  2054.1 224.6 %reduce-scatter.29.cloned.1.call-done = bf16[8,256,2048]{2,1,0:T(8,128)(2,1)} async-done(((bf16[8,1024,2048]{2,1,0:T(8,128)(2,1)}), bf16[8,256,2048]{2,1,0:T(8,128)(2,1)}) %reduce-scatter.29.cloned.1.call-update) | async-done | bytes 8388624 | tf_op jit(solution)/shard_map/reduce_scatter | solution.py:237
  2290.4 125.8 %reduce-scatter.23.cloned.1.call-done = f32[64,64]{1,0:T(8,128)} async-done(((f32[2048,64]{1,0:T(8,128)}), f32[64,64]{1,0:T(8,128)}) %reduce-scatter.23.cloned.1.call-update) | async-done | bytes 16400 | tf_op jit(solution)/shard_map/reduce_scatter | solution.py:279
  2416.3 181.6 %reduce-scatter.15.cloned.1.call-done = f32[64,2048]{1,0:T(8,128)} async-done(((f32[2048,2048]{1,0:T(8,128)}), f32[64,2048]{1,0:T(8,128)}) %reduce-scatter.15.cloned.1.call-update) | async-done | bytes 524304 | tf_op jit(solution)/shard_map/reduce_scatter | solution.py:272
  2597.9 187.4 %reduce-scatter.21.cloned.1.call-done = f32[64,2048]{1,0:T(8,128)} async-done(((f32[2048,2048]{1,0:T(8,128)}), f32[64,2048]{1,0:T(8,128)}) %reduce-scatter.21.cloned.1.call-update) | async-done | bytes 524304 | tf_op jit(solution)/shard_map/reduce_scatter | solution.py:277
  2785.3 187.4 %reduce-scatter.17.cloned.1.call-done = f32[64,2048]{1,0:T(8,128)} async-done(((f32[2048,2048]{1,0:T(8,128)}), f32[64,2048]{1,0:T(8,128)}) %reduce-scatter.17.cloned.1.call-update) | async-done | bytes 524304 | tf_op jit(solution)/shard_map/reduce_scatter | solution.py:273
  2972.7 187.3 %reduce-scatter.19.cloned.1.call-done = f32[64,2048]{1,0:T(8,128)} async-done(((f32[2048,2048]{1,0:T(8,128)}), f32[64,2048]{1,0:T(8,128)}) %reduce-scatter.19.cloned.1.call-update) | async-done | bytes 524304 | tf_op jit(solution)/shard_map/reduce_scatter | solution.py:274
  (328 shorter events, 469.1 us)
Async XLA Ops:
  7.2 84.2 %all-gather.16.cloned.1.call-start = ((), (), s32[]{:S(2)}) async-start(), calls=%async_computation.17 | async-start | bytes 8650752 | tf_op jit(solution)/shard_map/all_gather | solution.py:94
  7.9 162.4 %all-gather.14.cloned.1.call-start = ((), (), s32[]{:S(2)}) async-start(), calls=%async_computation.16 | async-start | bytes 8650752 | tf_op jit(solution)/shard_map/all_gather | solution.py:93
  8.7 240.6 %all-gather.10.cloned.1.call-start = ((), (), s32[]{:S(2)}) async-start(), calls=%async_computation.14 | async-start | bytes 8650752 | tf_op jit(solution)/shard_map/all_gather | solution.py:95
  9.4 263.0 %all-gather.18.cloned.1.call-start = ((), (), s32[]{:S(2)}) async-start(), calls=%async_computation.18 | async-start | bytes 2621440 | tf_op jit(solution)/shard_map/all_gather | solution.py:135
  178.2 119.0 %all-gather.12.cloned.1.call-start = ((), (), s32[]{:S(2)}) async-start(), calls=%async_computation.15 | async-start | bytes 2621440 | tf_op jit(solution)/shard_map/all_gather | solution.py:136
  255.0 122.5 %all-gather.20.cloned.1.call-start = ((), (), s32[]{:S(2)}) async-start(), calls=%async_computation.19 | async-start | bytes 8650752 | tf_op jit(solution)/shard_map/all_gather | solution.py:98
  255.5 576.0 %all-gather.22.cloned.1.call-start = ((), (), s32[]{:S(2)}) async-start(), calls=%async_computation.20 | async-start | bytes 41943040 | tf_op jit(solution)/shard_map/all_gather | solution.py:114
  256.3 598.5 %all-gather.24.cloned.1.call-start = ((), (), s32[]{:S(2)}) async-start(), calls=%async_computation.21 | async-start | bytes 41943040 | tf_op jit(solution)/shard_map/all_gather | solution.py:115
  257.0 742.3 %all-gather.26.cloned.1.call-start = ((), (), s32[]{:S(2)}) async-start(), calls=%async_computation.22 | async-start | bytes 41943040 | tf_op jit(solution)/shard_map/all_gather | solution.py:116
  391.3 231.7 %all-to-all-start = ((bf16[64,32,2048]{2,1,0:T(8,128)(2,1)}), bf16[64,32,2048]{2,1,0:T(8,128)(2,1)}, u32[]{:S(2)}, u32[]{:S(2)}) async-start(bf16[64,32,2048]{2,1,0:T(8,128)(2,1)} %bitcast.136), calls=%async_computation | async-start | bytes 16777216 | tf_op jit(solution)/shard_map/all_to_all | solution.py:167
  396.8 216.6 %copy-start.10 = (f32[128,2048]{1,0:T(8,128)}, f32[128,2048]{1,0:T(8,128)S(1)}, u32[]{:S(2)}) copy-start(f32[128,2048]{1,0:T(8,128)S(1)} %convert_element_type.172) | copy-start | bytes 3145732
  623.1 199.4 %all-to-all-start.2 = ((bf16[64,32,2048]{2,1,0:T(8,128)(2,1)}), bf16[64,32,2048]{2,1,0:T(8,128)(2,1)}, u32[]{:S(2)}, u32[]{:S(2)}) async-start(bf16[64,32,2048]{2,1,0:T(8,128)(2,1)} %bitcast.137), calls=%async_computation.2 | async-start | bytes 16777216 | tf_op jit(solution)/shard_map/all_to_all | solution.py:194
  1055.0 189.1 %all-to-all-start.1 = ((bf16[8,256,2048]{2,0,1:T(8,128)(2,1)}), bf16[8,256,2048]{2,0,1:T(8,128)(2,1)}, u32[]{:S(2)}, u32[]{:S(2)}) async-start(bf16[8,256,2048]{2,0,1:T(8,128)(2,1)} %copy.202), calls=%async_computation.1 | async-start | bytes 16777216 | tf_op jit(solution)/shard_map/all_to_all | solution.py:181
  1244.0 187.6 %all-to-all-start.3 = ((bf16[8,256,2048]{2,0,1:T(8,128)(2,1)}), bf16[8,256,2048]{2,0,1:T(8,128)(2,1)}, u32[]{:S(2)}, u32[]{:S(2)}) async-start(bf16[8,256,2048]{2,0,1:T(8,128)(2,1)} %copy.209), calls=%async_computation.3 | async-start | bytes 16777216 | tf_op jit(solution)/shard_map/all_to_all | solution.py:217
  1249.0 354.5 %reduce-scatter.13.cloned.1.call-start = ((), (), s32[]{:S(2)}) async-start(), calls=%async_computation.23 | async-start | bytes 2621440 | tf_op jit(solution)/shard_map/reduce_scatter | solution.py:248
  1501.3 116.3 %reduce-scatter.31.cloned.1.call-start = ((), (), s32[]{:S(2)}) async-start(), calls=%async_computation.32 | async-start | bytes 2621440 | tf_op jit(solution)/shard_map/convert_element_type | solution.py:259
  1509.8 294.1 %reduce-scatter.25.cloned.1.call-start = ((), (), s32[]{:S(2)}) async-start(), calls=%async_computation.29 | async-start | bytes 41943040 | tf_op jit(solution)/shard_map/reduce_scatter | solution.py:231
  1527.7 513.7 %reduce-scatter.27.cloned.1.call-start = ((), (), s32[]{:S(2)}) async-start(), calls=%async_computation.30 | async-start | bytes 41943040 | tf_op jit(solution)/shard_map/reduce_scatter | solution.py:234
  1546.2 732.5 %reduce-scatter.29.cloned.1.call-start = ((), (), s32[]{:S(2)}) async-start(), calls=%async_computation.31 | async-start | bytes 41943040 | tf_op jit(solution)/shard_map/reduce_scatter | solution.py:237
  1564.7 851.6 %reduce-scatter.23.cloned.1.call-start = ((), (), s32[]{:S(2)}) async-start(), calls=%async_computation.28 | async-start | bytes 1081344 | tf_op jit(solution)/shard_map/reduce_scatter | solution.py:279
  1575.5 1022.4 %reduce-scatter.15.cloned.1.call-start = ((), (), s32[]{:S(2)}) async-start(), calls=%async_computation.24 | async-start | bytes 17301504 | tf_op jit(solution)/shard_map/reduce_scatter | solution.py:272
  1589.8 1195.5 %reduce-scatter.21.cloned.1.call-start = ((), (), s32[]{:S(2)}) async-start(), calls=%async_computation.27 | async-start | bytes 17301504 | tf_op jit(solution)/shard_map/reduce_scatter | solution.py:277
  1603.2 1369.5 %reduce-scatter.17.cloned.1.call-start = ((), (), s32[]{:S(2)}) async-start(), calls=%async_computation.25 | async-start | bytes 17301504 | tf_op jit(solution)/shard_map/reduce_scatter | solution.py:273
  1617.5 1542.5 %reduce-scatter.19.cloned.1.call-start = ((), (), s32[]{:S(2)}) async-start(), calls=%async_computation.26 | async-start | bytes 17301504 | tf_op jit(solution)/shard_map/reduce_scatter | solution.py:274
  (75 other events, 2999.4 us)
Sparse Core Ops, SparseCore 0:
  10.9 80.4 all-gather.15
  94.2 76.0 all-gather.13
  173.2 76.0 all-gather.9
  251.2 21.1 all-gather.17
  274.4 22.8 all-gather.11
  300.0 77.4 all-gather.19
  379.1 208.8 all-gather.21
  589.5 206.7 all-gather.23
  797.8 201.5 all-gather.25
  1501.4 29.5 reduce-scatter.12
  1533.7 31.4 reduce-scatter.30
  1567.6 236.3 reduce-scatter.24
  1806.5 234.8 reduce-scatter.26
  2043.8 234.8 reduce-scatter.28
  2281.4 134.7 reduce-scatter.22
  2419.1 178.7 reduce-scatter.14
  2600.7 184.5 reduce-scatter.20
  2788.1 184.5 reduce-scatter.16
  2975.7 184.2 reduce-scatter.18
where the time goes:
time: 3180 us; the launch traced here: 3170 us
  waiting for transfers between devices  2320 us (73%)
  matrix products  303 us (10%)
  blocking collectives  279 us (9%)
  local copies, waits for them, and re-layouts  115 us (4%)
  other arithmetic  108 us (3%)
    reduce_scatter x1, waiting for transfers between devices, shards(): lax.psum_scatter(grad_up_w.astype(jnp.bfloat16), 'dp', scatter_dimension=...  225 us
    reduce_scatter x1, waiting for transfers between devices, shards(): lax.psum_scatter(grad_down.astype(jnp.bfloat16), 'dp', scatter_dimension=...  225 us
    all_gather x1, blocking collectives, shards(): lax.all_gather(router, ('ep', 'dp'), axis=0, tiled=True)  197 us
    reduce_scatter x1, waiting for transfers between devices, shards(): lax.psum_scatter(grad_w_k, ('ep', 'dp'), scatter_dimension=0, tiled=True)  187 us
    reduce_scatter x1, waiting for transfers between devices, shards(): lax.psum_scatter(grad_w_o, ('ep', 'dp'), scatter_dimension=0, tiled=True)  187 us
    reduce_scatter x1, waiting for transfers between devices, shards(): lax.psum_scatter(grad_w_v, ('ep', 'dp'), scatter_dimension=0, tiled=True)  187 us
    reduce_scatter x1, waiting for transfers between devices, shards(): lax.psum_scatter(grad_w_q, ('ep', 'dp'), scatter_dimension=0, tiled=True)  182 us
    all_to_all x1, waiting for transfers between devices, shards(): lax.all_to_all(grad_buffer.astype(jnp.bfloat16).reshape(experts, capacity...  177 us
  transfers between devices with their start and end apart: 23, of which 18 were waited for; matrix products, arithmetic and copies ran while one was open for 12% of the time, Pallas kernels for 0%

commit v1 on v0

v1 whole, which is shorter than its diff:
```python
import jax
import jax.numpy as jnp
from jax import lax
from jax.sharding import PartitionSpec as P

HEAD_DIM = 128
EPSILON = 1e-05
BF = jnp.bfloat16
F32 = jnp.float32
AXES = ("ep", "dp")


def dot(left, right):
    return jnp.dot(left, right, preferred_element_type=F32)


def ein(spec, left, right):
    return jnp.einsum(spec, left, right, preferred_element_type=F32)


def inv_rms(value):
    return lax.rsqrt(jnp.mean(value * value, axis=-1, keepdims=True) + EPSILON)


def half_turn(value):
    half = value.shape[-1] // 2
    return jnp.concatenate([-value[..., half:], value[..., :half]], axis=-1)


def half_turn_back(value):
    half = value.shape[-1] // 2
    return jnp.concatenate([value[..., half:], -value[..., :half]], axis=-1)


def build(n_ep, n_dp):
    n_dev = n_ep * n_dp
    group = 2 * n_dp
    n_group = n_dev // group
    rows_of = [[g * group + r for r in range(group)] for g in range(n_group)]
    cols_of = [[g * group + r for g in range(n_group)] for r in range(group)]

    def group_gather(value, axis=0):
        return lax.all_gather(value, AXES, axis=axis, tiled=True, axis_index_groups=rows_of)

    def group_scatter(value):
        return lax.psum_scatter(
            value, AXES, scatter_dimension=0, tiled=True, axis_index_groups=rows_of
        )

    def group_swap(value):
        return lax.all_to_all(value, AXES, 0, 0, tiled=True, axis_index_groups=rows_of)

    def column_gather(value):
        return lax.all_gather(value, AXES, axis=0, tiled=False, axis_index_groups=cols_of)

    def column_scatter(value):
        return lax.psum_scatter(
            value, AXES, scatter_dimension=0, tiled=False, axis_index_groups=cols_of
        )

    def shards(
        layer_input, grad_out, attn_gain, w_q, w_k, w_v, q_gain, k_gain, w_o, ffn_gain,
        router, w_gate, w_up, w_down, routes,
    ):
        rows, width = layer_input.shape
        cols = width // group
        heads = cols // HEAD_DIM
        seqs = 2
        seq_len = rows * n_dp
        scale = HEAD_DIM ** (-0.5)
        own = width // n_dev
        rank = (lax.axis_index("ep") % 2) * n_dp + lax.axis_index("dp")
        local_experts = w_gate.shape[0]
        experts = router.shape[1]
        top = routes.shape[1]
        cap = 2 * rows * top // experts

        qkv = jnp.stack([w_q, w_k, w_v]).reshape(3, own, group, cols).transpose(2, 0, 1, 3)
        qkv = group_swap(qkv)
        qkv = column_gather(qkv)
        qkv = qkv.transpose(2, 0, 1, 3, 4).reshape(3, width, cols)
        wq, wk, wv = qkv[0], qkv[1], qkv[2]
        wo = column_gather(w_o)
        halves = group // n_dp
        return_rank = [(halves * g) % group for g in range(n_group)]
        del return_rank
        full_o = lax.all_gather(w_o, AXES, axis=0, tiled=True)
        wo = lax.dynamic_slice_in_dim(full_o, rank * cols, cols, 0)

        small = jnp.concatenate(
            [jnp.stack([attn_gain, q_gain, k_gain, ffn_gain], axis=1), router], axis=1
        )
        small = lax.all_gather(small, AXES, axis=0, tiled=True)
        full_attn_gain = small[:, 0].astype(F32)
        full_ffn_gain = small[:, 3].astype(F32)
        full_router = small[:, 4:]
        q_gain_own = lax.dynamic_slice_in_dim(small[:, 1], rank * cols, cols, 0).astype(F32)
        k_gain_own = lax.dynamic_slice_in_dim(small[:, 2], rank * cols, cols, 0).astype(F32)

        group_input = group_gather(layer_input).astype(F32)
        normed = (group_input * inv_rms(group_input) * full_attn_gain).astype(BF)
        q_raw, k_raw = dot(normed, wq), dot(normed, wk)
        v_low = dot(normed, wv).astype(BF)
        squares = jnp.stack([jnp.sum(q_raw * q_raw, -1), jnp.sum(k_raw * k_raw, -1)])
        squares = lax.psum(squares, AXES, axis_index_groups=rows_of)
        roots = lax.rsqrt(squares / width + EPSILON)
        q_root, k_root = roots[0][:, None], roots[1][:, None]
        half_dim = HEAD_DIM // 2
        frequency = 10000.0 ** (-jnp.arange(half_dim, dtype=F32) * 2.0 / HEAD_DIM)
        angle = jnp.arange(seq_len, dtype=F32)[:, None] * frequency[None, :]
        cosine = jnp.concatenate([jnp.cos(angle)] * 2, axis=-1)[None, :, None, :]
        sine = jnp.concatenate([jnp.sin(angle)] * 2, axis=-1)[None, :, None, :]
        by_head = (seqs, seq_len, heads, HEAD_DIM)

        def rope(value):
            value = value.reshape(by_head)
            return (value * cosine + half_turn(value) * sine).astype(BF)

        def rope_back(value):
            return (value * cosine + half_turn_back(value * sine)).reshape(seqs * seq_len, cols)

        q_n, k_n = q_raw * q_root, k_raw * k_root
        q_rot, k_rot = rope(q_n * q_gain_own), rope(k_n * k_gain_own)
        values = v_low.reshape(by_head)
        causal = jnp.arange(seq_len)[:, None] >= jnp.arange(seq_len)[None, :]
        scores = jnp.where(causal, ein("bqhd,bkhd->bhqk", q_rot, k_rot) * scale, -1e30)
        probs = jax.nn.softmax(scores, axis=-1)
        probs_low = probs.astype(BF)
        mixed = ein("bhqk,bkhd->bqhd", probs_low, values).astype(BF).reshape(-1, cols)
        attn_out = group_scatter(dot(mixed, wo).astype(BF)).astype(F32)
        residual = layer_input.astype(F32) + attn_out
        res_root = inv_rms(residual)
        res_n = residual * res_root
        normed2 = (res_n * full_ffn_gain).astype(BF)

        logits = dot(normed2, full_router)
        expert_ids = jnp.arange(experts, dtype=jnp.int32)
        picked = routes[:, :, None] == expert_ids
        chosen = jnp.sum(jnp.where(picked, logits[:, None, :], 0.0), axis=-1)
        gates = jax.nn.softmax(chosen, axis=-1)
        gates_dense = jnp.sum(jnp.where(picked, gates[:, :, None], 0.0), axis=1)
        hits = jnp.any(picked, axis=1)

        all_x = lax.all_gather(normed2, AXES, axis=0, tiled=True).reshape(n_dev, rows, width)
        all_g = lax.all_gather(grad_out, AXES, axis=0, tiled=True).reshape(n_dev, rows, width)
        first = lax.axis_index("ep") * local_experts
        all_gates = lax.all_gather(gates_dense, AXES, axis=0, tiled=False)
        all_routes = lax.all_gather(routes, AXES, axis=0, tiled=False)
        local_ids = first + jnp.arange(local_experts, dtype=jnp.int32)
        local_hits = jnp.any(all_routes[..., None] == local_ids, axis=2).astype(jnp.int32)
        before = jnp.cumsum(local_hits, axis=1) - local_hits
        place = jnp.where(local_hits > 0, before, -1)
        table = (
            place.transpose(0, 2, 1)[:, :, None, :]
            == jnp.arange(cap, dtype=jnp.int32)[None, None, :, None]
        )
        table_low = table.astype(BF)
        local_gates = lax.dynamic_slice_in_dim(all_gates, first, local_experts, 2)
        slot_gates = jnp.sum(
            jnp.where(table, local_gates.transpose(0, 2, 1)[:, :, None, :], 0.0), axis=-1
        )
        slot_gates = slot_gates.transpose(1, 0, 2).reshape(local_experts, n_dev * cap, 1)
        slots = (local_experts, n_dev * cap)
        x_rows = ein("best,btd->ebsd", table_low, all_x).astype(BF).reshape(*slots, width)
        g_rows = ein("best,btd->ebsd", table_low, all_g).astype(BF).reshape(*slots, width)
        gate_part = ein("erd,edf->erf", x_rows, w_gate)
        up_part = ein("erd,edf->erf", x_rows, w_up)
        sig = jax.nn.sigmoid(gate_part)
        silu = gate_part * sig
        hidden = silu * up_part
        raw_grad = ein("erd,efd->erf", g_rows, w_down)
        hidden_gated = (slot_gates * hidden).astype(BF)
        slot_gate_grads = jnp.sum(hidden * raw_grad, axis=-1).reshape(local_experts, n_dev, cap)
        grad_hidden = raw_grad * slot_gates
        gpart_low = (grad_hidden * up_part * sig * (1.0 + gate_part * (1.0 - sig))).astype(BF)
        upart_low = (grad_hidden * silu).astype(BF)
        out_rows = ein("erf,efd->erd", hidden_gated, w_down).astype(BF)
        grad_rows = (
            ein("erf,edf->erd", gpart_low, w_gate) + ein("erf,edf->erd", upart_low, w_up)
        ).astype(BF)
        back = (local_experts, n_dev, cap, width)
        out_part = ein("best,ebsd->btd", table_low, out_rows.reshape(back)).astype(BF)
        grad_part = ein("best,ebsd->btd", table_low, grad_rows.reshape(back)).astype(BF)
        grad_w_down = ein("erf,erd->efd", hidden_gated, g_rows)
        grad_w_gate = ein("erd,erf->edf", x_rows, gpart_low)
        grad_w_up = ein("erd,erf->edf", x_rows, upart_low)

        expert_sum = lax.psum_scatter(out_part, AXES, scatter_dimension=0, tiled=True)
        output = (residual + expert_sum[0].astype(F32)).astype(BF)
        grad_n2 = lax.psum_scatter(grad_part, AXES, scatter_dimension=0, tiled=True)[0]

        gate_grads = jnp.sum(
            jnp.where(table, slot_gate_grads.transpose(1, 0, 2)[..., None], 0.0), axis=2
        )
        gate_grads = gate_grads.reshape(n_ep, n_dp, local_experts, rows)
        gate_grads = lax.psum_scatter(gate_grads, "dp", scatter_dimension=1, tiled=False)
        gate_grads = lax.all_to_all(gate_grads, "ep", 0, 0, tiled=True)
        gate_grads = gate_grads.reshape(experts, rows).T
        gate_grads = jnp.where(hits, gate_grads, 0.0)
        weighted = jnp.sum(gates_dense * gate_grads, axis=-1, keepdims=True)
        grad_logits = (gates_dense * (gate_grads - weighted)).astype(BF)

        grad_n2 = grad_n2.astype(F32) + ein("te,de->td", grad_logits, full_router)
        grad_router = ein("td,te->de", normed2, grad_logits)
        grad_y = grad_out.astype(F32)
        grad_ffn_gain = jnp.sum(grad_n2 * res_n, axis=0)
        dn = grad_n2 * full_ffn_gain
        grad_residual = grad_y + res_root * (dn - res_n * jnp.mean(dn * res_n, -1, keepdims=True))

        gao = group_gather(grad_residual.astype(BF))
        grad_wo = ein("td,te->de", mixed, gao)
        grad_mixed = ein("te,de->td", gao, wo).astype(BF).reshape(by_head)
        grad_values = ein("bhqk,bqhd->bkhd", probs_low, grad_mixed)
        grad_probs = ein("bqhd,bkhd->bhqk", grad_mixed, values)
        delta = jnp.sum(probs * grad_probs, axis=-1, keepdims=True)
        grad_scores = (probs * (grad_probs - delta)).astype(BF)
        grad_q_rot = ein("bhqk,bkhd->bqhd", grad_scores, k_rot) * scale
        grad_k_rot = ein("bhqk,bqhd->bkhd", grad_scores, q_rot) * scale
        gq, gk = rope_back(grad_q_rot), rope_back(grad_k_rot)
        grad_q_gain, grad_k_gain = jnp.sum(gq * q_n, axis=0), jnp.sum(gk * k_n, axis=0)
        gq, gk = gq * q_gain_own, gk * k_gain_own
        inner = jnp.stack([jnp.sum(gq * q_n, -1), jnp.sum(gk * k_n, -1)])
        inner = lax.psum(inner, AXES, axis_index_groups=rows_of) / width
        gq = (q_root * (gq - q_n * inner[0][:, None])).astype(BF)
        gk = (k_root * (gk - k_n * inner[1][:, None])).astype(BF)
        gv = grad_values.reshape(-1, cols).astype(BF)
        grad_normed = ein("te,de->td", gq, wq) + ein("te,de->td", gk, wk)
        grad_normed = grad_normed + ein("te,de->td", gv, wv)
        grad_normed = group_scatter(grad_normed.astype(BF)).astype(F32)
        own_input = layer_input.astype(F32)
        in_root = inv_rms(own_input)
        in_n = own_input * in_root
        grad_attn_gain = jnp.sum(grad_normed * in_n, axis=0)
        dn = grad_normed * full_attn_gain
        grad_input = grad_residual + in_root * (
            dn - in_n * jnp.mean(dn * in_n, -1, keepdims=True)
        )
        grad_qkv = jnp.stack(
            [ein("td,te->de", normed, part) for part in (gq, gk, gv)]
        ).astype(BF)
        grad_qkv = grad_qkv.reshape(3, n_group, group, own, cols).transpose(1, 2, 0, 3, 4)
        grad_qkv = column_scatter(grad_qkv)
        grad_qkv = group_swap(grad_qkv).transpose(1, 2, 0, 3).reshape(3, own, width).astype(F32)
        grad_o = jnp.zeros((width, width), BF)
        grad_o = lax.dynamic_update_slice_in_dim(grad_o, grad_wo.astype(BF), rank * cols, 0)
        grad_o = lax.psum_scatter(grad_o, AXES, scatter_dimension=0, tiled=True).astype(F32)

        def spread(part):
            return lax.dynamic_update_slice_in_dim(jnp.zeros((width,), F32), part, rank * cols, 0)

        small_grads = jnp.concatenate(
            [
                jnp.stack(
                    [grad_attn_gain, spread(grad_q_gain), spread(grad_k_gain), grad_ffn_gain],
                    axis=1,
                ),
                grad_router,
            ],
            axis=1,
        )
        small_grads = lax.psum_scatter(small_grads, AXES, scatter_dimension=0, tiled=True)
        return (
            output, grad_input, small_grads[:, 0], grad_qkv[0], grad_qkv[1], grad_qkv[2],
            small_grads[:, 1], small_grads[:, 2], grad_o, small_grads[:, 3], small_grads[:, 4:],
            grad_w_gate, grad_w_up, grad_w_down,
        )

    return shards


def solution(mesh):
    row, vec = P(("ep", "dp"), None), P(("ep", "dp"))
    wide, deep = P("ep", None, "dp"), P("ep", "dp", None)
    in_specs = (
        row, row, vec, row, row, row, vec, vec, row, vec, row, wide, wide, deep, row,
    )
    out_specs = (
        row, row, vec, row, row, row, vec, vec, row, vec, row, wide, wide, deep,
    )
    shards = build(mesh.shape["ep"], mesh.shape["dp"])
    return jax.shard_map(shards, mesh=mesh, in_specs=in_specs, out_specs=out_specs, check_vma=False)
```

time: 3180 us -> 1710 us (0.54)
  waiting for transfers between devices: 2320 us -> 1040 us
  blocking collectives: 279 us -> 131 us
  other arithmetic: 108 us -> 59.1 us
  matrix products: 303 us -> 340 us
    reduce_scatter x9 -> x5, waiting for transfers between devices: 1440 us -> 516 us  [the longest x1 167 us: shards(): lax.psum_scatter(grad_part, AXES, scatter_dimension=0, tiled=True)[0]]
    all_to_all x4 -> x2, waiting for transfers between devices: 476 us -> 10.8 us  [the longest x1 6.71 us: shards(): gate_grads = lax.all_to_all(gate_grads, 'ep', 0, 0, tiled=True)]
    unnamed x19 -> x18, waiting for transfers between devices: 4.68 us -> 212 us
    all_gather x1 -> x2, blocking collectives: 197 us -> 85.2 us  [the longest x1 44.1 us: shards(): small = lax.all_gather(small, AXES, axis=0, tiled=True)]
    all_gather x9 -> x7, waiting for transfers between devices: 399 us -> 304 us  [the longest x1 116 us: shards(): lax.all_gather(grad_out, AXES, axis=0, tiled=True)]
    unnamed x2 -> x0, blocking collectives: 81.8 us -> none
    all_to_all x4 -> x0, local copies, waits for them, and re-layouts: 42.2 us -> none  [the longest x1 12.3 us: shards(): lax.all_to_all(expert_out, 'ep', split_axis=1, concat_axis=0, tiled=True)]
    dot_general x31 -> x33, matrix products: 303 us -> 335 us  [the longest x28 324 us: ein(): return jnp.einsum(spec, left, right, preferred_element_type=F32)]
  transfers between devices with their start and end apart: 23 -> 17, of which waited for: 18 -> 16; matrix products, arithmetic and copies ran while one was open for 12% -> 20% of each run, Pallas kernels for 0% -> 0%
where the time goes in v1:
time: 1710 us; the launch traced here: 1700 us
  waiting for transfers between devices  1040 us (61%)
  matrix products  340 us (20%)
  blocking collectives  131 us (8%)
  local copies, waits for them, and re-layouts  106 us (6%)
  other arithmetic  59.1 us (3%)
    dot_general x28, matrix products, ein(): return jnp.einsum(spec, left, right, preferred_element_type=F32)  324 us
    unnamed x18, waiting for transfers between devices  212 us
    reduce_scatter x1, waiting for transfers between devices, shards(): lax.psum_scatter(grad_part, AXES, scatter_dimension=0, tiled=True)[0]  167 us
    reduce_scatter x1, waiting for transfers between devices, shards(): lax.psum_scatter(out_part, AXES, scatter_dimension=0, tiled=True)  154 us
    reduce_scatter x1, waiting for transfers between devices, shards(): lax.psum_scatter(grad_o, AXES, scatter_dimension=0, tiled=True).astype(F32)  142 us
    all_gather x1, waiting for transfers between devices, shards(): lax.all_gather(grad_out, AXES, axis=0, tiled=True)  116 us
    all_gather x2, waiting for transfers between devices, group_gather(): lax.all_gather(value, AXES, axis=axis, tiled=True, axis_index_groups=rows...  73.9 us
    all_gather x1, waiting for transfers between devices, shards(): lax.all_gather(normed2, AXES, axis=0, tiled=True)  70.2 us
  transfers between devices with their start and end apart: 17, of which 16 were waited for; matrix products, arithmetic and copies ran while one was open for 20% of the time, Pallas kernels for 0%

profile of v1, /device:TPU:0, one launch (start us, length us, event | category | flops | bytes accessed | tf_op | source)
XLA Modules:
  0.0 1702.6 jit_solution(4768153246919719350)
XLA Ops:
  31.7 44.1 %all_gather.37 = bf16[2048,68]{1,0:T(8,128)(2,1)S(1)} all-gather(bf16[64,68]{1,0:T(8,128)(2,1)S(1)} %concatenate.27), channel_id=1, replica_groups=mesh['ep'=8,'dp'=4] {'ep','dp'}, dimensions={0}, use_global_device_ids=true | all-gather | bytes 287232 | tf_op jit(solution)/shard_map/all_gather | solution.py:93
  96.5 35.6 %all-gather.11.cloned.1.call-done = bf16[1024,2048]{0,1:T(8,128)(2,1)} async-done(((bf16[128,2048]{0,1:T(8,128)(2,1)}), bf16[1024,2048]{0,1:T(8,128)(2,1)}) %all-gather.11.cloned.1.call-update) | async-done | bytes 4194320 | tf_op jit(solution)/shard_map/all_gather | solution.py:43
  186.9 25.5 %all-gather.13.cloned.1.call-done = bf16[2048,2048]{1,0:T(8,128)(2,1)} async-done(((bf16[64,2048]{1,0:T(8,128)(2,1)}), bf16[2048,2048]{1,0:T(8,128)(2,1)}) %all-gather.13.cloned.1.call-update) | async-done | bytes 8388624 | tf_op jit(solution)/shard_map/all_gather | solution.py:87
  217.0 50.0 %reduce-scatter.13.cloned.1.call-done = bf16[128,2048]{1,0:T(8,128)(2,1)} async-done(((bf16[1024,2048]{1,0:T(8,128)(2,1)}), bf16[128,2048]{1,0:T(8,128)(2,1)}) %reduce-scatter.13.cloned.1.call-update) | async-done | bytes 524304 | tf_op jit(solution)/shard_map/reduce_scatter | solution.py:46
  272.5 41.1 %all-gather.1 = s32[4096,8]{0,1:T(8,128)S(1)} all-gather(s32[128,8]{0,1:T(8,128)S(1)} %copy-done.50), channel_id=3, replica_groups=mesh['ep'=8,'dp'=4] {'ep','dp'}, dimensions={0}, use_global_device_ids=true | all-gather | bytes 135168 | tf_op jit(solution)/shard_map/all_gather | solution.py:148
  325.2 116.4 %all-gather.17.cloned.1.call-done = bf16[4096,2048]{1,0:T(8,128)(2,1)} async-done(((bf16[128,2048]{1,0:T(8,128)(2,1)}), bf16[4096,2048]{1,0:T(8,128)(2,1)}) %all-gather.17.cloned.1.call-update) | async-done | bytes 16777232 | tf_op jit(solution)/shard_map/all_gather | solution.py:145
  441.6 23.5 %convert_bitcast_fusion = bf16[8,32,32,2048]{3,2,0,1:T(8,128)(2,1)} fusion(bf16[32,128,2048,1]{2,1,3,0:T(8,128)(2,1)} %bitcast.224, s32[32,8,128]{2,1,0:T(8,128)S(1)} %copy.292), kind=kOutput, calls=%fused_computation.8 | convolution fusion | flops 4312793088 | bytes 50462720 | tf_op jit(solution)/shard_map/best,btd->ebsd/dot_general | solution.py:18
  465.2 23.2 %copy.300 = bf16[8,32,32,2048]{3,2,1,0:T(8,128)(2,1)} copy(bf16[8,32,32,2048]{3,2,0,1:T(8,128)(2,1)} %convert_bitcast_fusion) | data formatting | bytes 67108864 | tf_op jit(solution)/shard_map/convert_element_type | solution.py:165
  488.3 70.2 %all-gather.15.cloned.1.call-done = bf16[4096,2048]{1,0:T(8,128)(2,1)} async-done(((bf16[128,2048]{1,0:T(8,128)(2,1)}), bf16[4096,2048]{1,0:T(8,128)(2,1)}) %all-gather.15.cloned.1.call-update) | async-done | bytes 16777232 | tf_op jit(solution)/shard_map/all_gather | solution.py:144
  578.2 22.9 %copy.295 = bf16[8,32,32,2048]{3,2,1,0:T(8,128)(2,1)} copy(bf16[8,32,32,2048]{3,2,0,1:T(8,128)(2,1)} %convert_bitcast_fusion.1) | data formatting | bytes 67108864 | tf_op jit(solution)/shard_map/convert_element_type | solution.py:164
  601.2 19.9 %fusion.85 = f32[8,1024,256]{1,2,0:T(8,128)} fusion(bf16[8,1024,2048]{2,1,0:T(8,128)(2,1)} %bitcast.218, bf16[8,2048,256]{2,1,0:T(8,128)(2,1)} %param.27), kind=kOutput, calls=%fused_computation.181 | convolution fusion | flops 8589934592 | bytes 50331648 | tf_op jit(solution)/shard_map/erd,edf->erf/dot_general | solution.py:18
  621.1 19.9 %fusion.84 = f32[8,1024,256]{1,2,0:T(8,128)} fusion(bf16[8,1024,2048]{2,1,0:T(8,128)(2,1)} %bitcast.219, bf16[8,2048,256]{2,1,0:T(8,128)(2,1)} %param.26), kind=kOutput, calls=%fused_computation.180 | convolution fusion | flops 8589934592 | bytes 50331648 | tf_op jit(solution)/shard_map/erd,edf->erf/dot_general | solution.py:18
  641.0 24.0 %multiply_reduce_fusion = (f32[8,1024]{1,0:T(8,128)S(1)}, f32[8,1024,256]{1,2,0:T(8,128)}) fusion(f32[8,1024,256]{1,2,0:T(8,128)} %fusion.85, f32[8,1024,256]{1,2,0:T(8,128)} %fusion.84, bf16[8,1024,2048]{2,1,0:T(8,128)(2,1)} %bitcast.222, bf16[8,256,2048]{2,1,0:T(8,128)(2,1)} %param.28), kind=kOutput, calls=%fused_computation.17 | convolution fusion | flops 8604606464 | bytes 67141632 | tf_op jit(solution)/shard_map/erd,efd->erf/dot_general | solution.py:18
  684.0 27.6 %fusion.86 = f32[8,1024,2048]{2,1,0:T(8,128)} fusion(bf16[8,1024,256]{1,2,0:T(8,128)(2,1)} %get-tuple-element.112, bf16[8,2048,256]{2,1,0:T(8,128)(2,1)} %param.26), kind=kOutput, calls=%fused_computation.182 | convolution fusion | flops 8589934592 | bytes 79691776 | tf_op jit(solution)/shard_map/erf,edf->erd/dot_general | solution.py:18
  711.7 36.8 %add_convert_fusion = bf16[8,1024,2048]{2,1,0:T(8,128)(2,1)} fusion(f32[8,1024,2048]{2,1,0:T(8,128)} %fusion.86, bf16[8,1024,256]{1,2,0:T(8,128)(2,1)} %get-tuple-element.111, bf16[8,2048,256]{2,1,0:T(8,128)(2,1)} %param.27), kind=kOutput, calls=%fused_computation.1 | convolution fusion | flops 8623489024 | bytes 113246208 | tf_op jit(solution)/shard_map/erf,edf->erd/dot_general | solution.py:18
  781.4 167.5 %reduce-scatter.17.cloned.1.call-done = bf16[1,128,2048]{2,1,0:T(8,128)(2,1)} async-done(((bf16[32,128,2048]{2,1,0:T(8,128)(2,1)}), bf16[1,128,2048]{2,1,0:T(8,128)(2,1)}) %reduce-scatter.17.cloned.1.call-update) | async-done | bytes 524304 | tf_op jit(solution)/shard_map/reduce_scatter | solution.py:190
  952.2 38.3 %all-gather.19.cloned.1.call-done = bf16[1024,2048]{1,0:T(8,128)(2,1)} async-done(((bf16[128,2048]{1,0:T(8,128)(2,1)}), bf16[1024,2048]{1,0:T(8,128)(2,1)}) %all-gather.19.cloned.1.call-update) | async-done | bytes 4194320 | tf_op jit(solution)/shard_map/all_gather | solution.py:43
  1102.4 19.8 %fusion.91 = f32[8,256,2048]{2,1,0:T(8,128)} fusion(bf16[8,1024,256]{1,2,0:T(8,128)(2,1)} %get-tuple-element.113, bf16[8,1024,2048]{2,1,0:T(8,128)(2,1)} %bitcast.223), kind=kOutput, calls=%fused_computation.187 | convolution fusion | flops 8589934592 | bytes 54525952 | tf_op jit(solution)/shard_map/erf,erd->efd/dot_general | solution.py:18
  1122.3 21.1 %fusion.90 = f32[8,2048,256]{2,1,0:T(8,128)} fusion(bf16[8,1024,2048]{2,1,0:T(8,128)(2,1)} %bitcast.220, bf16[8,1024,256]{1,2,0:T(8,128)(2,1)} %get-tuple-element.111), kind=kOutput, calls=%fused_computation.186 | convolution fusion | flops 8589934592 | bytes 54525952 | tf_op jit(solution)/shard_map/erd,erf->edf/dot_general | solution.py:18
  1143.4 72.4 %all-reduce.7.cloned.1.call-done = bf16[4,8,3,64,256]{4,3,1,0,2:T(8,128)(2,1)} async-done(((bf16[4,8,3,64,256]{4,3,1,0,2:T(8,128)(2,1)}), bf16[4,8,3,64,256]{4,3,1,0,2:T(8,128)(2,1)}) %all-reduce.7.cloned.1.call-update) | async-done | bytes 3145744
  1223.0 21.2 %fusion.89 = f32[8,2048,256]{2,1,0:T(8,128)} fusion(bf16[8,1024,2048]{2,1,0:T(8,128)(2,1)} %bitcast.221, bf16[8,1024,256]{1,2,0:T(8,128)(2,1)} %get-tuple-element.112), kind=kOutput, calls=%fused_computation.185 | convolution fusion | flops 8589934592 | bytes 54525952 | tf_op jit(solution)/shard_map/erd,erf->edf/dot_general | solution.py:18
  1252.3 154.1 %reduce-scatter.15.cloned.1.call-done = bf16[1,128,2048]{2,1,0:T(8,128)(2,1)} async-done(((bf16[32,128,2048]{2,1,0:T(8,128)(2,1)}), bf16[1,128,2048]{2,1,0:T(8,128)(2,1)}) %reduce-scatter.15.cloned.1.call-update) | async-done | bytes 524304 | tf_op jit(solution)/shard_map/reduce_scatter | solution.py:188
  1409.9 137.4 %reduce-scatter.23.cloned.1.call-done = f32[64,68]{1,0:T(8,128)} async-done(((f32[2048,68]{1,0:T(8,128)}), f32[64,68]{1,0:T(8,128)}) %reduce-scatter.23.cloned.1.call-update) | async-done | bytes 17424
  1552.0 142.0 %reduce-scatter.21.cloned.1.call-done = bf16[64,2048]{1,0:T(8,128)(2,1)} async-done(((bf16[2048,2048]{1,0:T(8,128)(2,1)}), bf16[64,2048]{1,0:T(8,128)(2,1)}) %reduce-scatter.21.cloned.1.call-update) | async-done | bytes 262160 | tf_op jit(solution)/shard_map/reduce_scatter | solution.py:246
  (312 shorter events, 332.6 us)
Async XLA Ops:
  7.2 85.7 %all-gather.21.cloned.1.call-start = ((), (), s32[]{:S(2)}) async-start(), calls=%async_computation.19 | async-start | bytes 3932160 | tf_op jit(solution)/shard_map/all_gather | solution.py:54
  28.2 103.9 %all-gather.11.cloned.1.call-start = ((), (), s32[]{:S(2)}) async-start(), calls=%async_computation.9 | async-start | bytes 4718592 | tf_op jit(solution)/shard_map/all_gather | solution.py:43
  30.3 182.1 %all-gather.13.cloned.1.call-start = ((), (), s32[]{:S(2)}) async-start(), calls=%async_computation.10 | async-start | bytes 8650752 | tf_op jit(solution)/shard_map/all_gather | solution.py:87
  31.1 236.0 %reduce-scatter.13.cloned.1.call-start = ((), (), s32[]{:S(2)}) async-start(), calls=%async_computation.11 | async-start | bytes 4718592 | tf_op jit(solution)/shard_map/reduce_scatter | solution.py:46
  75.8 193.8 %copy-start.2 = (bf16[2048,68]{1,0:T(8,128)(2,1)}, bf16[2048,68]{1,0:T(8,128)(2,1)S(1)}, u32[]{:S(2)}) copy-start(bf16[2048,68]{1,0:T(8,128)(2,1)S(1)} %all_gather.37) | copy-start | bytes 835588
  79.1 189.2 %copy-start.42 = (f32[2048]{0:T(1024)}, f32[2048]{0:T(1024)S(1)}, u32[]{:S(2)}) copy-start(f32[2048]{0:T(1024)S(1)} %get-tuple-element.107) | copy-start | bytes 24580
  217.0 106.7 %all-gather.23.cloned.1.call-start = ((), (), s32[]{:S(2)}) async-start(), calls=%async_computation.20 | async-start | bytes 1081344 | tf_op jit(solution)/shard_map/all_gather | solution.py:147
  271.1 170.6 %all-gather.17.cloned.1.call-start = ((), (), s32[]{:S(2)}) async-start(), calls=%async_computation.14 | async-start | bytes 17301504 | tf_op jit(solution)/shard_map/all_gather | solution.py:145
  271.7 286.9 %all-gather.15.cloned.1.call-start = ((), (), s32[]{:S(2)}) async-start(), calls=%async_computation.12 | async-start | bytes 17301504 | tf_op jit(solution)/shard_map/all_gather | solution.py:144
  272.4 496.4 %all-reduce.5.cloned.1.call-start = ((), (), s32[]{:S(2)}) async-start(), calls=%async_computation.22 | async-start | bytes 262144
  668.7 280.2 %reduce-scatter.17.cloned.1.call-start = ((), (), s32[]{:S(2)}) async-start(), calls=%async_computation.15 | async-start | bytes 17301504 | tf_op jit(solution)/shard_map/reduce_scatter | solution.py:190
  767.6 181.2 %copy-start.1 = (bf16[128,2048]{1,0:T(8,128)(2,1)S(1)}, bf16[128,2048]{1,0:T(8,128)(2,1)}, u32[]{:S(2)}) copy-start(bf16[128,2048]{1,0:T(8,128)(2,1)} %param.15) | copy-start | bytes 1572868
  767.6 181.2 %copy-start.3 = (bf16[2048,68]{1,0:T(8,128)(2,1)S(1)}, bf16[2048,68]{1,0:T(8,128)(2,1)}, u32[]{:S(2)}) copy-start(bf16[2048,68]{1,0:T(8,128)(2,1)} %copy-done.2) | copy-start | bytes 835588
  767.6 181.2 %copy-start.13 = (bf16[128,2048]{1,0:T(8,128)(2,1)S(1)}, bf16[128,2048]{1,0:T(8,128)(2,1)}, u32[]{:S(2)}) copy-start(bf16[128,2048]{1,0:T(8,128)(2,1)} %reduce-scatter.13.cloned.1.call-done) | copy-start | bytes 1572868
  767.7 183.0 %copy-start.17 = (bf16[128,2048]{1,0:T(8,128)(2,1)S(1)}, bf16[128,2048]{1,0:T(8,128)(2,1)}, u32[]{:S(2)}) copy-start(bf16[128,2048]{1,0:T(8,128)(2,1)} %param.16) | copy-start | bytes 1572868
  770.9 10.5 all-to-all-start.1
  774.5 215.9 %all-gather.19.cloned.1.call-start = ((), (), s32[]{:S(2)}) async-start(), calls=%async_computation.16 | async-start | bytes 4718592 | tf_op jit(solution)/shard_map/all_gather | solution.py:43
  781.4 214.1 %copy-start.58 = (f32[2,2,512]{2,1,0:T(2,128)S(1)}, f32[2,2,512]{2,1,0:T(2,128)}, u32[]{:S(2)}) copy-start(f32[2,2,512]{2,1,0:T(2,128)} %copy-done.57) | copy-start | bytes 24580
  951.9 139.8 %reduce-scatter.19.cloned.1.call-start = ((), (), s32[]{:S(2)}) async-start(), calls=%async_computation.17 | async-start | bytes 4718592 | tf_op jit(solution)/shard_map/reduce_scatter | solution.py:46
  1040.2 175.5 %all-reduce.7.cloned.1.call-start = ((), (), s32[]{:S(2)}) async-start(), calls=%async_computation.23 | async-start | bytes 6291456
  1049.7 356.7 %reduce-scatter.15.cloned.1.call-start = ((), (), s32[]{:S(2)}) async-start(), calls=%async_computation.13 | async-start | bytes 17301504 | tf_op jit(solution)/shard_map/reduce_scatter | solution.py:188
  1088.5 458.7 %reduce-scatter.23.cloned.1.call-start = ((), (), s32[]{:S(2)}) async-start(), calls=%async_computation.21 | async-start | bytes 1081344
  1094.9 599.1 %reduce-scatter.21.cloned.1.call-start = ((), (), s32[]{:S(2)}) async-start(), calls=%async_computation.18 | async-start | bytes 8650752 | tf_op jit(solution)/shard_map/reduce_scatter | solution.py:246
  1218.5 29.8 %all-to-all-start.2 = ((bf16[8,3,64,256]{3,2,1,0:T(8,128)(2,1)}), bf16[8,3,64,256]{3,2,1,0:T(8,128)(2,1)}, u32[]{:S(2)}, u32[]{:S(2)}) async-start(bf16[8,3,64,256]{3,2,1,0:T(8,128)(2,1)} %copy.314), calls=%async_computation.6 | async-start | bytes 1572864 | tf_op jit(solution)/shard_map/all_to_all | solution.py:51
  (60 other events, 1542.3 us)
Sparse Core Ops, SparseCore 0:
  28.3 64.5 all-gather.20
  95.4 36.6 all-gather.10
  135.0 77.4 all-gather.12
  217.1 49.9 reduce-scatter.12
  271.2 52.4 all-gather.22
  326.8 114.7 all-gather.16
  445.5 113.0 all-gather.14
  668.8 29.5 all-reduce.4
  767.8 180.9 reduce-scatter.16
  952.0 38.3 all-gather.18
  1040.3 51.3 reduce-scatter.18
  1094.6 121.0 all-reduce.6
  1218.2 188.2 reduce-scatter.14
  1408.6 138.5 reduce-scatter.22
  1549.4 144.6 reduce-scatter.20

commit v2 on v1

--- a/solution.py
+++ b/solution.py
@@ -1,17 +1,562 @@
+import functools
+
 import jax
 import jax.numpy as jnp
 from jax import lax
+from jax.experimental import pallas as pl
+from jax.experimental.pallas import tpu as pltpu
 from jax.sharding import PartitionSpec as P
 
 HEAD_DIM = 128
 EPSILON = 1e-05
+AXES = ("ep", "dp")
 BF = jnp.bfloat16
 F32 = jnp.float32
-AXES = ("ep", "dp")
+ANY = pl.BlockSpec(memory_space=pl.ANY)
+VMEM = pl.BlockSpec(memory_space=pltpu.VMEM)
+MESH = pl.DeviceIdType.MESH
+STEP = 512
+HOOKS = 8
 
 
 def dot(left, right):
     return jnp.dot(left, right, preferred_element_type=F32)
+
+
+def dot_t(left, right):
+    return lax.dot_general(left, right, (((1,), (1,)), ((), ())), preferred_element_type=F32)
+
+
+def tdot(left, right):
+    return lax.dot_general(left, right, (((0,), (0,)), ((), ())), preferred_element_type=F32)
+
+
+def flip(value, other, count):
+    result, bit = 0, 1
+    while bit < count:
+        result = result + ((value // bit) % 2 + (other // bit) % 2) % 2 * bit
+        bit *= 2
+    return result
+
+
+class Place:
+    def __init__(self, n_dp):
+        ep, dp = lax.axis_index("ep"), lax.axis_index("dp")
+        half = n_dp // 2
+        self.n_dp, self.half = n_dp, half
+        self.layer, self.y = ep // 2, ep % 2
+        self.x, self.core = dp // 2, dp % 2
+        self.rank = self.y * n_dp + dp
+        self.ep, self.dp = ep, dp
+        self.sibling = (ep, self.x * 2 + 1 - self.core)
+        self.over_x = (ep, (1 - self.x) * 2 + self.core)
+        self.over_y = (self.layer * 2 + 1 - self.y, dp)
+
+    def at_layer(self, layer):
+        return (layer * 2 + self.y, self.dp)
+
+
+def greet(partners):
+    barrier = pltpu.get_barrier_semaphore()
+    for partner in partners:
+        pl.semaphore_signal(barrier, inc=1, device_id=partner, device_id_type=MESH)
+    pl.semaphore_wait(barrier, len(partners))
+
+
+def experts_kernel(
+    n_dp, experts,
+    x_own, all_g, table, wg_hbm, wu_hbm, wd_hbm,
+    out_sum, grad_sum, x_out, g_out, acts_out, all_x,
+    sib_o, sib_g, one_o, one_g, two_o, two_g, z_o, z_g,
+    wg, wu, wd, xs, gs, gate_rows, acts, xin, gin, stage_o, stage_g, acc_o, acc_g, tmp_o, tmp_g,
+    mine_o, mine_g,
+    w_sem, in_sem, keep_sem, act_sem, own_sem, zx_send, zx_recv, ag_send, ag_recv,
+    sib_send, sib_recv, one_send, one_recv, two_send, two_recv, z_send, z_recv, tmp_sem,
+):
+    n_dev, rows, wide = all_x.shape
+    local, width, hid = wg.shape
+    cap = xs.shape[2]
+    group = 2 * n_dp
+    layers = n_dev // group
+    m = group * cap
+    slots = xin.shape[0]
+    half = width // 2
+    here = Place(n_dp)
+    rank, core, x, y = here.rank, here.core, here.x, here.y
+    first = here.ep * local
+
+    def remote(src, dst, send, recv, device):
+        return pltpu.make_async_remote_copy(
+            src_ref=src, dst_ref=dst, send_sem=send, recv_sem=recv,
+            device_id=device, device_id_type=MESH,
+        )
+
+    def layer_of(i):
+        return flip(here.layer, i, layers)
+
+    def weights():
+        return [
+            pltpu.make_async_copy(s, d, w_sem.at[i])
+            for i, (s, d) in enumerate(((wg_hbm, wg), (wu_hbm, wu), (wd_hbm, wd)))
+        ]
+
+    def z_copy(i):
+        me = here.layer * group + rank
+        return remote(
+            x_own, all_x.at[me], zx_send.at[i], zx_recv.at[i], here.at_layer(layer_of(i))
+        )
+
+    def own_copy():
+        return pltpu.make_async_copy(x_own, all_x.at[here.layer * group + rank], own_sem.at[0])
+
+    over_x_rank = y * n_dp + (1 - x) * 2 + core
+    over_y_rank = (1 - y) * n_dp + x * 2 + core
+    across_rank = (1 - y) * n_dp + (1 - x) * 2 + core
+    first_half, second_half = pl.ds(0, half), pl.ds(half, wide - half)
+
+    def gather_copy(i, kind):
+        base = layer_of(i) * group
+        which, cols, device = {
+            0: (rank, first_half, here.over_x),
+            1: (rank, second_half, here.over_x),
+            2: (rank, first_half, here.over_y),
+            3: (rank, second_half, here.over_y),
+            4: (over_x_rank, first_half, here.over_y),
+            5: (over_y_rank, second_half, here.over_x),
+            6: (rank, pl.ds(0, wide), here.sibling),
+            7: (over_x_rank, pl.ds(0, wide), here.sibling),
+            8: (over_y_rank, pl.ds(0, wide), here.sibling),
+            9: (across_rank, pl.ds(0, wide), here.sibling),
+        }[kind]
+        ref = all_x.at[base + which, :, cols]
+        return remote(ref, ref, ag_send.at[i, kind], ag_recv.at[i, kind], device)
+
+    def gather_a(i):
+        if isinstance(i, int) and i == 0:
+            own_copy().wait()
+        else:
+            z_copy(i).wait_recv()
+        for kind in (0, 3, 1, 2, 6):
+            gather_copy(i, kind).start()
+
+    def gather_b(i):
+        for got, then in ((0, 4), (3, 5), (1, 7), (2, 8)):
+            gather_copy(i, got).wait_recv()
+            gather_copy(i, then).start()
+
+    def gather_c(i):
+        gather_copy(i, 4).wait_recv()
+        gather_copy(i, 5).wait_recv()
+        gather_copy(i, 9).start()
+
+    def gather_d(i):
+        for kind in (6, 7, 8, 9):
+            gather_copy(i, kind).wait_recv()
+
+    def sib_copy(i, q, slot):
+        return (
+            remote(stage_o.at[slot], sib_o.at[i, q], sib_send.at[0, slot], sib_recv.at[0, i, q],
+                   here.sibling),
+            remote(stage_g.at[slot], sib_g.at[i, q], sib_send.at[1, slot], sib_recv.at[1, i, q],
+                   here.sibling),
+        )
+
+    def one_copy(i, j):
+        return (
+            remote(acc_o.at[j * 2 + 1 - x], one_o.at[i, j], one_send.at[0, j],
+                   one_recv.at[0, i, j], here.over_x),
+            remote(acc_g.at[(1 - y) * 2 + j], one_g.at[i, j], one_send.at[1, j],
+                   one_recv.at[1, i, j], here.over_y),
+        )
+
+    def two_copy(i):
+        return (
+            remote(acc_o.at[(1 - y) * 2 + x], two_o.at[i], two_send.at[0], two_recv.at[0, i],
+                   here.over_y),
+            remote(acc_g.at[y * 2 + 1 - x], two_g.at[i], two_send.at[1], two_recv.at[1, i],
+                   here.over_x),
+        )
+
+    def out_copy(i):
+        device = here.at_layer(layer_of(i))
+        own = y * 2 + x
+        return (
+            remote(acc_o.at[own], z_o.at[i], z_send.at[0], z_recv.at[0, i], device),
+            remote(acc_g.at[own], z_g.at[i], z_send.at[1], z_recv.at[1, i], device),
+        )
+
+    def fetch(src_o, src_g, slot):
+        return (
+            pltpu.make_async_copy(src_o, tmp_o.at[slot], tmp_sem.at[0, slot]),
+            pltpu.make_async_copy(src_g, tmp_g.at[slot], tmp_sem.at[1, slot]),
+        )
+
+    def start(copies):
+        for copy in copies:
+            copy.start()
+
+    def finish(copies):
+        for copy in copies:
+            copy.wait()
+
+    def add(dst, q, tmp, slot):
+        total = dst[q].astype(F32) + tmp[slot].astype(F32)
+        dst[q] = total.astype(BF)
+
+    def sum_sibling(i):
+        def bring(q, slot):
+            for copy in sib_copy(i, q, 0):
+                copy.wait_recv()
+            start(fetch(sib_o.at[i, q], sib_g.at[i, q], slot))
+
+        bring(0, 0)
+        for q in range(4):
+            if q < 3:
+                bring(q + 1, (q + 1) % 2)
+            finish(fetch(sib_o.at[i, q], sib_g.at[i, q], q % 2))
+            add(acc_o, q, tmp_o, q % 2)
+            add(acc_g, q, tmp_g, q % 2)
+        for j in range(2):
+            start(one_copy(i, j))
+
+    def sum_one(i):
+        def bring(j):
+            for copy in one_copy(i, j):
+                copy.wait_recv()
+            start(fetch(one_o.at[i, j], one_g.at[i, j], j))
+
+        bring(0)
+        bring(1)
+        for j in range(2):
+            finish(fetch(one_o.at[i, j], one_g.at[i, j], j))
+            add(acc_o, j * 2 + x, tmp_o, j)
+            add(acc_g, y * 2 + j, tmp_g, j)
+        start(two_copy(i))
+
+    def sum_two(i):
+        for copy in two_copy(i):
+            copy.wait_recv()
+        start(fetch(two_o.at[i], two_g.at[i], 0))
+        finish(fetch(two_o.at[i], two_g.at[i], 0))
+        own = y * 2 + x
+        add(acc_o, own, tmp_o, 0)
+        add(acc_g, own, tmp_g, 0)
+        for j in range(2):
+            for copy in one_copy(i, j):
+                copy.wait_send()
+        for copy in two_copy(i):
+            copy.wait_send()
+
+        @pl.when(i == 0)
+        def _():
+            mine_o[...] = acc_o[own]
+            mine_g[...] = acc_g[own]
+
+        @pl.when(i > 0)
+        def _():
+            start(out_copy(i))
+
+    start(weights())
+    greet([here.over_x, here.over_y, here.sibling]
+          + [here.at_layer(layer_of(i)) for i in range(1, layers)])
+    own_copy().start()
+    for i in range(1, layers):
+        z_copy(i).start()
+    gather_a(0)
+    gather_b(0)
+    gather_c(0)
+    gather_a(1)
+
+    def chunk(i, carry):
+        base = layer_of(i) * group
+
+        @pl.when(i > 0)
+        def _():
+            sum_sibling(i - 1)
+
+        gather_d(i)
+
+        def load(b, slot):
+            return (
+                pltpu.make_async_copy(all_x.at[base + b], xin.at[slot], in_sem.at[0, slot]),
+                pltpu.make_async_copy(
+                    all_g.at[base + b, :, pl.ds(0, width)], gin.at[slot], in_sem.at[1, slot]
+                ),
+            )
+
+        for b in range(slots - 1):
+            start(load(b, b))
+
+        def bring(b, c):
+            slot = lax.rem(b, slots)
+            finish(load(b, slot))
+
+            @pl.when(b + slots - 1 < group)
+            def _():
+                start(load(b + slots - 1, lax.rem(b + slots - 1, slots)))
+
+            hot = table[base + b]
+            for src, dst in ((xin, xs), (gin, gs)):
+                for n in range(0, width, STEP):
+                    got = dot(hot, src[slot, :, n : n + STEP]).astype(BF)
+                    dst[:, b, :, n : n + STEP] = got.reshape(local, cap, STEP)
+            gates = dot(hot, xin[slot, :, width:wide])
+            lanes = lax.broadcasted_iota(jnp.int32, gates.shape, 1) % experts
+            expert = lax.broadcasted_iota(jnp.int32, gates.shape, 0) // cap + first
+            gates = jnp.sum(jnp.where(lanes == expert, gates, 0.0), axis=1, keepdims=True)
+            gate_rows[:, b] = jnp.broadcast_to(gates, (local * cap, 128)).reshape(local, cap, 128)
+            return c
+
+        lax.fori_loop(0, group, bring, 0)
+
+        def keep(e):
+            return (
+                pltpu.make_async_copy(xs.at[e], x_out.at[e, pl.ds(base, group)], keep_sem.at[0, e]),
+                pltpu.make_async_copy(gs.at[e], g_out.at[e, pl.ds(base, group)], keep_sem.at[1, e]),
+            )
+
+        def keep_acts(e, slot):
+            return pltpu.make_async_copy(
+                acts.at[slot], acts_out.at[:, e, pl.ds(base * cap, m)], act_sem.at[slot]
+            )
+
+        lax.fori_loop(0, local, lambda e, c: (start(keep(e)), c)[1], 0)
+
+        @pl.when(i == 0)
+        def _():
+            finish(weights())
+
+        def expert(e, c):
+            def hook(number, when, action):
+                @pl.when(jnp.logical_and(e == number * local // HOOKS, when))
+                def _():
+                    action()
+
+            hook(1, i + 2 < layers, lambda: gather_a(i + 2))
+            hook(2, i + 1 < layers, lambda: gather_b(i + 1))
+            hook(4, i + 1 < layers, lambda: gather_c(i + 1))
+            hook(5, i > 0, lambda: sum_one(i - 1))
+            hook(7, i > 0, lambda: sum_two(i - 1))
+            slot = lax.rem(e, 2)
+
+            @pl.when(jnp.logical_or(i > 0, e >= 2))
+            def _():
+                keep_acts(e, slot).wait()
+
+            xe = xs[e].reshape(m, width)
+            ge = gs[e].reshape(m, width)
+            gate_part = dot(xe, wg[e])
+            up_part = dot(xe, wu[e])
+            raw = dot_t(ge, wd[e])
+            gate = gate_rows[e].reshape(m, 128)[:, :1]
+            sig = 1.0 / (1.0 + jnp.exp(-gate_part))
+            silu = gate_part * sig
+            hidden = silu * up_part
+            own = jnp.sum(hidden * raw, axis=1, keepdims=True)
+            lanes = lax.broadcasted_iota(jnp.int32, (m, 128), 1)
+            grad_hidden = raw * gate
+            hg = (hidden * gate).astype(BF)
+            dg = (grad_hidden * up_part * sig * (1.0 + gate_part * (1.0 - sig))).astype(BF)
+            du = (grad_hidden * silu).astype(BF)
+            gate_rows[e] = jnp.where(lanes == first + e, own, 0.0).reshape(group, cap, 128)
+            acts[slot, 0] = hg
+            acts[slot, 1] = dg
+            acts[slot, 2] = du
+            keep_acts(e, slot).start()
+            finish(keep(e))
+            for n in range(0, width, STEP):
+                out = dot(hg, wd[e, :, n : n + STEP]).astype(BF)
+                gs[e, :, :, n : n + STEP] = out.reshape(group, cap, STEP)
+                back = dot_t(dg, wg[e, n : n + STEP, :]) + dot_t(du, wu[e, n : n + STEP, :])
+                xs[e, :, :, n : n + STEP] = back.astype(BF).reshape(group, cap, STEP)
+            return c
+
+        lax.fori_loop(0, local, expert, 0)
+
+        def combine(b, put_o, put_g):
+            hot = table[base + b]
+            for n in range(0, width, STEP):
+                got = gs[:, b, :, n : n + STEP].reshape(local * cap, STEP)
+                put_o(n, STEP, tdot(hot, got).astype(BF))
+                got = xs[:, b, :, n : n + STEP].reshape(local * cap, STEP)
+                put_g(n, STEP, tdot(hot, got).astype(BF))
+            got = gate_rows[:, b].reshape(local * cap, 128).astype(BF)
+            put_g(width, 128, tdot(hot, got).astype(BF))
+
+        def give(q, c):
+            slot = lax.rem(q, 2)
+
+            @pl.when(jnp.logical_or(i > 0, q >= 2))
+            def _():
+                for copy in sib_copy(i, q, slot):
+                    copy.wait_send()
+
+            def put_o(n, size, value):
+                stage_o[slot, :, pl.ds(n, size)] = value
+
+            def put_g(n, size, value):
+                stage_g[slot, :, pl.ds(n, size)] = value
+
+            combine(q * 2 + 1 - core, put_o, put_g)
+            start(sib_copy(i, q, slot))
+            return c
+
+        lax.fori_loop(0, 4, give, 0)
+
+        @pl.when(i > 1)
+        def _():
+            for copy in out_copy(i - 1):
+                copy.wait_send()
+
+        def hold(q, c):
+            def put_o(n, size, value):
+                acc_o[q, :, pl.ds(n, size)] = value
+
+            def put_g(n, size, value):
+                acc_g[q, :, pl.ds(n, size)] = value
+
+            combine(q * 2 + core, put_o, put_g)
+            return c
+
+        lax.fori_loop(0, 4, hold, 0)
+        return carry
+
+    lax.fori_loop(0, layers, chunk, 0)
+    last = layers - 1
+    sum_sibling(last)
+    sum_one(last)
+    sum_two(last)
+    out_sum[...] = mine_o[...].astype(F32)
+    grad_sum[...] = mine_g[...].astype(F32)
+
+    def last_sum(i, c):
+        for copy in out_copy(i):
+            copy.wait_recv()
+        start(fetch(z_o.at[i], z_g.at[i], 0))
+        finish(fetch(z_o.at[i], z_g.at[i], 0))
+        out_sum[...] += tmp_o[0].astype(F32)
+        grad_sum[...] += tmp_g[0].astype(F32)
+        return c
+
+    lax.fori_loop(1, layers, last_sum, 0)
+    for copy in out_copy(last):
+        copy.wait_send()
+    for slot in range(2):
+        for copy in sib_copy(last, slot, slot):
+            copy.wait_send()
+        pltpu.make_async_copy(
+            acts.at[slot], acts_out.at[:, 0, pl.ds(0, m)], act_sem.at[slot]
+        ).wait()
+
+    def drain(i, c):
+        for kind in range(10):
+            gather_copy(i, kind).wait_send()
+        return c
+
+    lax.fori_loop(0, layers, drain, 0)
+    lax.fori_loop(1, layers, lambda i, c: (z_copy(i).wait_send(), c)[1], 0)
+
+
+def run_experts(x_own, all_g, table, wg, wu, wd, n_dp, experts, cap):
+    rows, wide = x_own.shape
+    n_dev = all_g.shape[0]
+    local, width, hid = wg.shape
+    group = 2 * n_dp
+    layers = n_dev // group
+    m = group * cap
+    wide_g = width + 128
+    slots = 3
+    dma = pltpu.SemaphoreType.DMA
+    shape = jax.ShapeDtypeStruct
+    slot_rows = shape((local, n_dev, cap, width), BF)
+    flops = 12 * n_dev * cap * local * width * hid
+    result = pl.pallas_call(
+        functools.partial(experts_kernel, n_dp, experts),
+        out_shape=(
+            shape((rows, width), F32), shape((rows, wide_g), F32),
+            slot_rows, slot_rows,
+            shape((3, local, n_dev * cap, hid), BF),
+            shape((n_dev, rows, wide), BF),
+            shape((layers, 4, rows, width), BF), shape((layers, 4, rows, wide_g), BF),
+            shape((layers, 2, rows, width), BF), shape((layers, 2, rows, wide_g), BF),
+            shape((layers, rows, width), BF), shape((layers, rows, wide_g), BF),
+            shape((layers, rows, width), BF), shape((layers, rows, wide_g), BF),
+        ),
+        in_specs=[ANY, ANY, VMEM, ANY, ANY, ANY],
+        out_specs=(VMEM, VMEM) + (ANY,) * 12,
+        scratch_shapes=[
+            pltpu.VMEM(wg.shape, BF), pltpu.VMEM(wu.shape, BF), pltpu.VMEM(wd.shape, BF),
+            pltpu.VMEM((local, group, cap, width), BF),
+            pltpu.VMEM((local, group, cap, width), BF),
+            pltpu.VMEM((local, group, cap, 128), F32),
+            pltpu.VMEM((2, 3, m, hid), BF),
+            pltpu.VMEM((slots, rows, wide), BF),
+            pltpu.VMEM((slots, rows, width), BF),
+            pltpu.VMEM((2, rows, width), BF), pltpu.VMEM((2, rows, wide_g), BF),
+            pltpu.VMEM((4, rows, width), BF), pltpu.VMEM((4, rows, wide_g), BF),
+            pltpu.VMEM((2, rows, width), BF), pltpu.VMEM((2, rows, wide_g), BF),
+            pltpu.VMEM((rows, width), BF), pltpu.VMEM((rows, wide_g), BF),
+            dma((3,)), dma((2, slots)), dma((2, local)), dma((2,)), dma((1,)),
+            dma((layers,)), dma((layers,)), dma((layers, 10)), dma((layers, 10)),
+            dma((2, 2)), dma((2, layers, 4)), dma((2, 2)), dma((2, layers, 2)),
+            dma((2,)), dma((2, layers)), dma((2,)), dma((2, layers)), dma((2, 2)),
+        ],
+        compiler_params=pltpu.CompilerParams(
+            collective_id=1, has_side_effects=True, vmem_limit_bytes=64 * 2**20
+        ),
+        cost_estimate=pl.CostEstimate(flops=flops, bytes_accessed=200 * 2**20, transcendentals=0),
+    )(x_own, all_g, table, wg, wu, wd)
+    return result[:5]
+
+
+def weights_kernel(x, g, acts, grad_g, grad_u, grad_d):
+    first = pl.program_id(1) == 0
+    xe, ge = x[0], g[0]
+
+    def put(ref, n, size, value, axis):
+        at = (0, pl.ds(n, size), slice(None)) if axis == 0 else (0, slice(None), pl.ds(n, size))
+
+        @pl.when(first)
+        def _():
+            ref[at] = value
+
+        @pl.when(jnp.logical_not(first))
+        def _():
+            ref[at] += value
+
+    hg, dg, du = acts[0, 0], acts[1, 0], acts[2, 0]
+    for n in range(0, xe.shape[1], STEP):
+        part = xe[:, n : n + STEP]
+        put(grad_g, n, STEP, tdot(part, dg), 0)
+        put(grad_u, n, STEP, tdot(part, du), 0)
+        put(grad_d, n, STEP, tdot(hg, ge[:, n : n + STEP]), 1)
+
+
+def run_weights(x_slots, g_slots, acts):
+    local, n_dev, cap, width = x_slots.shape
+    hid = acts.shape[-1]
+    total = n_dev * cap
+    tile = min(1024, total)
+    x_slots = x_slots.reshape(local, total, width)
+    g_slots = g_slots.reshape(local, total, width)
+    row = pl.BlockSpec((1, tile, width), lambda e, k: (e, k, 0))
+    wide = pl.BlockSpec((1, width, hid), lambda e, k: (e, 0, 0))
+    deep = pl.BlockSpec((1, hid, width), lambda e, k: (e, 0, 0))
+    return pl.pallas_call(
+        weights_kernel,
+        grid=(local, total // tile),
+        out_shape=(
+            jax.ShapeDtypeStruct((local, width, hid), F32),
+            jax.ShapeDtypeStruct((local, width, hid), F32),
+            jax.ShapeDtypeStruct((local, hid, width), F32),
+        ),
+        in_specs=[row, row, pl.BlockSpec((3, 1, tile, hid), lambda e, k: (0, e, k, 0))],
+        out_specs=(wide, wide, deep),
+        compiler_params=pltpu.CompilerParams(vmem_limit_bytes=60 * 2**20),
+        cost_estimate=pl.CostEstimate(
+            flops=6 * local * total * width * hid, bytes_accessed=130 * 2**20, transcendentals=0
+        ),
+    )(x_slots, g_slots, acts)
 
 
 def ein(spec, left, right):
@@ -80,10 +625,6 @@
         qkv = column_gather(qkv)
         qkv = qkv.transpose(2, 0, 1, 3, 4).reshape(3, width, cols)
         wq, wk, wv = qkv[0], qkv[1], qkv[2]
-        wo = column_gather(w_o)
-        halves = group // n_dp
-        return_rank = [(halves * g) % group for g in range(n_group)]
-        del return_rank
         full_o = lax.all_gather(w_o, AXES, axis=0, tiled=True)
         wo = lax.dynamic_slice_in_dim(full_o, rank * cols, cols, 0)
 
@@ -141,66 +682,31 @@
         gates_dense = jnp.sum(jnp.where(picked, gates[:, :, None], 0.0), axis=1)
         hits = jnp.any(picked, axis=1)
 
-        all_x = lax.all_gather(normed2, AXES, axis=0, tiled=True).reshape(n_dev, rows, width)
-        all_g = lax.all_gather(grad_out, AXES, axis=0, tiled=True).reshape(n_dev, rows, width)
+        before = jnp.cumsum(hits.astype(jnp.int32), axis=0) - hits.astype(jnp.int32)
+        place = jnp.where(hits, before, -1).astype(BF)
+        sent = jnp.concatenate([grad_out, place, jnp.zeros((rows, 128 - experts), BF)], axis=1)
+        all_g = lax.all_gather(sent, AXES, axis=0, tiled=True).reshape(n_dev, rows, -1)
         first = lax.axis_index("ep") * local_experts
-        all_gates = lax.all_gather(gates_dense, AXES, axis=0, tiled=False)
-        all_routes = lax.all_gather(routes, AXES, axis=0, tiled=False)
-        local_ids = first + jnp.arange(local_experts, dtype=jnp.int32)
-        local_hits = jnp.any(all_routes[..., None] == local_ids, axis=2).astype(jnp.int32)
-        before = jnp.cumsum(local_hits, axis=1) - local_hits
-        place = jnp.where(local_hits > 0, before, -1)
+        own_place = lax.dynamic_slice_in_dim(all_g, width + first, local_experts, 2)
         table = (
-            place.transpose(0, 2, 1)[:, :, None, :]
-            == jnp.arange(cap, dtype=jnp.int32)[None, None, :, None]
-        )
-        table_low = table.astype(BF)
-        local_gates = lax.dynamic_slice_in_dim(all_gates, first, local_experts, 2)
-        slot_gates = jnp.sum(
-            jnp.where(table, local_gates.transpose(0, 2, 1)[:, :, None, :], 0.0), axis=-1
-        )
-        slot_gates = slot_gates.transpose(1, 0, 2).reshape(local_experts, n_dev * cap, 1)
-        slots = (local_experts, n_dev * cap)
-        x_rows = ein("best,btd->ebsd", table_low, all_x).astype(BF).reshape(*slots, width)
-        g_rows = ein("best,btd->ebsd", table_low, all_g).astype(BF).reshape(*slots, width)
-        gate_part = ein("erd,edf->erf", x_rows, w_gate)
-        up_part = ein("erd,edf->erf", x_rows, w_up)
-        sig = jax.nn.sigmoid(gate_part)
-        silu = gate_part * sig
-        hidden = silu * up_part
-        raw_grad = ein("erd,efd->erf", g_rows, w_down)
-        hidden_gated = (slot_gates * hidden).astype(BF)
-        slot_gate_grads = jnp.sum(hidden * raw_grad, axis=-1).reshape(local_experts, n_dev, cap)
-        grad_hidden = raw_grad * slot_gates
-        gpart_low = (grad_hidden * up_part * sig * (1.0 + gate_part * (1.0 - sig))).astype(BF)
-        upart_low = (grad_hidden * silu).astype(BF)
-        out_rows = ein("erf,efd->erd", hidden_gated, w_down).astype(BF)
-        grad_rows = (
-            ein("erf,edf->erd", gpart_low, w_gate) + ein("erf,edf->erd", upart_low, w_up)
-        ).astype(BF)
-        back = (local_experts, n_dev, cap, width)
-        out_part = ein("best,ebsd->btd", table_low, out_rows.reshape(back)).astype(BF)
-        grad_part = ein("best,ebsd->btd", table_low, grad_rows.reshape(back)).astype(BF)
-        grad_w_down = ein("erf,erd->efd", hidden_gated, g_rows)
-        grad_w_gate = ein("erd,erf->edf", x_rows, gpart_low)
-        grad_w_up = ein("erd,erf->edf", x_rows, upart_low)
-
-        expert_sum = lax.psum_scatter(out_part, AXES, scatter_dimension=0, tiled=True)
-        output = (residual + expert_sum[0].astype(F32)).astype(BF)
-        grad_n2 = lax.psum_scatter(grad_part, AXES, scatter_dimension=0, tiled=True)[0]
-
-        gate_grads = jnp.sum(
-            jnp.where(table, slot_gate_grads.transpose(1, 0, 2)[..., None], 0.0), axis=2
-        )
-        gate_grads = gate_grads.reshape(n_ep, n_dp, local_experts, rows)
-        gate_grads = lax.psum_scatter(gate_grads, "dp", scatter_dimension=1, tiled=False)
-        gate_grads = lax.all_to_all(gate_grads, "ep", 0, 0, tiled=True)
-        gate_grads = gate_grads.reshape(experts, rows).T
-        gate_grads = jnp.where(hits, gate_grads, 0.0)
+            own_place.transpose(0, 2, 1)[:, :, None, :]
+            == jnp.arange(cap, dtype=jnp.int32).astype(BF)[None, None, :, None]
+        )
+        table = table.astype(BF).reshape(n_dev, local_experts * cap, rows)
+
+        gates_high = gates_dense.astype(BF)
+        gates_rest = (gates_dense - gates_high.astype(F32)).astype(BF)
+        x_own = jnp.concatenate([normed2, gates_high, gates_rest], axis=1)
+        expert_sum, grad_sum, x_slots, g_slots, acts = run_experts(
+            x_own, all_g, table, w_gate, w_up, w_down, n_dp, experts, cap
+        )
+        grad_w_gate, grad_w_up, grad_w_down = run_weights(x_slots, g_slots, acts)
+        output = (residual + expert_sum).astype(BF)
+        gate_grads = jnp.where(hits, grad_sum[:, width : width + experts], 0.0)
         weighted = jnp.sum(gates_dense * gate_grads, axis=-1, keepdims=True)
         grad_logits = (gates_dense * (gate_grads - weighted)).astype(BF)
 
-        grad_n2 = grad_n2.astype(F32) + ein("te,de->td", grad_logits, full_router)
+        grad_n2 = grad_sum[:, :width] + ein("te,de->td", grad_logits, full_router)
         grad_router = ein("td,te->de", normed2, grad_logits)
         grad_y = grad_out.astype(F32)
         grad_ffn_gain = jnp.sum(grad_n2 * res_n, axis=0)

time: 1710 us -> 1360 us (0.80)
  Pallas kernels: 0 us -> 416 us
  waiting for transfers between devices: 1040 us -> 681 us
  matrix products: 340 us -> 50.5 us
  local copies, waits for them, and re-layouts: 106 us -> 51.2 us
  blocking collectives: 131 us -> 89.1 us
  other arithmetic: 59.1 us -> 39.7 us
    pallas_call x0 -> x2, Pallas kernels: none -> 416 us  [the longest x1 368 us: run_experts(): pl.pallas_call(functools.partial(experts_kernel, n_dp, experts), out_shap...]
    reduce_scatter x2 -> x0, waiting for transfers between devices: 322 us -> none  [the longest x1 167 us: shards(): lax.psum_scatter(grad_part, AXES, scatter_dimension=0, tiled=True)[0]]
    dot_general x28 -> x15, matrix products: 324 us -> 33.1 us  [ein(): return jnp.einsum(spec, left, right, preferred_element_type=F32)]
    all_gather x3 -> x1, waiting for transfers between devices: 190 us -> 118 us  [shards(): lax.all_gather(sent, AXES, axis=0, tiled=True).reshape(n_dev, rows, -1)]
    convert_element_type x2 -> x1, local copies, waits for them, and re-layouts: 46.1 us -> 0.11 us  [shards(): gates_high = gates_dense.astype(BF)]
    all_gather x1 -> x0, blocking collectives: 41.1 us -> none  [shards(): all_routes = lax.all_gather(routes, AXES, axis=0, tiled=False)]
    reduce_scatter x2, waiting for transfers between devices: 51.9 us -> 89.1 us  [group_scatter(): lax.psum_scatter(value, AXES, scatter_dimension=0, tiled=True, axis_index...]
    all_gather x2, waiting for transfers between devices: 73.9 us -> 101 us  [group_gather(): lax.all_gather(value, AXES, axis=axis, tiled=True, axis_index_groups=rows...]
  transfers between devices with their start and end apart: 17 -> 11, of which waited for: 16 -> 10; matrix products, arithmetic and copies ran while one was open for 20% -> 7% of each run, Pallas kernels for 0% -> 4%
where the time goes in v2:
time: 1360 us; the launch traced here: 1350 us
  waiting for transfers between devices  681 us (50%)
  Pallas kernels  416 us (31%)
  blocking collectives  89.1 us (7%)
  local copies, waits for them, and re-layouts  51.2 us (4%)
  matrix products  50.5 us (4%)
  other arithmetic  39.7 us (3%)
  between operations  16 us (1%)
    pallas_call x1, Pallas kernels, run_experts(): pl.pallas_call(functools.partial(experts_kernel, n_dp, experts), out_shap...  368 us
    unnamed x12, waiting for transfers between devices  189 us
    reduce_scatter x1, waiting for transfers between devices, shards(): lax.psum_scatter(grad_o, AXES, scatter_dimension=0, tiled=True).astype(F32)  142 us
    all_gather x1, waiting for transfers between devices, shards(): lax.all_gather(sent, AXES, axis=0, tiled=True).reshape(n_dev, rows, -1)  118 us
    all_gather x2, waiting for transfers between devices, group_gather(): lax.all_gather(value, AXES, axis=axis, tiled=True, axis_index_groups=rows...  101 us
    reduce_scatter x2, waiting for transfers between devices, group_scatter(): lax.psum_scatter(value, AXES, scatter_dimension=0, tiled=True, axis_index...  89.1 us
    pallas_call x1, Pallas kernels, run_weights(): pl.pallas_call(weights_kernel, grid=(local, total // tile), out_shape=(ja...  47.7 us
    all_gather x1, blocking collectives, shards(): small = lax.all_gather(small, AXES, axis=0, tiled=True)  43.9 us
  transfers between devices with their start and end apart: 11, of which 10 were waited for; matrix products, arithmetic and copies ran while one was open for 7% of the time, Pallas kernels for 4%

profile of v2, /device:TPU:0, one launch (start us, length us, event | category | flops | bytes accessed | tf_op | source)
XLA Modules:
  0.0 1348.2 jit_solution(4564838707236840517)
XLA Ops:
  10.7 17.6 %all_to_all.10 = bf16[8,3,64,256]{3,2,1,0:T(8,128)(2,1)} all-to-all(bf16[8,3,64,256]{3,2,1,0:T(8,128)(2,1)S(1)} %copy.240), channel_id=1, replica_groups={{0,1,2,3,4,5,6,7},{8,9,10,11,12,13,14,15},{16,17,18,19,20,21,22,23},{24..., dimensions={0} | all-to-all | bytes 1572864 | tf_op jit(solution)/shard_map/all_to_all | solution.py:596
  30.8 43.9 %all_gather.22 = bf16[2048,68]{1,0:T(8,128)(2,1)S(1)} all-gather(bf16[64,68]{1,0:T(8,128)(2,1)S(1)} %concatenate.33), channel_id=1, replica_groups=mesh['ep'=8,'dp'=4] {'ep','dp'}, dimensions={0}, use_global_device_ids=true | all-gather | bytes 287232 | tf_op jit(solution)/shard_map/all_gather | solution.py:634
  78.0 15.1 %all-gather.15.cloned.1.call-done = bf16[32,3,64,256]{3,2,1,0:T(8,128)(2,1)} async-done(((bf16[8,3,64,256]{3,2,1,0:T(8,128)(2,1)}), bf16[32,3,64,256]{3,2,1,0:T(8,128)(2,1)}) %all-gather.15.cloned.1.call-update) | async-done | bytes 3145744 | tf_op jit(solution)/shard_map/all_gather | solution.py:599
  97.2 34.9 %all-gather.7.cloned.1.call-done = bf16[1024,2048]{0,1:T(8,128)(2,1)} async-done(((bf16[128,2048]{0,1:T(8,128)(2,1)}), bf16[1024,2048]{0,1:T(8,128)(2,1)}) %all-gather.7.cloned.1.call-update) | async-done | bytes 4194320 | tf_op jit(solution)/shard_map/all_gather | solution.py:588
  140.0 14.0 %psum.14 = f32[2,1024]{1,0:T(2,128)S(1)} all-reduce(f32[2,1024]{1,0:T(2,128)S(1)} %pad_maximum_fusion.2), channel_id=1, replica_groups={{0,1,2,3,4,5,6,7},{8,9,10,11,12,13,14,15},{16,17,18,19,20,21,22,23},{24..., use_global_device_ids=true, to_apply=%region_3.4 | all-reduce | flops 2048 | bytes 16384 | tf_op jit(solution)/shard_map/psum | solution.py:646
  165.7 4.6 convolution_convert_fusion.8
  176.6 5.0 fusion.63
  181.6 3.9 fusion.14
  185.9 26.4 %all-gather.9.cloned.1.call-done = bf16[2048,2048]{1,0:T(8,128)(2,1)} async-done(((bf16[64,2048]{1,0:T(8,128)(2,1)}), bf16[2048,2048]{1,0:T(8,128)(2,1)}) %all-gather.9.cloned.1.call-update) | async-done | bytes 8388624 | tf_op jit(solution)/shard_map/all_gather | solution.py:628
  212.3 4.6 convolution_convert_fusion
  218.5 48.5 %reduce-scatter.10.cloned.1.call-done = bf16[128,2048]{1,0:T(8,128)(2,1)} async-done(((bf16[1024,2048]{1,0:T(8,128)(2,1)}), bf16[128,2048]{1,0:T(8,128)(2,1)}) %reduce-scatter.10.cloned.1.call-update) | async-done | bytes 524304 | tf_op jit(solution)/shard_map/reduce_scatter | solution.py:591
  271.8 118.2 %all-gather.11.cloned.1.call-done = bf16[4096,2176]{1,0:T(8,128)(2,1)} async-done(((bf16[128,2176]{1,0:T(8,128)(2,1)}), bf16[4096,2176]{1,0:T(8,128)(2,1)}) %all-gather.11.cloned.1.call-update) | async-done | bytes 17825808 | tf_op jit(solution)/shard_map/all_gather | solution.py:688
  393.8 367.9 %shard_map.254 = (f32[128,2048]{1,0:T(8,128)}, f32[128,2176]{1,0:T(8,128)}, bf16[8,32,32,2048]{3,2,1,0:T(8,128)(2,1)}, bf16[8,32,32,2048]{3,2,1,0:T(8,128)(2,1)}...) custom-call(bf16[128,2176]{1,0:T(8,128)(2,1)} %concatenate.38.x_own,, ...), custom_call_target="tpu_custom_call" | custom-call | flops 51539607552 | bytes 209715200 | tf_op jit(solution)/shard_map/pallas_call | solution.py:473
  767.7 66.0 %all-gather.13.cloned.1.call-done = bf16[1024,2048]{1,0:T(8,128)(2,1)} async-done(((bf16[128,2048]{1,0:T(8,128)(2,1)}), bf16[1024,2048]{1,0:T(8,128)(2,1)}) %all-gather.13.cloned.1.call-update) | async-done | bytes 4194320 | tf_op jit(solution)/shard_map/all_gather | solution.py:588
  833.7 3.8 convolution_convert_fusion.7
  845.5 4.7 multiply_convert_fusion
  856.9 13.6 %psum.15 = f32[2,1024]{1,0:T(2,128)S(1)} all-reduce(f32[2,1024]{1,0:T(2,128)S(1)} %pad_maximum_fusion.3), channel_id=1, replica_groups={{0,1,2,3,4,5,6,7},{8,9,10,11,12,13,14,15},{16,17,18,19,20,21,22,23},{24..., use_global_device_ids=true, to_apply=%region_20.21 | all-reduce | flops 2048 | bytes 16384 | tf_op jit(solution)/shard_map/psum | solution.py:729
  890.8 40.6 %reduce-scatter.12.cloned.1.call-done = bf16[128,2048]{1,0:T(8,128)(2,1)} async-done(((bf16[1024,2048]{1,0:T(8,128)(2,1)}), bf16[128,2048]{1,0:T(8,128)(2,1)}) %reduce-scatter.12.cloned.1.call-update) | async-done | bytes 524304 | tf_op jit(solution)/shard_map/reduce_scatter | solution.py:591
  934.7 4.3 broadcast_in_dim.50
  942.6 112.9 %all-reduce.3.cloned.1.call-done = bf16[4,8,3,64,256]{4,3,1,0,2:T(8,128)(2,1)} async-done(((bf16[4,8,3,64,256]{4,3,1,0,2:T(8,128)(2,1)}), bf16[4,8,3,64,256]{4,3,1,0,2:T(8,128)(2,1)}) %all-reduce.3.cloned.1.call-update) | async-done | bytes 3145744
  1058.2 4.5 all-to-all-start.1
  1062.8 47.7 %shard_map.255 = (f32[8,2048,256]{2,1,0:T(8,128)}, f32[8,2048,256]{2,1,0:T(8,128)}, f32[8,256,2048]{2,1,0:T(8,128)}) custom-call(bf16[8,1024,2048]{2,1,0:T(8,128)(2,1)} %bitcast.203, bf16[8,1024,2048]{2,1,0:T(8,128)(2,1)} %bitcast.204, bf16[3,8,1024,256]{3,2,1,0:T(8,128)(2,1)} %get-tuple-element.26.acts), custom_call_target="tpu_custom_call" | custom-call | flops 25769803776 | bytes 136314880 | tf_op jit(solution)/shard_map/pallas_call | solution.py:545
  1116.7 75.4 %reduce-scatter.16.cloned.1.call-done = f32[64,68]{1,0:T(8,128)} async-done(((f32[2048,68]{1,0:T(8,128)}), f32[64,68]{1,0:T(8,128)}) %reduce-scatter.16.cloned.1.call-update) | async-done | bytes 17424
  1196.9 142.3 %reduce-scatter.14.cloned.1.call-done = bf16[64,2048]{1,0:T(8,128)(2,1)} async-done(((bf16[2048,2048]{1,0:T(8,128)(2,1)}), bf16[64,2048]{1,0:T(8,128)(2,1)}) %reduce-scatter.14.cloned.1.call-update) | async-done | bytes 262160 | tf_op jit(solution)/shard_map/reduce_scatter | solution.py:752
  (287 shorter events, 112.0 us)
Async XLA Ops:
  7.2 85.9 %all-gather.15.cloned.1.call-start = ((), (), s32[]{:S(2)}) async-start(), calls=%async_computation.13 | async-start | bytes 3932160 | tf_op jit(solution)/shard_map/all_gather | solution.py:599
  8.3 22.3 %copy-start.60 = (bf16[64,64]{1,0:T(8,128)(2,1)S(1)}, bf16[64,64]{1,0:T(8,128)(2,1)}, u32[]{:S(2)}) copy-start(bf16[64,64]{1,0:T(8,128)(2,1)} %param.25) | copy-start | bytes 24580
  28.3 103.8 %all-gather.7.cloned.1.call-start = ((), (), s32[]{:S(2)}) async-start(), calls=%async_computation.6 | async-start | bytes 4718592 | tf_op jit(solution)/shard_map/all_gather | solution.py:588
  29.4 182.9 %all-gather.9.cloned.1.call-start = ((), (), s32[]{:S(2)}) async-start(), calls=%async_computation.7 | async-start | bytes 8650752 | tf_op jit(solution)/shard_map/all_gather | solution.py:628
  30.1 236.9 %reduce-scatter.10.cloned.1.call-start = ((), (), s32[]{:S(2)}) async-start(), calls=%async_computation.8 | async-start | bytes 4718592 | tf_op jit(solution)/shard_map/reduce_scatter | solution.py:591
  74.7 194.9 %copy-start = (bf16[2048,68]{1,0:T(8,128)(2,1)}, bf16[2048,68]{1,0:T(8,128)(2,1)S(1)}, u32[]{:S(2)}) copy-start(bf16[2048,68]{1,0:T(8,128)(2,1)S(1)} %all_gather.22) | copy-start | bytes 835588
  75.2 78.9 %copy-start.56 = (f32[256]{0:T(256)}, f32[256]{0:T(256)S(1)}, u32[]{:S(2)}) copy-start(f32[256]{0:T(256)S(1)} %get-tuple-element.190) | copy-start | bytes 3076
  75.2 83.9 %copy-start.58 = (f32[256]{0:T(256)}, f32[256]{0:T(256)S(1)}, u32[]{:S(2)}) copy-start(f32[256]{0:T(256)S(1)} %get-tuple-element.189) | copy-start | bytes 3076
  78.0 57.4 %copy-start.49 = (f32[2048]{0:T(1024)}, f32[2048]{0:T(1024)S(1)}, u32[]{:S(2)}) copy-start(f32[2048]{0:T(1024)S(1)} %get-tuple-element.138) | copy-start | bytes 24580
  78.0 190.3 %copy-start.47 = (f32[2048]{0:T(1024)}, f32[2048]{0:T(1024)S(1)}, u32[]{:S(2)}) copy-start(f32[2048]{0:T(1024)S(1)} %get-tuple-element.137) | copy-start | bytes 24580
  97.2 39.5 %copy-start.25 = (bf16[1,4,8,64,256]{4,3,2,1,0:T(8,128)(2,1)}, bf16[1,4,8,64,256]{4,3,2,1,0:T(8,128)(2,1)S(1)}, u32[]{:S(2)}) copy-start(bf16[1,4,8,64,256]{4,3,2,1,0:T(8,128)(2,1)S(1)} %get-tuple-element.140) | copy-start | bytes 3145732
  185.9 31.0 %copy-start.12 = (bf16[2,512,2,128]{3,2,1,0:T(2,128)(2,1)}, bf16[2,512,2,128]{3,2,1,0:T(2,128)(2,1)S(1)}, u32[]{:S(2)}) copy-start(bf16[2,512,2,128]{3,2,1,0:T(2,128)(2,1)S(1)} %copy.252) | copy-start | bytes 1572868
  216.9 173.0 %all-gather.11.cloned.1.call-start = ((), (), s32[]{:S(2)}) async-start(), calls=%async_computation.9 | async-start | bytes 18382848 | tf_op jit(solution)/shard_map/all_gather | solution.py:688
  217.1 51.2 %copy-start.42 = (pred[128,64]{1,0:T(32,128)(4,1)}, pred[128,64]{1,0:T(32,128)(4,1)S(1)}, u32[]{:S(2)}) copy-start(pred[128,64]{1,0:T(32,128)(4,1)S(1)} %copy.257) | copy-start | bytes 24580
  218.4 615.3 %all-gather.13.cloned.1.call-start = ((), (), s32[]{:S(2)}) async-start(), calls=%async_computation.10 | async-start | bytes 4718592 | tf_op jit(solution)/shard_map/all_gather | solution.py:588
  270.5 119.5 %copy-start.39 = (f32[128,64]{1,0:T(8,128)}, f32[128,64]{1,0:T(8,128)S(1)}, u32[]{:S(2)}) copy-start(f32[128,64]{1,0:T(8,128)S(1)} %copy.254) | copy-start | bytes 98308
  765.3 72.1 %copy-start.29 = (f32[128,2048]{1,0:T(8,128)}, f32[128,2048]{1,0:T(8,128)S(1)}, u32[]{:S(2)}) copy-start(f32[128,2048]{1,0:T(8,128)S(1)} %get-tuple-element.183) | copy-start | bytes 3145732
  767.4 70.6 %copy-start.62 = (f32[2,2,512]{2,1,0:T(2,128)S(1)}, f32[2,2,512]{2,1,0:T(2,128)}, u32[]{:S(2)}) copy-start(f32[2,2,512]{2,1,0:T(2,128)} %copy-done.61) | copy-start | bytes 24580
  767.4 164.0 %reduce-scatter.12.cloned.1.call-start = ((), (), s32[]{:S(2)}) async-start(), calls=%async_computation.11 | async-start | bytes 4718592 | tf_op jit(solution)/shard_map/reduce_scatter | solution.py:591
  879.9 175.5 %all-reduce.3.cloned.1.call-start = ((), (), s32[]{:S(2)}) async-start(), calls=%async_computation.15 | async-start | bytes 6291456
  887.4 44.0 %copy-start.50 = (f32[2048]{0:T(1024)S(1)}, f32[2048]{0:T(1024)}, u32[]{:S(2)}) copy-start(f32[2048]{0:T(1024)} %copy-done.49) | copy-start | bytes 24580
  889.4 302.6 %reduce-scatter.16.cloned.1.call-start = ((), (), s32[]{:S(2)}) async-start(), calls=%async_computation.14 | async-start | bytes 1081344
  934.6 404.5 %reduce-scatter.14.cloned.1.call-start = ((), (), s32[]{:S(2)}) async-start(), calls=%async_computation.12 | async-start | bytes 8650752 | tf_op jit(solution)/shard_map/reduce_scatter | solution.py:752
  1058.2 52.2 %all-to-all-start.1 = ((bf16[8,3,64,256]{3,2,1,0:T(8,128)(2,1)}), bf16[8,3,64,256]{3,2,1,0:T(8,128)(2,1)}, u32[]{:S(2)}, u32[]{:S(2)}) async-start(bf16[8,3,64,256]{3,2,1,0:T(8,128)(2,1)} %copy.271), calls=%async_computation.3 | async-start | bytes 1572864 | tf_op jit(solution)/shard_map/all_to_all | solution.py:596
  (57 other events, 299.1 us)
Sparse Core Ops, SparseCore 0:
  28.4 64.6 all-gather.14
  95.6 36.4 all-gather.6
  135.0 77.3 all-gather.8
  217.0 49.9 reduce-scatter.9
  270.1 119.7 all-gather.10
  767.5 66.1 all-gather.12
  880.0 51.3 reduce-scatter.11
  934.3 121.0 all-reduce.2
  1057.7 134.3 reduce-scatter.15
  1194.3 144.7 reduce-scatter.13

commit v3 on v2

--- a/solution.py
+++ b/solution.py
@@ -559,6 +559,675 @@
     )(x_slots, g_slots, acts)
 
 
+def peer(here, rank):
+    return (here.layer * 2 + rank // here.n_dp, rank % here.n_dp)
+
+
+def others(here, group):
+    return [lax.rem(here.rank + k, group) for k in range(1, group)]
+
+
+def remote(src, dst, send, recv, device):
+    return pltpu.make_async_remote_copy(
+        src_ref=src, dst_ref=dst, send_sem=send, recv_sem=recv,
+        device_id=device, device_id_type=MESH,
+    )
+
+
+class LayerGather:
+    def __init__(self, here, own, buf, own_sem, send, recv):
+        self.here, self.own, self.buf = here, own, buf
+        self.own_sem, self.send, self.recv = own_sem, send, recv
+
+    def copy(self, kind):
+        here, buf = self.here, self.buf
+        wide = buf.shape[-1]
+        half = wide // 256 * 128
+        low, high, full = pl.ds(0, half), pl.ds(half, wide - half), pl.ds(0, wide)
+        n_dp, x, y, core = here.n_dp, here.x, here.y, here.core
+        over_x = y * n_dp + (1 - x) * 2 + core
+        over_y = (1 - y) * n_dp + x * 2 + core
+        across = (1 - y) * n_dp + (1 - x) * 2 + core
+        which, cols, device = {
+            0: (here.rank, low, here.over_x),
+            1: (here.rank, high, here.over_x),
+            2: (here.rank, low, here.over_y),
+            3: (here.rank, high, here.over_y),
+            4: (over_x, low, here.over_y),
+            5: (over_y, high, here.over_x),
+            6: (here.rank, full, here.sibling),
+            7: (over_x, full, here.sibling),
+            8: (over_y, full, here.sibling),
+            9: (across, full, here.sibling),
+        }[kind]
+        dst = buf.at[which, :, cols]
+        src = self.own.at[:, cols] if kind in (0, 1, 2, 3, 6) else dst
+        return remote(src, dst, self.send.at[kind], self.recv.at[kind], device)
+
+    def keep(self):
+        return pltpu.make_async_copy(self.own, self.buf.at[self.here.rank], self.own_sem.at[0])
+
+    def begin(self):
+        self.keep().start()
+        for kind in (0, 3, 1, 2, 6):
+            self.copy(kind).start()
+
+    def forward(self):
+        for got, then in ((0, 4), (3, 5), (1, 7), (2, 8)):
+            self.copy(got).wait_recv()
+            self.copy(then).start()
+
+    def across(self):
+        self.copy(4).wait_recv()
+        self.copy(5).wait_recv()
+        self.copy(9).start()
+
+    def end(self):
+        for kind in (6, 7, 8, 9):
+            self.copy(kind).wait_recv()
+        for kind in range(10):
+            self.copy(kind).wait_send()
+        self.keep().wait()
+
+
+class LayerSum:
+    def __init__(self, here, part, acc, sib, one, two, load, send, recv):
+        self.here, self.part, self.acc, self.sib = here, part, acc, sib
+        self.one, self.two, self.load_sem, self.send, self.recv = one, two, load, send, recv
+        wide = acc.shape[-1]
+        half = wide // 256 * 128
+        self.cols = (pl.ds(0, half), pl.ds(half, wide - half))
+
+    def load(self, q):
+        return pltpu.make_async_copy(
+            self.part.at[q * 2 + self.here.core], self.acc.at[q], self.load_sem.at[q]
+        )
+
+    def copy(self, kind):
+        here, acc = self.here, self.acc
+        x, y = here.x, here.y
+        low, high = self.cols
+        if kind < 4:
+            src, dst = self.part.at[kind * 2 + 1 - here.core], self.sib.at[kind]
+            device = here.sibling
+        elif kind < 6:
+            j = kind - 4
+            src, dst, device = acc.at[j * 2 + 1 - x, :, low], self.one.at[j, :, low], here.over_x
+        elif kind < 8:
+            j = kind - 6
+            src, dst = acc.at[(1 - y) * 2 + j, :, high], self.one.at[j, :, high]
+            device = here.over_y
+        elif kind == 8:
+            src, dst, device = acc.at[(1 - y) * 2 + x, :, low], self.two.at[:, low], here.over_y
+        else:
+            src, dst, device = acc.at[y * 2 + 1 - x, :, high], self.two.at[:, high], here.over_x
+        return remote(src, dst, self.send.at[kind], self.recv.at[kind], device)
+
+    def add(self, q, cols, got):
+        total = self.acc[q, :, cols].astype(F32) + got.astype(F32)
+        self.acc[q, :, cols] = total.astype(BF)
+
+    def begin(self):
+        for q in range(4):
+            self.copy(q).start()
+            self.load(q).start()
+
+    def first(self):
+        for q in range(4):
+            self.load(q).wait()
+            self.copy(q).wait_recv()
+            for cols in self.cols:
+                self.add(q, cols, self.sib[q, :, cols])
+        for kind in (4, 5, 6, 7):
+            self.copy(kind).start()
+
+    def second(self):
+        x, y = self.here.x, self.here.y
+        low, high = self.cols
+        for j in range(2):
+            self.copy(4 + j).wait_recv()
+            self.add(j * 2 + x, low, self.one[j, :, low])
+            self.copy(6 + j).wait_recv()
+            self.add(y * 2 + j, high, self.one[j, :, high])
+        self.copy(8).start()
+        self.copy(9).start()
+
+    def third(self, out):
+        own = self.here.y * 2 + self.here.x
+        for kind, cols in zip((8, 9), self.cols):
+            self.copy(kind).wait_recv()
+            out[:, cols] = self.acc[own, :, cols].astype(F32) + self.two[:, cols].astype(F32)
+        for kind in range(10):
+            self.copy(kind).wait_send()
+
+    @staticmethod
+    def scratch(rows, wide):
+        return [
+            pltpu.VMEM((4, rows, wide), BF), pltpu.VMEM((4, rows, wide), BF),
+            pltpu.VMEM((2, rows, wide), BF), pltpu.VMEM((rows, wide), BF),
+            pltpu.SemaphoreType.DMA((4,)),
+            pltpu.SemaphoreType.DMA((10,)), pltpu.SemaphoreType.DMA((10,)),
+        ]
+
+
+def comm_params(number):
+    return pltpu.CompilerParams(
+        collective_id=number, has_side_effects=True, vmem_limit_bytes=48 * 2**20
+    )
+
+
+def gather_kernel(n_dp, own, buf, own_sem, send, recv):
+    here = Place(n_dp)
+    greet([here.over_x, here.over_y, here.sibling])
+    job = LayerGather(here, own, buf, own_sem, send, recv)
+    job.begin()
+    job.forward()
+    job.across()
+    job.end()
+
+
+def layer_gather(value, n_dp):
+    rows, wide = value.shape
+    dma = pltpu.SemaphoreType.DMA
+    return pl.pallas_call(
+        functools.partial(gather_kernel, n_dp),
+        out_shape=jax.ShapeDtypeStruct((2 * n_dp, rows, wide), value.dtype),
+        in_specs=[ANY],
+        out_specs=ANY,
+        scratch_shapes=[dma((1,)), dma((10,)), dma((10,))],
+        compiler_params=comm_params(2),
+    )(value)
+
+
+def sum_kernel(n_dp, part, out, *scratch):
+    here = Place(n_dp)
+    greet([here.over_x, here.over_y, here.sibling])
+    job = LayerSum(here, part, *scratch)
+    job.begin()
+    job.first()
+    job.second()
+    job.third(out)
+
+
+def layer_sum(part, n_dp):
+    group, rows, wide = part.shape
+    return pl.pallas_call(
+        functools.partial(sum_kernel, n_dp),
+        out_shape=jax.ShapeDtypeStruct((rows, wide), F32),
+        in_specs=[ANY],
+        out_specs=VMEM,
+        scratch_shapes=LayerSum.scratch(rows, wide),
+        compiler_params=comm_params(3),
+    )(part)
+
+
+def stats_kernel(n_dp, value, out, land, send, recv):
+    here = Place(n_dp)
+    group = 2 * n_dp
+    ranks = others(here, group)
+    greet([peer(here, rank) for rank in ranks])
+
+    def copy(k):
+        return remote(
+            value, land.at[k], send.at[k], recv.at[k], peer(here, ranks[k])
+        )
+
+    for k in range(group - 1):
+        copy(k).start()
+    total = value[...]
+    for k in range(group - 1):
+        copy(k).wait_recv()
+        total += land[k]
+    out[...] = total
+    for k in range(group - 1):
+        copy(k).wait_send()
+
+
+def layer_stats(value, n_dp):
+    dma = pltpu.SemaphoreType.DMA
+    peers = 2 * n_dp - 1
+    flat = value.reshape(-1, 128)
+    out = pl.pallas_call(
+        functools.partial(stats_kernel, n_dp),
+        out_shape=jax.ShapeDtypeStruct(flat.shape, F32),
+        in_specs=[VMEM],
+        out_specs=VMEM,
+        scratch_shapes=[pltpu.VMEM((peers,) + flat.shape, F32), dma((peers,)), dma((peers,))],
+        compiler_params=comm_params(4),
+    )(flat)
+    return out.reshape(value.shape)
+
+
+def front_kernel(
+    n_dp, layers, x_own, w_q, w_k, w_v, w_o, small,
+    x_all, qkv, wo, small_all, wo_col,
+    own_sem, x_send, x_recv, a_keep, a_send, a_recv, up_send, up_recv, down_send, down_recv,
+    o_keep, o_send, o_recv, s_send, s_recv, t_send, t_recv,
+):
+    here = Place(n_dp)
+    group = 2 * n_dp
+    layer, rank = here.layer, here.rank
+    own = w_q.shape[0]
+    cols = qkv.shape[-1]
+    ranks = others(here, group)
+    away = [flip(layer, i, layers) for i in range(1, layers)]
+    greet([peer(here, r) for r in ranks] + [here.at_layer(z) for z in away])
+    gather = LayerGather(here, x_own, x_all, own_sem, x_send, x_recv)
+    weights = (w_q, w_k, w_v)
+
+    def rows_at(index):
+        return pl.ds(pl.multiple_of(index * own, own), own)
+
+    def block_cols(index):
+        return pl.ds(pl.multiple_of(index * cols, cols), cols)
+
+    def swap(w, k):
+        return remote(
+            weights[w].at[:, block_cols(ranks[k])], qkv.at[w, layer, rows_at(rank)],
+            a_send.at[w, k], a_recv.at[w, k], peer(here, ranks[k]),
+        )
+
+    def swap_own(w):
+        return pltpu.make_async_copy(
+            weights[w].at[:, block_cols(rank)], qkv.at[w, layer, rows_at(rank)], a_keep.at[w]
+        )
+
+    def small_out(i):
+        ref = small_all.at[layer, rank]
+        return remote(small, ref, s_send.at[i], s_recv.at[i], here.at_layer(away[i]))
+
+    def small_keep():
+        return pltpu.make_async_copy(small, small_all.at[layer, rank], a_keep.at[3])
+
+    def small_share(k):
+        ref = small_all.at[:, rank]
+        return remote(ref, ref, t_send.at[k], t_recv.at[k], peer(here, ranks[k]))
+
+    def o_own():
+        return pltpu.make_async_copy(w_o, wo_col.at[layer], a_keep.at[4])
+
+    for w in range(3):
+        swap_own(w).start()
+        for k in range(group - 1):
+            swap(w, k).start()
+    o_own().start()
+    small_keep().start()
+    for i in range(layers - 1):
+        small_out(i).start()
+    gather.begin()
+    for w in range(3):
+        swap_own(w).wait()
+        for k in range(group - 1):
+            swap(w, k).wait_recv()
+    o_own().wait()
+
+    def chain(which, up, s):
+        block = layer - s if up else layer + s
+        ref = qkv.at[:, block] if which == 0 else wo_col.at[block]
+        device = here.at_layer(layer + 1 if up else layer - 1)
+        sems = (up_send, up_recv) if up else (down_send, down_recv)
+        return remote(ref, ref, sems[0].at[which, s], sems[1].at[which, s], device)
+
+    def step(which, s, wait):
+        for up in (True, False):
+            leaves = (
+                jnp.logical_and(layer + 1 < layers, layer - s >= 0) if up
+                else jnp.logical_and(layer >= 1, layer + s < layers)
+            )
+            comes = layer - 1 - s >= 0 if up else layer + 1 + s < layers
+            if wait:
+                @pl.when(comes)
+                def _():
+                    chain(which, up, s).wait_recv()
+            else:
+                @pl.when(leaves)
+                def _():
+                    chain(which, up, s).start()
+
+    step(0, 0, False)
+    gather.forward()
+    step(1, 0, False)
+    gather.across()
+    small_keep().wait()
+    for i in range(layers - 1):
+        small_out(i).wait_recv()
+    for k in range(group - 1):
+        small_share(k).start()
+    for s in range(layers - 1):
+        step(0, s, True)
+        if s + 1 < layers - 1:
+            step(0, s + 1, False)
+        step(1, s, True)
+        if s + 1 < layers - 1:
+            step(1, s + 1, False)
+
+    def share(z):
+        number = z * group + rank
+        target, index = number // layers, number % layers
+
+        def far():
+            return remote(
+                wo_col.at[z], wo.at[index], o_send.at[z], o_recv.at[index], peer(here, target)
+            )
+
+        def near():
+            return pltpu.make_async_copy(wo_col.at[z], wo.at[index], o_keep.at[index])
+
+        return target, far, near
+
+    def source(index):
+        number = rank * layers + index
+        return number % group
+
+    for z in range(layers):
+        target, far, near = share(z)
+
+        @pl.when(target != rank)
+        def _():
+            far().start()
+
+        @pl.when(target == rank)
+        def _():
+            near().start()
+
+    for index in range(layers):
+        @pl.when(source(index) != rank)
+        def _():
+            remote(
+                wo_col.at[0], wo.at[index], o_send.at[0], o_recv.at[index], here.sibling
+            ).wait_recv()
+
+        @pl.when(source(index) == rank)
+        def _():
+            pltpu.make_async_copy(wo_col.at[0], wo.at[index], o_keep.at[index]).wait()
+
+    gather.end()
+    for k in range(group - 1):
+        small_share(k).wait_recv()
+    for w in range(3):
+        for k in range(group - 1):
+            swap(w, k).wait_send()
+    for i in range(layers - 1):
+        small_out(i).wait_send()
+    for k in range(group - 1):
+        small_share(k).wait_send()
+    for z in range(layers):
+        target, far, near = share(z)
+
+        @pl.when(target != rank)
+        def _():
+            far().wait_send()
+
+    for which in range(2):
+        for s in range(layers - 1):
+            @pl.when(jnp.logical_and(layer + 1 < layers, layer - s >= 0))
+            def _():
+                chain(which, True, s).wait_send()
+
+            @pl.when(jnp.logical_and(layer >= 1, layer + s < layers))
+            def _():
+                chain(which, False, s).wait_send()
+
+
+def run_front(x_own, w_q, w_k, w_v, w_o, small, n_dp, n_dev):
+    rows, width = x_own.shape
+    own = w_q.shape[0]
+    group = 2 * n_dp
+    layers = n_dev // group
+    cols = width // group
+    dma = pltpu.SemaphoreType.DMA
+    shape = jax.ShapeDtypeStruct
+    chain = dma((2, layers))
+    result = pl.pallas_call(
+        functools.partial(front_kernel, n_dp, layers),
+        out_shape=(
+            shape((group, rows, width), BF),
+            shape((3, layers, group * own, cols), BF),
+            shape((layers, own, width), BF),
+            shape((layers, group) + small.shape, BF),
+            shape((layers, own, width), BF),
+        ),
+        in_specs=[ANY] * 6,
+        out_specs=(ANY,) * 5,
+        scratch_shapes=[
+            dma((1,)), dma((10,)), dma((10,)), dma((5,)),
+            dma((3, group - 1)), dma((3, group - 1)), chain, chain, chain, chain,
+            dma((layers,)), dma((layers,)), dma((layers,)),
+            dma((layers,)), dma((layers,)), dma((group,)), dma((group,)),
+        ],
+        compiler_params=comm_params(5),
+    )(x_own, w_q, w_k, w_v, w_o, small)
+    x_all, qkv, wo, small_all, _ = result
+    return (
+        x_all.reshape(group * rows, width), qkv.reshape(3, width, cols),
+        wo.reshape(cols, width), small_all.reshape(width, -1),
+    )
+
+
+def back_kernel(
+    n_dp, layers, part, gw, go, small,
+    out, grad_w, grad_o, small_out,
+    acc, sib, one, two, load_sem, n_send, n_recv,
+    acc_w, acc_o, up_w, up_o, down_w, down_o, swapped, s_own, s_land, s_sum, s_far,
+    w_load, o_keep, o_send, o_recv, up_send, up_recv, down_send, down_recv,
+    a_keep, a_send, a_recv, s_keep, s_send, s_recv, t_send, t_recv,
+):
+    here = Place(n_dp)
+    group = 2 * n_dp
+    layer, rank = here.layer, here.rank
+    own = grad_w.shape[1]
+    cols = gw.shape[-1]
+    ranks = others(here, group)
+    away = [flip(layer, i, layers) for i in range(1, layers)]
+    greet([peer(here, r) for r in ranks] + [here.at_layer(z) for z in away])
+    job = LayerSum(here, part, acc, sib, one, two, load_sem, n_send, n_recv)
+
+    def bring():
+        return pltpu.make_async_copy(gw, acc_w, w_load.at[0])
+
+    def share(i):
+        number = rank * layers + i
+        z, target = number // group, number % group
+
+        def far():
+            return remote(
+                go.at[i], acc_o.at[z], o_send.at[i], o_recv.at[z], peer(here, target)
+            )
+
+        def near():
+            return pltpu.make_async_copy(go.at[i], acc_o.at[z], o_keep.at[z])
+
+        return target, far, near
+
+    def small_swap(k):
+        return remote(
+            small.at[:, ranks[k]], s_land.at[k], s_send.at[k], s_recv.at[k], peer(here, ranks[k])
+        )
+
+    def small_keep():
+        return pltpu.make_async_copy(small.at[:, rank], s_own, s_keep.at[0])
+
+    bring().start()
+    job.begin()
+    for i in range(layers):
+        target, far, near = share(i)
+
+        @pl.when(target != rank)
+        def _():
+            far().start()
+
+        @pl.when(target == rank)
+        def _():
+            near().start()
+    small_keep().start()
+    for k in range(group - 1):
+        small_swap(k).start()
+
+    def chain(which, up, z):
+        acc_ref = (acc_w.at[:, z], acc_o.at[z])[which]
+        land = ((up_w, up_o) if up else (down_w, down_o))[which].at[z]
+        sems = (up_send, up_recv) if up else (down_send, down_recv)
+        device = here.at_layer(layer + 1 if up else layer - 1)
+        return remote(acc_ref, land, sems[0].at[which, z], sems[1].at[which, z], device)
+
+    def take(which, up, z):
+        chain(which, up, z).wait_recv()
+        if which == 0:
+            land = up_w if up else down_w
+            for w in range(3):
+                total = acc_w[w, z].astype(F32) + land[z, w].astype(F32)
+                acc_w[w, z] = total.astype(BF)
+        else:
+            land = up_o if up else down_o
+            acc_o[z] = (acc_o[z].astype(F32) + land[z].astype(F32)).astype(BF)
+
+    def hop(which, d):
+        @pl.when(layer + d < layers)
+        def _():
+            @pl.when(layer > 0)
+            def _():
+                take(which, True, layer + d)
+            chain(which, True, layer + d).start()
+
+        @pl.when(layer - d >= 0)
+        def _():
+            @pl.when(layer + 1 < layers)
+            def _():
+                take(which, False, layer - d)
+            chain(which, False, layer - d).start()
+
+    bring().wait()
+    hop(0, layers - 1)
+    job.first()
+    for z in range(layers):
+        source = (z * group + rank) // layers
+
+        @pl.when(source != rank)
+        def _():
+            remote(
+                go.at[0], acc_o.at[z], o_send.at[0], o_recv.at[z], here.sibling
+            ).wait_recv()
+
+        @pl.when(source == rank)
+        def _():
+            pltpu.make_async_copy(go.at[0], acc_o.at[z], o_keep.at[z]).wait()
+    hop(1, layers - 1)
+    small_keep().wait()
+    total = s_own[...]
+    for k in range(group - 1):
+        small_swap(k).wait_recv()
+        total += s_land[k]
+    s_sum[...] = total
+
+    def small_far(i):
+        return remote(
+            s_sum.at[away[i]], s_far.at[i], t_send.at[i], t_recv.at[i], here.at_layer(away[i])
+        )
+
+    for i in range(layers - 1):
+        small_far(i).start()
+    job.second()
+    for d in range(layers - 2, 0, -1):
+        hop(0, d)
+        hop(1, d)
+    job.third(out)
+    total = s_sum[layer]
+    for i in range(layers - 1):
+        small_far(i).wait_recv()
+        total += s_far[i]
+    small_out[...] = total
+
+    for which in range(2):
+        @pl.when(layer > 0)
+        def _():
+            take(which, True, layer)
+
+        @pl.when(layer + 1 < layers)
+        def _():
+            take(which, False, layer)
+
+    def rows_at(index):
+        return pl.ds(pl.multiple_of(index * own, own), own)
+
+    def swap(k):
+        return remote(
+            acc_w.at[:, layer, rows_at(ranks[k])], swapped.at[rank],
+            a_send.at[k], a_recv.at[k], peer(here, ranks[k]),
+        )
+
+    def swap_own():
+        return pltpu.make_async_copy(
+            acc_w.at[:, layer, rows_at(rank)], swapped.at[rank], a_keep.at[0]
+        )
+
+    swap_own().start()
+    for k in range(group - 1):
+        swap(k).start()
+    grad_o[...] = acc_o[layer].astype(F32)
+    swap_own().wait()
+    for k in range(group - 1):
+        swap(k).wait_recv()
+    for r in range(group):
+        for w in range(3):
+            grad_w[w, :, r * cols : (r + 1) * cols] = swapped[r, w].astype(F32)
+
+    for k in range(group - 1):
+        swap(k).wait_send()
+        small_swap(k).wait_send()
+    for i in range(layers - 1):
+        small_far(i).wait_send()
+    for i in range(layers):
+        target, far, near = share(i)
+
+        @pl.when(target != rank)
+        def _():
+            far().wait_send()
+    for which in range(2):
+        for d in range(1, layers):
+            @pl.when(layer + d < layers)
+            def _():
+                chain(which, True, layer + d).wait_send()
+
+            @pl.when(layer - d >= 0)
+            def _():
+                chain(which, False, layer - d).wait_send()
+
+
+def run_back(part, gw, go, small, n_dp):
+    group, rows, width = part.shape
+    cols = gw.shape[-1]
+    layers = small.shape[0]
+    own = small.shape[2]
+    dma = pltpu.SemaphoreType.DMA
+    shape = jax.ShapeDtypeStruct
+    deep = pltpu.VMEM((layers, 3, group * own, cols), BF)
+    flat = pltpu.VMEM((layers, own, width), BF)
+    chain = dma((2, layers))
+    tiny = small.shape[2:]
+    return pl.pallas_call(
+        functools.partial(back_kernel, n_dp, layers),
+        out_shape=(
+            shape((rows, width), F32), shape((3, own, width), F32),
+            shape((own, width), F32), shape(tiny, F32),
+        ),
+        in_specs=[ANY] * 4,
+        out_specs=(VMEM,) * 4,
+        scratch_shapes=LayerSum.scratch(rows, width) + [
+            pltpu.VMEM((3, layers, group * own, cols), BF), flat, deep, flat, deep, flat,
+            pltpu.VMEM((group, 3, own, cols), BF),
+            pltpu.VMEM((layers,) + tiny, F32), pltpu.VMEM((group - 1, layers) + tiny, F32),
+            pltpu.VMEM((layers,) + tiny, F32), pltpu.VMEM((layers,) + tiny, F32),
+            dma((1,)), dma((layers,)), dma((layers,)), dma((layers,)),
+            chain, chain, chain, chain,
+            dma((1,)), dma((group - 1,)), dma((group - 1,)),
+            dma((1,)), dma((group - 1,)), dma((group - 1,)), dma((layers,)), dma((layers,)),
+        ],
+        compiler_params=comm_params(6),
+    )(
+        part, gw.reshape(3, layers, group * own, cols), go.reshape(layers, own, width), small
+    )
+
+
 def ein(spec, left, right):
     return jnp.einsum(spec, left, right, preferred_element_type=F32)
 
@@ -580,28 +1249,7 @@
 def build(n_ep, n_dp):
     n_dev = n_ep * n_dp
     group = 2 * n_dp
-    n_group = n_dev // group
-    rows_of = [[g * group + r for r in range(group)] for g in range(n_group)]
-    cols_of = [[g * group + r for g in range(n_group)] for r in range(group)]
-
-    def group_gather(value, axis=0):
-        return lax.all_gather(value, AXES, axis=axis, tiled=True, axis_index_groups=rows_of)
-
-    def group_scatter(value):
-        return lax.psum_scatter(
-            value, AXES, scatter_dimension=0, tiled=True, axis_index_groups=rows_of
-        )
-
-    def group_swap(value):
-        return lax.all_to_all(value, AXES, 0, 0, tiled=True, axis_index_groups=rows_of)
-
-    def column_gather(value):
-        return lax.all_gather(value, AXES, axis=0, tiled=False, axis_index_groups=cols_of)
-
-    def column_scatter(value):
-        return lax.psum_scatter(
-            value, AXES, scatter_dimension=0, tiled=False, axis_index_groups=cols_of
-        )
+    layers = n_dev // group
 
     def shards(
         layer_input, grad_out, attn_gain, w_q, w_k, w_v, q_gain, k_gain, w_o, ffn_gain,
@@ -620,30 +1268,27 @@
         top = routes.shape[1]
         cap = 2 * rows * top // experts
 
-        qkv = jnp.stack([w_q, w_k, w_v]).reshape(3, own, group, cols).transpose(2, 0, 1, 3)
-        qkv = group_swap(qkv)
-        qkv = column_gather(qkv)
-        qkv = qkv.transpose(2, 0, 1, 3, 4).reshape(3, width, cols)
+        gains = jnp.stack([attn_gain, q_gain, k_gain, ffn_gain], axis=1)
+        small = jnp.concatenate(
+            [router, gains, jnp.zeros((own, 128 - experts - 4), BF)], axis=1
+        )
+        group_input, qkv, wo, small = run_front(
+            layer_input, w_q, w_k, w_v, w_o, small, n_dp, n_dev
+        )
         wq, wk, wv = qkv[0], qkv[1], qkv[2]
-        full_o = lax.all_gather(w_o, AXES, axis=0, tiled=True)
-        wo = lax.dynamic_slice_in_dim(full_o, rank * cols, cols, 0)
-
-        small = jnp.concatenate(
-            [jnp.stack([attn_gain, q_gain, k_gain, ffn_gain], axis=1), router], axis=1
-        )
-        small = lax.all_gather(small, AXES, axis=0, tiled=True)
-        full_attn_gain = small[:, 0].astype(F32)
-        full_ffn_gain = small[:, 3].astype(F32)
-        full_router = small[:, 4:]
-        q_gain_own = lax.dynamic_slice_in_dim(small[:, 1], rank * cols, cols, 0).astype(F32)
-        k_gain_own = lax.dynamic_slice_in_dim(small[:, 2], rank * cols, cols, 0).astype(F32)
-
-        group_input = group_gather(layer_input).astype(F32)
-        normed = (group_input * inv_rms(group_input) * full_attn_gain).astype(BF)
+        full_router = small[:, :experts]
+        full_attn_gain = small[:, experts].astype(F32)
+        full_ffn_gain = small[:, experts + 3].astype(F32)
+        head_gains = lax.dynamic_slice_in_dim(small, rank * cols, cols, 0).astype(F32)
+        q_gain_own, k_gain_own = head_gains[:, experts + 1], head_gains[:, experts + 2]
+
+        group_input = group_input.astype(F32)
+        group_root = inv_rms(group_input)
+        normed = (group_input * group_root * full_attn_gain).astype(BF)
         q_raw, k_raw = dot(normed, wq), dot(normed, wk)
         v_low = dot(normed, wv).astype(BF)
         squares = jnp.stack([jnp.sum(q_raw * q_raw, -1), jnp.sum(k_raw * k_raw, -1)])
-        squares = lax.psum(squares, AXES, axis_index_groups=rows_of)
+        squares = layer_stats(squares, n_dp)
         roots = lax.rsqrt(squares / width + EPSILON)
         q_root, k_root = roots[0][:, None], roots[1][:, None]
         half_dim = HEAD_DIM // 2
@@ -668,7 +1313,7 @@
         probs = jax.nn.softmax(scores, axis=-1)
         probs_low = probs.astype(BF)
         mixed = ein("bhqk,bkhd->bqhd", probs_low, values).astype(BF).reshape(-1, cols)
-        attn_out = group_scatter(dot(mixed, wo).astype(BF)).astype(F32)
+        attn_out = layer_sum(dot(mixed, wo).astype(BF).reshape(group, rows, width), n_dp)
         residual = layer_input.astype(F32) + attn_out
         res_root = inv_rms(residual)
         res_n = residual * res_root
@@ -713,7 +1358,7 @@
         dn = grad_n2 * full_ffn_gain
         grad_residual = grad_y + res_root * (dn - res_n * jnp.mean(dn * res_n, -1, keepdims=True))
 
-        gao = group_gather(grad_residual.astype(BF))
+        gao = layer_gather(grad_residual.astype(BF), n_dp).reshape(group * rows, width)
         grad_wo = ein("td,te->de", mixed, gao)
         grad_mixed = ein("te,de->td", gao, wo).astype(BF).reshape(by_head)
         grad_values = ein("bhqk,bqhd->bkhd", probs_low, grad_mixed)
@@ -726,49 +1371,40 @@
         grad_q_gain, grad_k_gain = jnp.sum(gq * q_n, axis=0), jnp.sum(gk * k_n, axis=0)
         gq, gk = gq * q_gain_own, gk * k_gain_own
         inner = jnp.stack([jnp.sum(gq * q_n, -1), jnp.sum(gk * k_n, -1)])
-        inner = lax.psum(inner, AXES, axis_index_groups=rows_of) / width
+        inner = layer_stats(inner, n_dp) / width
         gq = (q_root * (gq - q_n * inner[0][:, None])).astype(BF)
         gk = (k_root * (gk - k_n * inner[1][:, None])).astype(BF)
         gv = grad_values.reshape(-1, cols).astype(BF)
         grad_normed = ein("te,de->td", gq, wq) + ein("te,de->td", gk, wk)
         grad_normed = grad_normed + ein("te,de->td", gv, wv)
-        grad_normed = group_scatter(grad_normed.astype(BF)).astype(F32)
+        grad_attn_gain = jnp.sum(grad_normed * (group_input * group_root), axis=0)
+        grad_qkv = jnp.stack([ein("td,te->de", normed, part) for part in (gq, gk, gv)]).astype(BF)
+
+        def spread(part):
+            return lax.dynamic_update_slice_in_dim(jnp.zeros((width,), F32), part, rank * cols, 0)
+
+        gain_grads = jnp.stack(
+            [grad_attn_gain, spread(grad_q_gain), spread(grad_k_gain), grad_ffn_gain], axis=1
+        )
+        small_grads = jnp.concatenate(
+            [grad_router, gain_grads, jnp.zeros((width, 128 - experts - 4), F32)], axis=1
+        )
+        grad_normed, grad_qkv, grad_o, small_grads = run_back(
+            grad_normed.astype(BF).reshape(group, rows, width), grad_qkv, grad_wo.astype(BF),
+            small_grads.reshape(layers, group, own, 128), n_dp,
+        )
         own_input = layer_input.astype(F32)
         in_root = inv_rms(own_input)
         in_n = own_input * in_root
-        grad_attn_gain = jnp.sum(grad_normed * in_n, axis=0)
         dn = grad_normed * full_attn_gain
         grad_input = grad_residual + in_root * (
             dn - in_n * jnp.mean(dn * in_n, -1, keepdims=True)
         )
-        grad_qkv = jnp.stack(
-            [ein("td,te->de", normed, part) for part in (gq, gk, gv)]
-        ).astype(BF)
-        grad_qkv = grad_qkv.reshape(3, n_group, group, own, cols).transpose(1, 2, 0, 3, 4)
-        grad_qkv = column_scatter(grad_qkv)
-        grad_qkv = group_swap(grad_qkv).transpose(1, 2, 0, 3).reshape(3, own, width).astype(F32)
-        grad_o = jnp.zeros((width, width), BF)
-        grad_o = lax.dynamic_update_slice_in_dim(grad_o, grad_wo.astype(BF), rank * cols, 0)
-        grad_o = lax.psum_scatter(grad_o, AXES, scatter_dimension=0, tiled=True).astype(F32)
-
-        def spread(part):
-            return lax.dynamic_update_slice_in_dim(jnp.zeros((width,), F32), part, rank * cols, 0)
-
-        small_grads = jnp.concatenate(
-            [
-                jnp.stack(
-                    [grad_attn_gain, spread(grad_q_gain), spread(grad_k_gain), grad_ffn_gain],
-                    axis=1,
-                ),
-                grad_router,
-            ],
-            axis=1,
-        )
-        small_grads = lax.psum_scatter(small_grads, AXES, scatter_dimension=0, tiled=True)
+        gain_grads = small_grads[:, experts : experts + 4]
         return (
-            output, grad_input, small_grads[:, 0], grad_qkv[0], grad_qkv[1], grad_qkv[2],
-            small_grads[:, 1], small_grads[:, 2], grad_o, small_grads[:, 3], small_grads[:, 4:],
-            grad_w_gate, grad_w_up, grad_w_down,
+            output, grad_input, gain_grads[:, 0], grad_qkv[0], grad_qkv[1], grad_qkv[2],
+            gain_grads[:, 1], gain_grads[:, 2], grad_o, gain_grads[:, 3],
+            small_grads[:, :experts], grad_w_gate, grad_w_up, grad_w_down,
         )
 
     return shards

time: 1360 us -> 969 us (0.71)
  waiting for transfers between devices: 681 us -> 0.02 us
  Pallas kernels: 416 us -> 775 us
  blocking collectives: 89.1 us -> 0 us
  local copies, waits for them, and re-layouts: 51.2 us -> 67.6 us
    pallas_call x0 -> x6, Pallas kernels: none -> 357 us  [the longest x1 179 us: run_front(): pl.pallas_call(functools.partial(front_kernel, n_dp, layers), out_shape=(...]
    reduce_scatter x3 -> x0, waiting for transfers between devices: 231 us -> none  [the longest x1 142 us: shards(): lax.psum_scatter(grad_o, AXES, scatter_dimension=0, tiled=True).astype(F32)]
    unnamed x12 -> x1, waiting for transfers between devices: 189 us -> 0.02 us
    all_gather x4 -> x0, waiting for transfers between devices: 142 us -> none  [the longest x2 101 us: group_gather(): lax.all_gather(value, AXES, axis=axis, tiled=True, axis_index_groups=rows...]
    all_gather x1, waiting for transfers between devices: 118 us -> 0.01 us  [shards(): lax.all_gather(sent, AXES, axis=0, tiled=True).reshape(n_dev, rows, -1)]
    all_gather x1 -> x0, blocking collectives: 43.9 us -> none  [shards(): small = lax.all_gather(small, AXES, axis=0, tiled=True)]
    psum x2 -> x0, blocking collectives: 27.6 us -> none  [the longest x1 14 us: shards(): squares = lax.psum(squares, AXES, axis_index_groups=rows_of)]
    all_to_all x1 -> x0, blocking collectives: 17.6 us -> none  [group_swap(): lax.all_to_all(value, AXES, 0, 0, tiled=True, axis_index_groups=rows_of)]
  transfers between devices with their start and end apart: 11 -> 1, of which waited for: 10 -> 0; matrix products, arithmetic and copies ran while one was open for 7% -> 6% of each run, Pallas kernels for 4% -> 22%
where the time goes in v3:
time: 969 us; the launch traced here: 953 us
  Pallas kernels  775 us (80%)
  local copies, waits for them, and re-layouts  67.6 us (7%)
  matrix products  62.4 us (6%)
  other arithmetic  32.2 us (3%)
  between operations  15.7 us (2%)
    pallas_call x1, Pallas kernels, run_experts(): pl.pallas_call(functools.partial(experts_kernel, n_dp, experts), out_shap...  370 us
    pallas_call x1, Pallas kernels, run_front(): pl.pallas_call(functools.partial(front_kernel, n_dp, layers), out_shape=(...  179 us
    pallas_call x1, Pallas kernels, run_back(): pl.pallas_call(functools.partial(back_kernel, n_dp, layers), out_shape=(s...  120 us
    dot_general x15, matrix products, ein(): return jnp.einsum(spec, left, right, preferred_element_type=F32)  48.2 us
    pallas_call x1, Pallas kernels, run_weights(): pl.pallas_call(weights_kernel, grid=(local, total // tile), out_shape=(ja...  47.6 us
    pallas_call x1, Pallas kernels, layer_sum(): pl.pallas_call(functools.partial(sum_kernel, n_dp), out_shape=jax.ShapeDt...  26.8 us
    pallas_call x1, Pallas kernels, layer_gather(): pl.pallas_call(functools.partial(gather_kernel, n_dp), out_shape=jax.Shap...  20.7 us
  transfers between devices with their start and end apart: 1, of which 0 were waited for; matrix products, arithmetic and copies ran while one was open for 6% of the time, Pallas kernels for 22%

profile of v3, /device:TPU:0, one launch (start us, length us, event | category | flops | bytes accessed | tf_op | source)
XLA Modules:
  0.0 952.7 jit_solution(14192502090884980790)
XLA Ops:
  18.9 178.5 %shard_map.254 = (bf16[8,128,2048]{2,1,0:T(8,128)(2,1)}, bf16[3,4,512,256]{3,2,1,0:T(8,128)(2,1)}, bf16[4,64,2048]{2,1,0:T(8,128)(2,1)S(1)}, bf16[4,8,64,128]{3,2,1,0:T(8,128)(2,1)S(1)}, bf16[4,64,2048]{2,1,0:T(8,128)(2,1)}) custom-call(bf16[128,2048]{1,0:T(8,128)(2,1)S(1)} %copy-done.1, bf16[64,2048]{1,0:T(8,128)(2,1)S(1)} %copy-done.8, ...), custom_call_target="tpu_custom_call" | custom-call | tf_op jit(solution)/shard_map/pallas_call | solution.py:981
  199.3 3.2 multiply_reduce_fusion.1
  210.8 3.9 multiply_reduce_fusion.10
  217.2 5.9 shard_map.255
  224.9 3.2 reshape.317
  237.8 5.2 fusion.52
  243.0 2.7 fusion.10
  247.5 26.8 %shard_map.256 = f32[128,2048]{1,0:T(8,128)S(1)} custom-call(bf16[8,128,2048]{2,1,0:T(8,128)(2,1)S(1)} %bitcast.141), custom_call_target="tpu_custom_call" | custom-call | tf_op jit(solution)/shard_map/pallas_call | solution.py:754
  277.6 6.4 copy.185
  288.4 370.1 %shard_map.257 = (f32[128,2048]{1,0:T(8,128)}, f32[128,2176]{1,0:T(8,128)}, bf16[8,32,32,2048]{3,2,1,0:T(8,128)(2,1)}, bf16[8,32,32,2048]{3,2,1,0:T(8,128)(2,1)}...) custom-call(bf16[128,2176]{1,0:T(8,128)(2,1)} %concatenate.48.x_own,, ...), custom_call_target="tpu_custom_call" | custom-call | flops 51539607552 | bytes 209715200 | tf_op jit(solution)/shard_map/pallas_call | solution.py:473
  664.6 20.7 %shard_map.258 = bf16[8,128,2048]{2,1,0:T(8,128)(2,1)S(1)} custom-call(bf16[128,2048]{1,0:T(8,128)(2,1)S(1)} %fusion.47.own), custom_call_target="tpu_custom_call" | custom-call | tf_op jit(solution)/shard_map/pallas_call | solution.py:732
  689.3 3.2 fusion.11
  692.8 2.7 multiply_reduce_fusion.2
  696.7 4.7 multiply_convert_fusion.2
  706.3 5.3 shard_map.259
  713.1 6.1 fusion.54
  719.5 4.7 fusion.55
  725.4 11.8 %multiply_reduce_fusion = (f32[2048]{0:T(1024)S(1)}, bf16[1024,2048]{1,0:T(8,128)(2,1)}, bf16[1024,2048]{1,0:T(8,128)(2,1)}) fusion(bf16[8,128,2048]{2,1,0:T(8,128)(2,1)} %get-tuple-element.30, f32[1024]{0:T(1024)S(1)} %copy-done.67, f32[2048]{0:T(1024)S(1)} %bitcast.178, bf16[2048,256]{1,0:T(8,128)(2,1)S(1)} %bitcast.168, ...), kind=kOutput, calls=%fused_computation.2 | convolution fusion | flops 1092614144 | bytes 30953472 | tf_op jit(solution)/shard_map/te,de->td/dot_general | solution.py:1232
  737.2 6.6 copy.202
  743.8 3.6 fusion.6
  761.9 3.6 fusion.7
  768.7 4.0 concatenate.57.small
  772.7 119.7 %shard_map.260 = (f32[128,2048]{1,0:T(8,128)S(1)}, f32[3,64,2048]{2,1,0:T(8,128)S(1)}, f32[64,2048]{1,0:T(8,128)S(1)}, f32[64,128]{1,0:T(8,128)S(1)}) custom-call(bf16[8,128,2048]{2,1,0:T(8,128)(2,1)} %bitcast.152, bf16[3,4,512,256]{3,2,1,0:T(8,128)(2,1)} %pad_maximum_fusion.gw, bf16[4,64,2048]{2,1,0:T(8,128)(2,1)S(1)} %bitcast.148, ...), custom_call_target="tpu_custom_call" | custom-call | tf_op jit(solution)/shard_map/pallas_call | solution.py:1207
  896.3 47.6 %shard_map.261 = (f32[8,2048,256]{2,1,0:T(8,128)}, f32[8,2048,256]{2,1,0:T(8,128)}, f32[8,256,2048]{2,1,0:T(8,128)}) custom-call(bf16[8,1024,2048]{2,1,0:T(8,128)(2,1)} %bitcast.203, bf16[8,1024,2048]{2,1,0:T(8,128)(2,1)} %bitcast.204, bf16[3,8,1024,256]{3,2,1,0:T(8,128)(2,1)} %get-tuple-element.42.acts), custom_call_target="tpu_custom_call" | custom-call | flops 25769803776 | bytes 136314880 | tf_op jit(solution)/shard_map/pallas_call | solution.py:545
  (262 shorter events, 86.5 us)
Async XLA Ops:
  7.2 277.3 %all-gather.2.cloned.1.call-start = ((), (), s32[]{:S(2)}) async-start(), calls=%async_computation | async-start | bytes 18382848 | tf_op jit(solution)/shard_map/all_gather | solution.py:1333
  8.1 5.2 copy-start.50
  197.4 48.7 %copy-start.6 = (bf16[4,64,2048]{2,1,0:T(8,128)(2,1)}, bf16[4,64,2048]{2,1,0:T(8,128)(2,1)S(1)}, u32[]{:S(2)}) copy-start(bf16[4,64,2048]{2,1,0:T(8,128)(2,1)S(1)} %get-tuple-element.33) | copy-start | bytes 3145732
  197.4 78.3 %copy-start = (bf16[4,8,64,128]{3,2,1,0:T(8,128)(2,1)}, bf16[4,8,64,128]{3,2,1,0:T(8,128)(2,1)S(1)}, u32[]{:S(2)}) copy-start(bf16[4,8,64,128]{3,2,1,0:T(8,128)(2,1)S(1)} %get-tuple-element.31) | copy-start | bytes 1572868
  199.2 5.5 copy-start.54
  214.7 8.4 copy-start.17
  223.1 8.6 copy-start.65
  223.2 8.5 copy-start.60
  224.9 5.6 copy-start.19
  237.8 7.9 copy-start.42
  237.8 5.2 copy-start.52
  247.5 26.9 %copy-start.29 = (f32[2048,1]{1,0:T(8,128)S(1)}, f32[2048,1]{1,0:T(8,128)}, u32[]{:S(2)}) copy-start(f32[2048,1]{1,0:T(8,128)} %get-tuple-element.78) | copy-start | bytes 24580
  247.5 27.2 %copy-start.2 = (bf16[128,2048]{1,0:T(8,128)(2,1)S(1)}, bf16[128,2048]{1,0:T(8,128)(2,1)}, u32[]{:S(2)}) copy-start(bf16[128,2048]{1,0:T(8,128)(2,1)} %x_own.1) | copy-start | bytes 1572868
  274.7 9.3 copy-start.56
  275.8 8.2 copy-start.24
  276.4 7.6 copy-start.45
  661.8 25.4 %copy-start.7 = (bf16[4,64,2048]{2,1,0:T(8,128)(2,1)S(1)}, bf16[4,64,2048]{2,1,0:T(8,128)(2,1)}, u32[]{:S(2)}) copy-start(bf16[4,64,2048]{2,1,0:T(8,128)(2,1)} %copy-done.6) | copy-start | bytes 3145732
  713.1 6.2 copy-start.39
  713.1 6.4 copy-start.33
  719.5 5.9 copy-start.32
  719.5 5.9 copy-start.55
  719.5 5.9 copy-start.67
  772.7 119.8 %copy-start.3 = (bf16[128,2048]{1,0:T(8,128)(2,1)S(1)}, bf16[128,2048]{1,0:T(8,128)(2,1)}, u32[]{:S(2)}) copy-start(bf16[128,2048]{1,0:T(8,128)(2,1)} %x_own.1) | copy-start | bytes 1572868
  772.7 119.8 %copy-start.72 = (f32[128]{0:T(128)S(1)}, f32[128]{0:T(128)}, u32[]{:S(2)}) copy-start(f32[128]{0:T(128)} %add_rsqrt_fusion.2) | copy-start | bytes 1540
  (50 other events, 115.9 us)
Sparse Core Ops, SparseCore 0:
  10.9 164.6 all-gather.1

commit v4 on v3

--- a/solution.py
+++ b/solution.py
@@ -37,6 +37,15 @@
         result = result + ((value // bit) % 2 + (other // bit) % 2) % 2 * bit
         bit *= 2
     return result
+
+
+def nearby(z, i, count):
+    both = jnp.minimum(z, count - 1 - z)
+    first = 1 - 2 * (z % 2)
+    paired = z + first * (1 - 2 * (i % 2)) * (i // 2 + 1)
+    side = jnp.where(2 * z < count, 1, -1)
+    single = z + side * (i - both + 1)
+    return jnp.where(i == count - 1, z, jnp.where(i < 2 * both, paired, single))
 
 
 class Place:
@@ -65,11 +74,11 @@
 
 def experts_kernel(
     n_dp, experts,
-    x_own, all_g, table, wg_hbm, wu_hbm, wd_hbm,
+    x_own, all_g, near_g, wg_hbm, wu_hbm, wd_hbm,
     out_sum, grad_sum, x_out, g_out, acts_out, all_x,
     sib_o, sib_g, one_o, one_g, two_o, two_g, z_o, z_g,
     wg, wu, wd, xs, gs, gate_rows, acts, xin, gin, stage_o, stage_g, acc_o, acc_g, tmp_o, tmp_g,
-    mine_o, mine_g,
+    leave_o, leave_g, pin, table,
     w_sem, in_sem, keep_sem, act_sem, own_sem, zx_send, zx_recv, ag_send, ag_recv,
     sib_send, sib_recv, one_send, one_recv, two_send, two_recv, z_send, z_recv, tmp_sem,
 ):
@@ -92,7 +101,7 @@
         )
 
     def layer_of(i):
-        return flip(here.layer, i, layers)
+        return nearby(here.layer, i, layers)
 
     def weights():
         return [
@@ -100,11 +109,63 @@
             for i, (s, d) in enumerate(((wg_hbm, wg), (wu_hbm, wu), (wd_hbm, wd)))
         ]
 
-    def z_copy(i):
-        me = here.layer * group + rank
+    def z_copy(block, up):
+        at = all_x.at[block * group + rank]
+        device = here.at_layer(here.layer + 1 if up else here.layer - 1)
+        return remote(at, at, zx_send.at[block], zx_recv.at[block], device)
+
+    def z_own(act):
+        @pl.when(here.layer + 1 < layers)
+        def _():
+            act(own_z(True))
+
+        @pl.when(here.layer >= 1)
+        def _():
+            act(own_z(False))
+
+    def own_z(up):
+        device = here.at_layer(here.layer + 1 if up else here.layer - 1)
         return remote(
-            x_own, all_x.at[me], zx_send.at[i], zx_recv.at[i], here.at_layer(layer_of(i))
-        )
+            x_own, all_x.at[here.layer * group + rank],
+            zx_send.at[here.layer if up else layers], zx_recv.at[here.layer], device,
+        )
+
+    def passes(i):
+        block = layer_of(i)
+        up = jnp.logical_and(block < here.layer, here.layer + 1 < layers)
+        down = jnp.logical_and(block > here.layer, here.layer >= 1)
+        return block, up, down
+
+    def z_pass(i):
+        block, up, down = passes(i)
+
+        @pl.when(up)
+        def _():
+            z_copy(block, True).wait_recv()
+            z_copy(block, True).start()
+
+        @pl.when(down)
+        def _():
+            z_copy(block, False).wait_recv()
+            z_copy(block, False).start()
+
+    def z_arrive(i):
+        block, up, down = passes(i)
+
+        @pl.when(jnp.logical_not(jnp.logical_or(up, down)))
+        def _():
+            z_copy(block, True).wait_recv()
+
+    def z_drain(i):
+        block, up, down = passes(i)
+
+        @pl.when(up)
+        def _():
+            z_copy(block, True).wait_send()
+
+        @pl.when(down)
+        def _():
+            z_copy(block, False).wait_send()
 
     def own_copy():
         return pltpu.make_async_copy(x_own, all_x.at[here.layer * group + rank], own_sem.at[0])
@@ -132,10 +193,14 @@
         return remote(ref, ref, ag_send.at[i, kind], ag_recv.at[i, kind], device)
 
     def gather_a(i):
-        if isinstance(i, int) and i == 0:
+        @pl.when(i < layers - 1)
+        def _():
+            z_arrive(i)
+
+        @pl.when(i == layers - 1)
+        def _():
             own_copy().wait()
-        else:
-            z_copy(i).wait_recv()
+
         for kind in (0, 3, 1, 2, 6):
             gather_copy(i, kind).start()
 
@@ -161,13 +226,13 @@
                    here.sibling),
         )
 
-    def one_copy(i, j):
-        return (
-            remote(acc_o.at[j * 2 + 1 - x], one_o.at[i, j], one_send.at[0, j],
-                   one_recv.at[0, i, j], here.over_x),
-            remote(acc_g.at[(1 - y) * 2 + j], one_g.at[i, j], one_send.at[1, j],
-                   one_recv.at[1, i, j], here.over_y),
-        )
+    def one_copy_o(i, j):
+        return remote(acc_o.at[j * 2 + 1 - x], one_o.at[i, j], one_send.at[0, j],
+                      one_recv.at[0, i, j], here.over_x)
+
+    def one_copy_g(i, j):
+        return remote(acc_g.at[(1 - y) * 2 + j], one_g.at[i, j], one_send.at[1, j],
+                      one_recv.at[1, i, j], here.over_y)
 
     def two_copy(i):
         return (
@@ -178,11 +243,10 @@
         )
 
     def out_copy(i):
-        device = here.at_layer(layer_of(i))
-        own = y * 2 + x
+        at, device = here.layer, here.at_layer(layer_of(i))
         return (
-            remote(acc_o.at[own], z_o.at[i], z_send.at[0], z_recv.at[0, i], device),
-            remote(acc_g.at[own], z_g.at[i], z_send.at[1], z_recv.at[1, i], device),
+            remote(leave_o, z_o.at[at], z_send.at[0], z_recv.at[0, at], device),
+            remote(leave_g, z_g.at[at], z_send.at[1], z_recv.at[1, at], device),
         )
 
     def fetch(src_o, src_g, slot):
@@ -203,76 +267,64 @@
         total = dst[q].astype(F32) + tmp[slot].astype(F32)
         dst[q] = total.astype(BF)
 
-    def sum_sibling(i):
-        def bring(q, slot):
-            for copy in sib_copy(i, q, 0):
-                copy.wait_recv()
-            start(fetch(sib_o.at[i, q], sib_g.at[i, q], slot))
-
-        bring(0, 0)
-        for q in range(4):
-            if q < 3:
-                bring(q + 1, (q + 1) % 2)
-            finish(fetch(sib_o.at[i, q], sib_g.at[i, q], q % 2))
-            add(acc_o, q, tmp_o, q % 2)
-            add(acc_g, q, tmp_g, q % 2)
-        for j in range(2):
-            start(one_copy(i, j))
-
     def sum_one(i):
-        def bring(j):
-            for copy in one_copy(i, j):
-                copy.wait_recv()
-            start(fetch(one_o.at[i, j], one_g.at[i, j], j))
-
-        bring(0)
-        bring(1)
-        for j in range(2):
-            finish(fetch(one_o.at[i, j], one_g.at[i, j], j))
-            add(acc_o, j * 2 + x, tmp_o, j)
-            add(acc_g, y * 2 + j, tmp_g, j)
+        o, g = one_copy_o(i, 1 - y), one_copy_g(i, 1 - x)
+        o.wait_recv()
+        g.wait_recv()
+        copies = fetch(one_o.at[i, 1 - y], one_g.at[i, 1 - x], 0)
+        start(copies)
+        finish(copies)
+        add(acc_o, (1 - y) * 2 + x, tmp_o, 0)
+        add(acc_g, y * 2 + 1 - x, tmp_g, 0)
         start(two_copy(i))
 
     def sum_two(i):
+        own = y * 2 + x
+        one_copy_o(i, y).wait_recv()
+        one_copy_g(i, x).wait_recv()
+        ones = fetch(one_o.at[i, y], one_g.at[i, x], 0)
+        start(ones)
         for copy in two_copy(i):
             copy.wait_recv()
-        start(fetch(two_o.at[i], two_g.at[i], 0))
-        finish(fetch(two_o.at[i], two_g.at[i], 0))
-        own = y * 2 + x
-        add(acc_o, own, tmp_o, 0)
-        add(acc_g, own, tmp_g, 0)
+        twos = fetch(two_o.at[i], two_g.at[i], 1)
+        start(twos)
+        finish(ones)
+        finish(twos)
+
+        @pl.when(i > 0)
+        def _():
+            for copy in out_copy(i - 1):
+                copy.wait_send()
+
+        for acc, tmp, leave in ((acc_o, tmp_o, leave_o), (acc_g, tmp_g, leave_g)):
+            total = acc[own].astype(F32) + tmp[0].astype(F32) + tmp[1].astype(F32)
+            leave[...] = total.astype(BF)
         for j in range(2):
-            for copy in one_copy(i, j):
-                copy.wait_send()
+            one_copy_o(i, j).wait_send()
+            one_copy_g(i, j).wait_send()
         for copy in two_copy(i):
             copy.wait_send()
 
-        @pl.when(i == 0)
-        def _():
-            mine_o[...] = acc_o[own]
-            mine_g[...] = acc_g[own]
-
-        @pl.when(i > 0)
+        @pl.when(i < layers - 1)
         def _():
             start(out_copy(i))
 
     start(weights())
     greet([here.over_x, here.over_y, here.sibling]
-          + [here.at_layer(layer_of(i)) for i in range(1, layers)])
+          + [here.at_layer(flip(here.layer, i, layers)) for i in range(1, layers)])
     own_copy().start()
-    for i in range(1, layers):
-        z_copy(i).start()
+    z_own(lambda copy: copy.start())
+    z_pass(0)
     gather_a(0)
+    z_pass(1)
     gather_b(0)
+    for i in range(2, layers - 1):
+        z_pass(i)
     gather_c(0)
     gather_a(1)
 
     def chunk(i, carry):
         base = layer_of(i) * group
-
-        @pl.when(i > 0)
-        def _():
-            sum_sibling(i - 1)
 
         gather_d(i)
 
@@ -280,22 +332,47 @@
             return (
                 pltpu.make_async_copy(all_x.at[base + b], xin.at[slot], in_sem.at[0, slot]),
                 pltpu.make_async_copy(
-                    all_g.at[base + b, :, pl.ds(0, width)], gin.at[slot], in_sem.at[1, slot]
+                    all_g.at[base + b, pl.ds(0, experts), pl.ds(width, rows)], pin.at[slot],
+                    in_sem.at[2, slot],
                 ),
             )
 
+        def load_g(b, slot, act):
+            @pl.when(i < layers - 1)
+            def _():
+                act(pltpu.make_async_copy(
+                    all_g.at[base + b, :, pl.ds(0, width)], gin.at[slot], in_sem.at[1, slot]
+                ))
+
+            @pl.when(i == layers - 1)
+            def _():
+                act(pltpu.make_async_copy(near_g.at[b], gin.at[slot], in_sem.at[1, slot]))
+
+        def begin_load(b, slot):
+            start(load(b, slot))
+            load_g(b, slot, lambda copy: copy.start())
+
         for b in range(slots - 1):
-            start(load(b, b))
+            begin_load(b, b)
 
         def bring(b, c):
             slot = lax.rem(b, slots)
             finish(load(b, slot))
+            load_g(b, slot, lambda copy: copy.wait())
 
             @pl.when(b + slots - 1 < group)
             def _():
-                start(load(b + slots - 1, lax.rem(b + slots - 1, slots)))
-
-            hot = table[base + b]
+                begin_load(b + slots - 1, lax.rem(b + slots - 1, slots))
+
+            size = local * cap
+            chooses = (
+                lax.broadcasted_iota(jnp.int32, (size, experts), 1)
+                == lax.broadcasted_iota(jnp.int32, (size, experts), 0) // cap + first
+            )
+            places = dot(jnp.where(chooses, 1.0, 0.0).astype(BF), pin[slot])
+            seat = lax.broadcasted_iota(jnp.int32, (size, rows), 0) % cap
+            hot = jnp.where(places == seat.astype(F32), 1.0, 0.0).astype(BF)
+            table[b] = hot
             for src, dst in ((xin, xs), (gin, gs)):
                 for n in range(0, width, STEP):
                     got = dot(hot, src[slot, :, n : n + STEP]).astype(BF)
@@ -332,11 +409,10 @@
                 def _():
                     action()
 
-            hook(1, i + 2 < layers, lambda: gather_a(i + 2))
-            hook(2, i + 1 < layers, lambda: gather_b(i + 1))
-            hook(4, i + 1 < layers, lambda: gather_c(i + 1))
-            hook(5, i > 0, lambda: sum_one(i - 1))
-            hook(7, i > 0, lambda: sum_two(i - 1))
+            hook(6, i + 2 < layers, lambda: gather_a(i + 2))
+            hook(4, i + 1 < layers, lambda: gather_b(i + 1))
+            hook(7, i + 1 < layers, lambda: gather_c(i + 1))
+            hook(4, i > 0, lambda: sum_one(i - 1))
             slot = lax.rem(e, 2)
 
             @pl.when(jnp.logical_or(i > 0, e >= 2))
@@ -374,28 +450,33 @@
         lax.fori_loop(0, local, expert, 0)
 
         def combine(b, put_o, put_g):
-            hot = table[base + b]
+            hot = table[b]
             for n in range(0, width, STEP):
                 got = gs[:, b, :, n : n + STEP].reshape(local * cap, STEP)
-                put_o(n, STEP, tdot(hot, got).astype(BF))
+                put_o(n, STEP, tdot(hot, got))
                 got = xs[:, b, :, n : n + STEP].reshape(local * cap, STEP)
-                put_g(n, STEP, tdot(hot, got).astype(BF))
+                put_g(n, STEP, tdot(hot, got))
             got = gate_rows[:, b].reshape(local * cap, 128).astype(BF)
-            put_g(width, 128, tdot(hot, got).astype(BF))
-
-        def give(q, c):
-            slot = lax.rem(q, 2)
-
-            @pl.when(jnp.logical_or(i > 0, q >= 2))
+            put_g(width, 128, tdot(hot, got))
+
+        def square(k):
+            return (y + 1 - k % 2) % 2, (x + 1 - k // 2) % 2
+
+        def give(k, c):
+            slot = lax.rem(k, 2)
+            to_y, to_x = square(k)
+            q = to_y * 2 + to_x
+
+            @pl.when(jnp.logical_or(i > 0, k >= 2))
             def _():
                 for copy in sib_copy(i, q, slot):
                     copy.wait_send()
 
             def put_o(n, size, value):
-                stage_o[slot, :, pl.ds(n, size)] = value
+                stage_o[slot, :, pl.ds(n, size)] = value.astype(BF)
 
             def put_g(n, size, value):
-                stage_g[slot, :, pl.ds(n, size)] = value
+                stage_g[slot, :, pl.ds(n, size)] = value.astype(BF)
 
             combine(q * 2 + 1 - core, put_o, put_g)
             start(sib_copy(i, q, slot))
@@ -403,19 +484,52 @@
 
         lax.fori_loop(0, 4, give, 0)
 
-        @pl.when(i > 1)
-        def _():
-            for copy in out_copy(i - 1):
-                copy.wait_send()
-
-        def hold(q, c):
+        def from_sibling(k):
+            to_y, to_x = square(k)
+            q = to_y * 2 + to_x
+            return fetch(sib_o.at[i, q], sib_g.at[i, q], lax.rem(k, 2))
+
+        def bring_sibling(k):
+            to_y, to_x = square(k)
+            for copy in sib_copy(i, to_y * 2 + to_x, 0):
+                copy.wait_recv()
+            start(from_sibling(k))
+
+        @pl.when(i > 0)
+        def _():
+            sum_two(i - 1)
+
+        bring_sibling(0)
+
+        def hold(k, c):
+            slot = lax.rem(k, 2)
+            to_y, to_x = square(k)
+            q = to_y * 2 + to_x
+
+            @pl.when(k < 3)
+            def _():
+                bring_sibling(k + 1)
+
+            finish(from_sibling(k))
+
             def put_o(n, size, value):
-                acc_o[q, :, pl.ds(n, size)] = value
+                cols = pl.ds(n, size)
+                acc_o[q, :, cols] = (value + tmp_o[slot, :, cols].astype(F32)).astype(BF)
 
             def put_g(n, size, value):
-                acc_g[q, :, pl.ds(n, size)] = value
+                cols = pl.ds(n, size)
+                acc_g[q, :, cols] = (value + tmp_g[slot, :, cols].astype(F32)).astype(BF)
 
             combine(q * 2 + core, put_o, put_g)
+
+            @pl.when(k < 2)
+            def _():
+                one_copy_o(i, to_y).start()
+
+            @pl.when(k % 2 == 0)
+            def _():
+                one_copy_g(i, to_x).start()
+
             return c
 
         lax.fori_loop(0, 4, hold, 0)
@@ -423,24 +537,27 @@
 
     lax.fori_loop(0, layers, chunk, 0)
     last = layers - 1
-    sum_sibling(last)
     sum_one(last)
     sum_two(last)
-    out_sum[...] = mine_o[...].astype(F32)
-    grad_sum[...] = mine_g[...].astype(F32)
-
-    def last_sum(i, c):
-        for copy in out_copy(i):
+    out_sum[...] = leave_o[...].astype(F32)
+    grad_sum[...] = leave_g[...].astype(F32)
+
+    def arrive(i):
+        at = layer_of(i)
+        for copy in (
+            remote(leave_o, z_o.at[at], z_send.at[0], z_recv.at[0, at], here.sibling),
+            remote(leave_g, z_g.at[at], z_send.at[1], z_recv.at[1, at], here.sibling),
+        ):
             copy.wait_recv()
-        start(fetch(z_o.at[i], z_g.at[i], 0))
-        finish(fetch(z_o.at[i], z_g.at[i], 0))
-        out_sum[...] += tmp_o[0].astype(F32)
-        grad_sum[...] += tmp_g[0].astype(F32)
-        return c
-
-    lax.fori_loop(1, layers, last_sum, 0)
-    for copy in out_copy(last):
-        copy.wait_send()
+        start(fetch(z_o.at[at], z_g.at[at], i % 2))
+
+    arrive(0)
+    for i in range(last):
+        if i + 1 < last:
+            arrive(i + 1)
+        finish(fetch(z_o.at[layer_of(i)], z_g.at[layer_of(i)], i % 2))
+        out_sum[...] += tmp_o[i % 2].astype(F32)
+        grad_sum[...] += tmp_g[i % 2].astype(F32)
     for slot in range(2):
         for copy in sib_copy(last, slot, slot):
             copy.wait_send()
@@ -454,10 +571,12 @@
         return c
 
     lax.fori_loop(0, layers, drain, 0)
-    lax.fori_loop(1, layers, lambda i, c: (z_copy(i).wait_send(), c)[1], 0)
-
-
-def run_experts(x_own, all_g, table, wg, wu, wd, n_dp, experts, cap):
+    z_own(lambda copy: copy.wait_send())
+    for i in range(last):
+        z_drain(i)
+
+
+def run_experts(x_own, all_g, near_g, wg, wu, wd, n_dp, experts, cap):
     rows, wide = x_own.shape
     n_dev = all_g.shape[0]
     local, width, hid = wg.shape
@@ -482,7 +601,7 @@
             shape((layers, rows, width), BF), shape((layers, rows, wide_g), BF),
             shape((layers, rows, width), BF), shape((layers, rows, wide_g), BF),
         ),
-        in_specs=[ANY, ANY, VMEM, ANY, ANY, ANY],
+        in_specs=[ANY] * 6,
         out_specs=(VMEM, VMEM) + (ANY,) * 12,
         scratch_shapes=[
             pltpu.VMEM(wg.shape, BF), pltpu.VMEM(wu.shape, BF), pltpu.VMEM(wd.shape, BF),
@@ -496,8 +615,9 @@
             pltpu.VMEM((4, rows, width), BF), pltpu.VMEM((4, rows, wide_g), BF),
             pltpu.VMEM((2, rows, width), BF), pltpu.VMEM((2, rows, wide_g), BF),
             pltpu.VMEM((rows, width), BF), pltpu.VMEM((rows, wide_g), BF),
-            dma((3,)), dma((2, slots)), dma((2, local)), dma((2,)), dma((1,)),
-            dma((layers,)), dma((layers,)), dma((layers, 10)), dma((layers, 10)),
+            pltpu.VMEM((slots, experts, rows), BF), pltpu.VMEM((group, local * cap, rows), BF),
+            dma((3,)), dma((3, slots)), dma((2, local)), dma((2,)), dma((1,)),
+            dma((layers + 1,)), dma((layers,)), dma((layers, 10)), dma((layers, 10)),
             dma((2, 2)), dma((2, layers, 4)), dma((2, 2)), dma((2, layers, 2)),
             dma((2,)), dma((2, layers)), dma((2,)), dma((2, layers)), dma((2, 2)),
         ],
@@ -505,7 +625,7 @@
             collective_id=1, has_side_effects=True, vmem_limit_bytes=64 * 2**20
         ),
         cost_estimate=pl.CostEstimate(flops=flops, bytes_accessed=200 * 2**20, transcendentals=0),
-    )(x_own, all_g, table, wg, wu, wd)
+    )(x_own, all_g, near_g, wg, wu, wd)
     return result[:5]
 
 
@@ -630,6 +750,111 @@
         self.keep().wait()
 
 
+class WideGather:
+    def __init__(self, here, layers, own, buf, own_sem, z_send, z_recv, send, recv):
+        self.here, self.layers, self.own, self.buf = here, layers, own, buf
+        self.own_sem, self.z_send, self.z_recv = own_sem, z_send, z_recv
+        self.send, self.recv = send, recv
+        self.last = layers - 1
+
+    def layer_of(self, i):
+        return nearby(self.here.layer, i, self.layers)
+
+    def keep(self):
+        return pltpu.make_async_copy(
+            self.own, self.buf.at[self.here.layer, self.here.rank], self.own_sem.at[0]
+        )
+
+    def over_z(self, block, up, own=False):
+        here = self.here
+        at = self.buf.at[block, here.rank]
+        return remote(
+            self.own if own else at, at,
+            self.z_send.at[self.layers if own and not up else block], self.z_recv.at[block],
+            here.at_layer(here.layer + 1 if up else here.layer - 1),
+        )
+
+    def own_z(self, act):
+        layer = self.here.layer
+
+        @pl.when(layer + 1 < self.layers)
+        def _():
+            act(self.over_z(layer, True, True))
+
+        @pl.when(layer >= 1)
+        def _():
+            act(self.over_z(layer, False, True))
+
+    def passes(self, i):
+        layer, block = self.here.layer, self.layer_of(i)
+        up = jnp.logical_and(block < layer, layer + 1 < self.layers)
+        down = jnp.logical_and(block > layer, layer >= 1)
+        return block, up, down
+
+    def pass_on(self, i):
+        block, up, down = self.passes(i)
+
+        @pl.when(up)
+        def _():
+            self.over_z(block, True).wait_recv()
+            self.over_z(block, True).start()
+
+        @pl.when(down)
+        def _():
+            self.over_z(block, False).wait_recv()
+            self.over_z(block, False).start()
+
+    def copy(self, i, kind):
+        here = self.here
+        block = self.buf.at[self.layer_of(i)]
+        job = LayerGather(here, block.at[here.rank], block, None, self.send.at[i], self.recv.at[i])
+        return job.copy(kind)
+
+    def begin(self):
+        self.keep().start()
+        self.own_z(lambda copy: copy.start())
+
+    def enter(self, i):
+        block, up, down = self.passes(i)
+
+        @pl.when(jnp.logical_not(jnp.logical_or(up, down)))
+        def _():
+            self.over_z(block, True).wait_recv()
+
+        for kind in (0, 3, 1, 2, 6):
+            self.copy(i, kind).start()
+
+    def forward(self, i):
+        for got, then in ((0, 4), (3, 5), (1, 7), (2, 8)):
+            self.copy(i, got).wait_recv()
+            self.copy(i, then).start()
+
+    def across(self, i):
+        self.copy(i, 4).wait_recv()
+        self.copy(i, 5).wait_recv()
+        self.copy(i, 9).start()
+
+    def end(self):
+        self.keep().wait()
+        for i in range(self.last):
+            for kind in (6, 7, 8, 9):
+                self.copy(i, kind).wait_recv()
+        for i in range(self.last):
+            for kind in range(10):
+                self.copy(i, kind).wait_send()
+        self.own_z(lambda copy: copy.wait_send())
+        for i in range(self.last):
+            block, up, down = self.passes(i)
+
+            @pl.when(up)
+            def _():
+                self.over_z(block, True).wait_send()
+
+            @pl.when(down)
+            def _():
+                self.over_z(block, False).wait_send()
+
+
 class LayerSum:
     def __init__(self, here, part, acc, sib, one, two, load, send, recv):
         self.here, self.part, self.acc, self.sib = here, part, acc, sib
@@ -716,51 +941,6 @@
     )
 
 
-def gather_kernel(n_dp, own, buf, own_sem, send, recv):
-    here = Place(n_dp)
-    greet([here.over_x, here.over_y, here.sibling])
-    job = LayerGather(here, own, buf, own_sem, send, recv)
-    job.begin()
-    job.forward()
-    job.across()
-    job.end()
-
-
-def layer_gather(value, n_dp):
-    rows, wide = value.shape
-    dma = pltpu.SemaphoreType.DMA
-    return pl.pallas_call(
-        functools.partial(gather_kernel, n_dp),
-        out_shape=jax.ShapeDtypeStruct((2 * n_dp, rows, wide), value.dtype),
-        in_specs=[ANY],
-        out_specs=ANY,
-        scratch_shapes=[dma((1,)), dma((10,)), dma((10,))],
-        compiler_params=comm_params(2),
-    )(value)
-
-
-def sum_kernel(n_dp, part, out, *scratch):
-    here = Place(n_dp)
-    greet([here.over_x, here.over_y, here.sibling])
-    job = LayerSum(here, part, *scratch)
-    job.begin()
-    job.first()
-    job.second()
-    job.third(out)
-
-
-def layer_sum(part, n_dp):
-    group, rows, wide = part.shape
-    return pl.pallas_call(
-        functools.partial(sum_kernel, n_dp),
-        out_shape=jax.ShapeDtypeStruct((rows, wide), F32),
-        in_specs=[ANY],
-        out_specs=VMEM,
-        scratch_shapes=LayerSum.scratch(rows, wide),
-        compiler_params=comm_params(3),
-    )(part)
-
-
 def stats_kernel(n_dp, value, out, land, send, recv):
     here = Place(n_dp)
     group = 2 * n_dp
@@ -799,10 +979,10 @@
 
 
 def front_kernel(
-    n_dp, layers, x_own, w_q, w_k, w_v, w_o, small,
-    x_all, qkv, wo, small_all, wo_col,
+    n_dp, layers, x_own, w_q, w_k, w_v, w_o, small, g_own,
+    x_all, qkv, wo, small_all, g_near, wo_col,
     own_sem, x_send, x_recv, a_keep, a_send, a_recv, up_send, up_recv, down_send, down_recv,
-    o_keep, o_send, o_recv, s_send, s_recv, t_send, t_recv,
+    o_keep, o_send, o_recv, s_send, s_recv, t_send, t_recv, g_keep, g_send, g_recv,
 ):
     here = Place(n_dp)
     group = 2 * n_dp
@@ -813,6 +993,7 @@
     away = [flip(layer, i, layers) for i in range(1, layers)]
     greet([peer(here, r) for r in ranks] + [here.at_layer(z) for z in away])
     gather = LayerGather(here, x_own, x_all, own_sem, x_send, x_recv)
+    cotangent = LayerGather(here, g_own, g_near, g_keep, g_send, g_recv)
     weights = (w_q, w_k, w_v)
 
     def rows_at(index):
@@ -893,13 +1074,18 @@
         small_out(i).wait_recv()
     for k in range(group - 1):
         small_share(k).start()
+    cotangent.begin()
     for s in range(layers - 1):
         step(0, s, True)
         if s + 1 < layers - 1:
             step(0, s + 1, False)
+        if s == 0:
+            cotangent.forward()
         step(1, s, True)
         if s + 1 < layers - 1:
             step(1, s + 1, False)
+        if s == 0:
+            cotangent.across()
 
     def share(z):
         number = z * group + rank
@@ -942,6 +1128,7 @@
             pltpu.make_async_copy(wo_col.at[0], wo.at[index], o_keep.at[index]).wait()
 
     gather.end()
+    cotangent.end()
     for k in range(group - 1):
         small_share(k).wait_recv()
     for w in range(3):
@@ -969,7 +1156,7 @@
                 chain(which, False, s).wait_send()
 
 
-def run_front(x_own, w_q, w_k, w_v, w_o, small, n_dp, n_dev):
+def run_front(x_own, w_q, w_k, w_v, w_o, small, g_own, n_dp, n_dev):
     rows, width = x_own.shape
     own = w_q.shape[0]
     group = 2 * n_dp
@@ -985,22 +1172,26 @@
             shape((3, layers, group * own, cols), BF),
             shape((layers, own, width), BF),
             shape((layers, group) + small.shape, BF),
+            shape((group, rows, width), BF),
             shape((layers, own, width), BF),
         ),
-        in_specs=[ANY] * 6,
-        out_specs=(ANY,) * 5,
+        in_specs=[ANY] * 7,
+        out_specs=(ANY,) * 6,
         scratch_shapes=[
             dma((1,)), dma((10,)), dma((10,)), dma((5,)),
             dma((3, group - 1)), dma((3, group - 1)), chain, chain, chain, chain,
             dma((layers,)), dma((layers,)), dma((layers,)),
             dma((layers,)), dma((layers,)), dma((group,)), dma((group,)),
+            dma((1,)), dma((10,)), dma((10,)),
         ],
-        compiler_params=comm_params(5),
-    )(x_own, w_q, w_k, w_v, w_o, small)
-    x_all, qkv, wo, small_all, _ = result
+        compiler_params=pltpu.CompilerParams(
+            collective_id=5, has_side_effects=True, vmem_limit_bytes=64 * 2**20
+        ),
+    )(x_own, w_q, w_k, w_v, w_o, small, g_own)
+    x_all, qkv, wo, small_all, g_near, _ = result
     return (
         x_all.reshape(group * rows, width), qkv.reshape(3, width, cols),
-        wo.reshape(cols, width), small_all.reshape(width, -1),
+        wo.reshape(cols, width), small_all.reshape(width, -1), g_near,
     )
 
 
@@ -1228,28 +1419,341 @@
     )
 
 
+class LayerTerms:
+    def __init__(self, here, ranks, pick, land, send, recv):
+        self.here, self.ranks, self.pick = here, ranks, pick
+        self.land, self.send, self.recv = land, send, recv
+
+    def copy(self, k):
+        return remote(
+            self.pick(self.ranks[k]), self.land.at[k], self.send.at[k], self.recv.at[k],
+            peer(self.here, self.ranks[k]),
+        )
+
+    def begin(self):
+        for k in range(len(self.ranks)):
+            self.copy(k).start()
+
+    def total(self, own):
+        for k in range(len(self.ranks)):
+            self.copy(k).wait_recv()
+            own = own + self.land[k].astype(F32)
+        return own
+
+    def end(self):
+        for k in range(len(self.ranks)):
+            self.copy(k).wait_send()
+
+
+def as_row(column):
+    return jnp.broadcast_to(column, (column.shape[0], 128)).T[:1]
+
+
+def as_column(row):
+    return jnp.broadcast_to(row, (128, row.shape[1])).T[:, :1]
+
+
+def row_sum(value):
+    return jnp.sum(value, axis=1, keepdims=True)
+
+
+def swap_halves(value):
+    half = value.shape[1] // 2
+    return jnp.concatenate([value[:, half:], value[:, :half]], axis=1)
+
+
+def probabilities(q_rot, k_rot, scale):
+    scores = dot_t(q_rot, k_rot) * scale
+    later = (
+        lax.broadcasted_iota(jnp.int32, scores.shape, 0)
+        >= lax.broadcasted_iota(jnp.int32, scores.shape, 1)
+    )
+    scores = jnp.where(later, scores, -1e30)
+    grown = jnp.exp(scores - jnp.max(scores, axis=1, keepdims=True))
+    return grown / row_sum(grown)
+
+
+def attend_kernel(
+    n_dp, layers, seqs,
+    x, gain, w, q_gain, k_gain, cosine, sine, wo, ffn_gain, router, hits, g_own,
+    normed, q_raw, k_raw, v, q_rot, k_rot, mixed, stats,
+    residual, res_unit, res_root, gates, x_out, g_all,
+    part, squares, land, n_send, n_recv, out, p_send, p_recv,
+    acc, sib, one, two, load_sem, l_send, l_recv, g_keep, gz_send, gz_recv, g_send, g_recv,
+):
+    here = Place(n_dp)
+    group = 2 * n_dp
+    ranks = others(here, group)
+    greet(
+        [peer(here, r) for r in ranks]
+        + [here.at_layer(flip(here.layer, i, layers)) for i in range(1, layers)]
+    )
+    terms = LayerTerms(here, ranks, lambda r: squares, land, n_send, n_recv)
+    rest = WideGather(here, layers, g_own, g_all, g_keep, gz_send, gz_recv, g_send, g_recv)
+    job = LayerSum(here, part, acc, sib, one, two, load_sem, l_send, l_recv)
+    last = layers - 1
+    total, width = normed.shape
+    rows_own = g_own.shape[0]
+    cols = q_raw.shape[1]
+    def seats(k):
+        ref = g_all.at[here.layer, here.rank, :, pl.ds(width, g_own.shape[1] - width)]
+        src = g_own.at[:, pl.ds(width, g_own.shape[1] - width)]
+        return remote(src, ref, p_send.at[k], p_recv.at[k], peer(here, ranks[k]))
+
+    rest.begin()
+    for k in range(group - 1):
+        seats(k).start()
+
+    tile = 256
+    squares[...] = jnp.zeros_like(squares)
+
+    def project(t):
+        at = slice(t * tile, (t + 1) * tile)
+        value = x[at, :].astype(F32)
+        root = lax.rsqrt(row_sum(value * value) / width + EPSILON)
+        low = (value * root * gain[...]).astype(BF)
+        normed[at, :] = low
+        q, k = dot(low, w[0]), dot(low, w[1])
+        q_raw[at, :] = q
+        k_raw[at, :] = k
+        v[at, :] = dot(low, w[2]).astype(BF)
+        squares[0:1, at] = as_row(row_sum(q * q))
+        squares[1:2, at] = as_row(row_sum(k * k))
+
+    for t in range(total // tile):
+        project(t)
+    terms.begin()
+    rest.pass_on(0)
+    rest.enter(0)
+    stats[...] = terms.total(squares[...])
+
+    length = total // seqs
+    for s in range(seqs):
+        rows = slice(s * length, (s + 1) * length)
+        roots = [
+            as_column(lax.rsqrt(stats[i : i + 1, rows] / width + EPSILON)) for i in range(2)
+        ]
+        for h in range(0, cols, HEAD_DIM):
+            head = slice(h, h + HEAD_DIM)
+            turned = []
+            for raw, root, scale, to in (
+                (q_raw, roots[0], q_gain, q_rot), (k_raw, roots[1], k_gain, k_rot),
+            ):
+                value = raw[rows, head] * root * scale[:, head]
+                value = (value * cosine[...] + swap_halves(value) * sine[...]).astype(BF)
+                to[rows, head] = value
+                turned.append(value)
+            probs = probabilities(turned[0], turned[1], HEAD_DIM ** (-0.5)).astype(BF)
+            mixed[rows, head] = dot(probs, v[rows, head]).astype(BF)
+        if s == 0:
+            rest.pass_on(1)
+    size = part.shape[1]
+    rest.forward(0)
+    rest.enter(1)
+
+    def project_out(b, c):
+        value = mixed[pl.ds(pl.multiple_of(b * size, size), size), :]
+        for n in range(0, width, STEP):
+            part[b, :, n : n + STEP] = dot(value, wo[:, n : n + STEP]).astype(BF)
+        return c
+
+    lax.fori_loop(0, group, project_out, 0)
+
+    job.begin()
+    rest.across(0)
+    for i in range(2, last):
+        rest.pass_on(i)
+    job.first()
+    rest.forward(1)
+    job.second()
+    if last > 2:
+        rest.enter(2)
+    rest.across(1)
+    job.third(out)
+
+    at = pl.ds(pl.multiple_of(here.rank * rows_own, rows_own), rows_own)
+    value = x[at, :].astype(F32) + out[...]
+    residual[...] = value
+    root = lax.rsqrt(row_sum(value * value) / width + EPSILON)
+    unit = value * root
+    res_unit[...] = unit
+    res_root[...] = jnp.broadcast_to(root, res_root.shape)
+    low = (unit * ffn_gain[...]).astype(BF)
+    x_out[:, :width] = low
+    logits = dot(low, router[...])
+    chosen = hits[...] > 0.0
+    top_logit = jnp.max(jnp.where(chosen, logits, -1e30), axis=1, keepdims=True)
+    grown = jnp.where(chosen, jnp.exp(jnp.minimum(logits - top_logit, 0.0)), 0.0)
+    shares = grown / row_sum(grown)
+    gates[...] = shares
+    high = shares.astype(BF).astype(F32)
+    x_out[:, width:] = (high + swap_halves(shares - high)).astype(BF)
+    for i in range(2, last):
+        rest.forward(i)
+        if i + 1 < last:
+            rest.enter(i + 1)
+        rest.across(i)
+    rest.end()
+    terms.end()
+    for k in range(group - 1):
+        seats(k).wait()
+
+
+def run_attend(seqs, n_dp, layers, x, gain, w, *rest):
+    g_own = rest[-1]
+    total, width = x.shape
+    cols = w.shape[-1]
+    group = 2 * n_dp
+    rows = total // group
+    shape = jax.ShapeDtypeStruct
+    dma = pltpu.SemaphoreType.DMA
+    narrow, narrow_f = shape((total, cols), BF), shape((total, cols), F32)
+    result = pl.pallas_call(
+        functools.partial(attend_kernel, n_dp, layers, seqs),
+        out_shape=(
+            shape((total, width), BF), narrow_f, narrow_f, narrow, narrow, narrow, narrow,
+            shape((8, total), F32), shape((rows, width), F32), shape((rows, width), F32),
+            shape((rows, 128), F32), shape((rows, 128), F32), shape((rows, width + 128), BF),
+            shape((layers, group) + g_own.shape, BF),
+        ),
+        in_specs=[VMEM] * 11 + [ANY],
+        out_specs=(VMEM,) * 13 + (ANY,),
+        scratch_shapes=[
+            pltpu.VMEM((group, rows, width), BF), pltpu.VMEM((8, total), F32),
+            pltpu.VMEM((group - 1, 8, total), F32), dma((group - 1,)), dma((group - 1,)),
+            pltpu.VMEM((rows, width), F32), dma((group - 1,)), dma((group - 1,)),
+        ] + LayerSum.scratch(rows, width) + [
+            dma((1,)), dma((layers + 1,)), dma((layers,)), dma((layers, 10)), dma((layers, 10)),
+        ],
+        compiler_params=pltpu.CompilerParams(
+            collective_id=2, has_side_effects=True, vmem_limit_bytes=56 * 2**20
+        ),
+    )(x, gain, w, *rest)
+    return result
+
+
+def attend_back_kernel(
+    seqs, gao, wo, mixed, q_rot, k_rot, v, q_raw, k_raw, stats, q_gain, k_gain, cosine, sine,
+    grad_wo, gq, gk, gv, gains, inner, grad_mixed,
+):
+    total, cols = q_raw.shape
+    width = wo.shape[1]
+    length = total // seqs
+    scale = HEAD_DIM ** (-0.5)
+    for n in range(0, width, STEP):
+        grad_wo[:, n : n + STEP] = tdot(mixed[...], gao[:, n : n + STEP]).astype(BF)
+    grad_mixed[...] = dot_t(gao[...], wo[...]).astype(BF)
+    inner[...] = jnp.zeros_like(inner)
+    gains[...] = jnp.zeros_like(gains)
+    for s in range(seqs):
+        rows = slice(s * length, (s + 1) * length)
+        roots = [
+            as_column(lax.rsqrt(stats[i : i + 1, rows] / width + EPSILON)) for i in range(2)
+        ]
+        inners = [jnp.zeros((length, 1), F32) for _ in range(2)]
+        for h in range(0, cols, HEAD_DIM):
+            head = slice(h, h + HEAD_DIM)
+            q, k = q_rot[rows, head], k_rot[rows, head]
+            probs = probabilities(q, k, scale)
+            gm = grad_mixed[rows, head]
+            gv[rows, head] = tdot(probs.astype(BF), gm).astype(BF)
+            grad_probs = dot_t(gm, v[rows, head])
+            delta = row_sum(probs * grad_probs)
+            grad_scores = (probs * (grad_probs - delta)).astype(BF)
+            for i, (turned, raw, gain, out) in enumerate((
+                (dot(grad_scores, k) * scale, q_raw, q_gain, gq),
+                (tdot(grad_scores, q) * scale, k_raw, k_gain, gk),
+            )):
+                back = turned * cosine[...] - swap_halves(turned) * sine[...]
+                unit = raw[rows, head] * roots[i]
+                gains[i : i + 1, head] += jnp.sum(back * unit, axis=0, keepdims=True)
+                back = back * gain[:, head]
+                out[rows, head] = back
+                inners[i] = inners[i] + row_sum(back * unit)
+        for i in range(2):
+            inner[i : i + 1, rows] = as_row(inners[i])
+
+
+def run_attend_back(seqs, gao, wo, mixed, q_rot, k_rot, v, q_raw, k_raw, stats, *rest):
+    total, cols = q_raw.shape
+    width = wo.shape[1]
+    shape = jax.ShapeDtypeStruct
+    return pl.pallas_call(
+        functools.partial(attend_back_kernel, seqs),
+        out_shape=(
+            shape((cols, width), BF), shape((total, cols), F32), shape((total, cols), F32),
+            shape((total, cols), BF), shape((8, cols), F32), shape((8, total), F32),
+        ),
+        in_specs=[VMEM] * 13,
+        out_specs=(VMEM,) * 6,
+        scratch_shapes=[pltpu.VMEM((total, cols), BF)],
+        compiler_params=pltpu.CompilerParams(vmem_limit_bytes=48 * 2**20),
+    )(gao, wo, mixed, q_rot, k_rot, v, q_raw, k_raw, stats, *rest)
+
+
+def project_back_kernel(
+    gq, gk, gv, q_raw, k_raw, stats, inner, w, normed, x, part, grad_w, gain, low,
+):
+    total, cols = gq.shape
+    group, rows, width = part.shape
+    for i, (grad, raw) in enumerate(((gq, q_raw), (gk, k_raw))):
+        root = as_column(lax.rsqrt(stats[i : i + 1, :] / width + EPSILON))
+        mean = as_column(inner[i : i + 1, :] / width)
+        low[i] = (root * (grad[...] - raw[...] * root * mean)).astype(BF)
+    low[2] = gv[...]
+    gain[...] = jnp.zeros_like(gain)
+
+    def block(b, c):
+        at = pl.ds(pl.multiple_of(b * rows, rows), rows)
+        value = x[at, :].astype(F32)
+        root = lax.rsqrt(row_sum(value * value) / width + EPSILON)
+        for n in range(0, width, STEP):
+            cut = slice(n, n + STEP)
+            total = dot_t(low[0, at, :], w[0, cut, :]) + dot_t(low[1, at, :], w[1, cut, :])
+            total = total + dot_t(low[2, at, :], w[2, cut, :])
+            part[b, :, cut] = total.astype(BF)
+            unit = x[at, cut].astype(F32) * root
+            gain[0:1, cut] += jnp.sum(total * unit, axis=0, keepdims=True)
+        return c
+
+    lax.fori_loop(0, group, block, 0)
+    for n in range(0, width, STEP):
+        cut = slice(n, n + STEP)
+        rows_t = normed[:, cut]
+        for i in range(3):
+            grad_w[i, cut, :] = tdot(rows_t, low[i]).astype(BF)
+
+
+def run_project_back(group, gq, gk, gv, q_raw, k_raw, stats, inner, w, normed, x):
+    total, cols = gq.shape
+    width = x.shape[1]
+    shape = jax.ShapeDtypeStruct
+    return pl.pallas_call(
+        project_back_kernel,
+        out_shape=(
+            shape((group, total // group, width), BF), shape((3, width, cols), BF),
+            shape((8, width), F32),
+        ),
+        in_specs=[VMEM] * 10,
+        out_specs=(VMEM,) * 3,
+        scratch_shapes=[pltpu.VMEM((3, total, cols), BF)],
+        compiler_params=pltpu.CompilerParams(vmem_limit_bytes=56 * 2**20),
+    )(gq, gk, gv, q_raw, k_raw, stats, inner, w, normed, x)
+
+
 def ein(spec, left, right):
     return jnp.einsum(spec, left, right, preferred_element_type=F32)
 
 
 def inv_rms(value):
     return lax.rsqrt(jnp.mean(value * value, axis=-1, keepdims=True) + EPSILON)
-
-
-def half_turn(value):
-    half = value.shape[-1] // 2
-    return jnp.concatenate([-value[..., half:], value[..., :half]], axis=-1)
-
-
-def half_turn_back(value):
-    half = value.shape[-1] // 2
-    return jnp.concatenate([value[..., half:], -value[..., :half]], axis=-1)
 
 
 def build(n_ep, n_dp):
     n_dev = n_ep * n_dp
     group = 2 * n_dp
     layers = n_dev // group
+    rows_of = [[z * group + r for r in range(group)] for z in range(layers)]
 
     def shards(
         layer_input, grad_out, attn_gain, w_q, w_k, w_v, q_gain, k_gain, w_o, ffn_gain,
@@ -1257,93 +1761,53 @@
     ):
         rows, width = layer_input.shape
         cols = width // group
-        heads = cols // HEAD_DIM
         seqs = 2
         seq_len = rows * n_dp
-        scale = HEAD_DIM ** (-0.5)
         own = width // n_dev
         rank = (lax.axis_index("ep") % 2) * n_dp + lax.axis_index("dp")
-        local_experts = w_gate.shape[0]
         experts = router.shape[1]
         top = routes.shape[1]
         cap = 2 * rows * top // experts
 
-        gains = jnp.stack([attn_gain, q_gain, k_gain, ffn_gain], axis=1)
+        gains = jnp.stack([attn_gain, q_gain, k_gain, ffn_gain]).T
         small = jnp.concatenate(
             [router, gains, jnp.zeros((own, 128 - experts - 4), BF)], axis=1
         )
-        group_input, qkv, wo, small = run_front(
-            layer_input, w_q, w_k, w_v, w_o, small, n_dp, n_dev
-        )
-        wq, wk, wv = qkv[0], qkv[1], qkv[2]
+        group_input, qkv, wo, small, near_g = run_front(
+            layer_input, w_q, w_k, w_v, w_o, small, grad_out, n_dp, n_dev
+        )
         full_router = small[:, :experts]
         full_attn_gain = small[:, experts].astype(F32)
         full_ffn_gain = small[:, experts + 3].astype(F32)
         head_gains = lax.dynamic_slice_in_dim(small, rank * cols, cols, 0).astype(F32)
         q_gain_own, k_gain_own = head_gains[:, experts + 1], head_gains[:, experts + 2]
 
-        group_input = group_input.astype(F32)
-        group_root = inv_rms(group_input)
-        normed = (group_input * group_root * full_attn_gain).astype(BF)
-        q_raw, k_raw = dot(normed, wq), dot(normed, wk)
-        v_low = dot(normed, wv).astype(BF)
-        squares = jnp.stack([jnp.sum(q_raw * q_raw, -1), jnp.sum(k_raw * k_raw, -1)])
-        squares = layer_stats(squares, n_dp)
-        roots = lax.rsqrt(squares / width + EPSILON)
-        q_root, k_root = roots[0][:, None], roots[1][:, None]
+        picked = routes[:, :, None] == jnp.arange(experts, dtype=jnp.int32)
+        hits = jnp.any(picked, axis=1)
+        before = jnp.cumsum(hits.astype(jnp.int32), axis=0) - hits.astype(jnp.int32)
+        place = jnp.where(hits, before, -1).astype(BF)
+        place = jnp.pad(place.T, ((0, rows - experts), (0, 0)))
+        sent = jnp.concatenate([grad_out, place], axis=1)
+        hits_wide = jnp.pad(hits.astype(F32), ((0, 0), (0, 128 - experts)))
+        router_wide = jnp.pad(full_router, ((0, 0), (0, 128 - experts)))
         half_dim = HEAD_DIM // 2
         frequency = 10000.0 ** (-jnp.arange(half_dim, dtype=F32) * 2.0 / HEAD_DIM)
         angle = jnp.arange(seq_len, dtype=F32)[:, None] * frequency[None, :]
-        cosine = jnp.concatenate([jnp.cos(angle)] * 2, axis=-1)[None, :, None, :]
-        sine = jnp.concatenate([jnp.sin(angle)] * 2, axis=-1)[None, :, None, :]
-        by_head = (seqs, seq_len, heads, HEAD_DIM)
-
-        def rope(value):
-            value = value.reshape(by_head)
-            return (value * cosine + half_turn(value) * sine).astype(BF)
-
-        def rope_back(value):
-            return (value * cosine + half_turn_back(value * sine)).reshape(seqs * seq_len, cols)
-
-        q_n, k_n = q_raw * q_root, k_raw * k_root
-        q_rot, k_rot = rope(q_n * q_gain_own), rope(k_n * k_gain_own)
-        values = v_low.reshape(by_head)
-        causal = jnp.arange(seq_len)[:, None] >= jnp.arange(seq_len)[None, :]
-        scores = jnp.where(causal, ein("bqhd,bkhd->bhqk", q_rot, k_rot) * scale, -1e30)
-        probs = jax.nn.softmax(scores, axis=-1)
-        probs_low = probs.astype(BF)
-        mixed = ein("bhqk,bkhd->bqhd", probs_low, values).astype(BF).reshape(-1, cols)
-        attn_out = layer_sum(dot(mixed, wo).astype(BF).reshape(group, rows, width), n_dp)
-        residual = layer_input.astype(F32) + attn_out
-        res_root = inv_rms(residual)
-        res_n = residual * res_root
-        normed2 = (res_n * full_ffn_gain).astype(BF)
-
-        logits = dot(normed2, full_router)
-        expert_ids = jnp.arange(experts, dtype=jnp.int32)
-        picked = routes[:, :, None] == expert_ids
-        chosen = jnp.sum(jnp.where(picked, logits[:, None, :], 0.0), axis=-1)
-        gates = jax.nn.softmax(chosen, axis=-1)
-        gates_dense = jnp.sum(jnp.where(picked, gates[:, :, None], 0.0), axis=1)
-        hits = jnp.any(picked, axis=1)
-
-        before = jnp.cumsum(hits.astype(jnp.int32), axis=0) - hits.astype(jnp.int32)
-        place = jnp.where(hits, before, -1).astype(BF)
-        sent = jnp.concatenate([grad_out, place, jnp.zeros((rows, 128 - experts), BF)], axis=1)
-        all_g = lax.all_gather(sent, AXES, axis=0, tiled=True).reshape(n_dev, rows, -1)
-        first = lax.axis_index("ep") * local_experts
-        own_place = lax.dynamic_slice_in_dim(all_g, width + first, local_experts, 2)
-        table = (
-            own_place.transpose(0, 2, 1)[:, :, None, :]
-            == jnp.arange(cap, dtype=jnp.int32).astype(BF)[None, None, :, None]
-        )
-        table = table.astype(BF).reshape(n_dev, local_experts * cap, rows)
-
-        gates_high = gates_dense.astype(BF)
-        gates_rest = (gates_dense - gates_high.astype(F32)).astype(BF)
-        x_own = jnp.concatenate([normed2, gates_high, gates_rest], axis=1)
+        cosine = jnp.concatenate([jnp.cos(angle)] * 2, axis=-1)
+        sine = jnp.concatenate([-jnp.sin(angle), jnp.sin(angle)], axis=-1)
+        tables = (q_gain_own[None], k_gain_own[None], cosine, sine)
+        (
+            normed, q_raw, k_raw, v_low, q_rot, k_rot, mixed, stats,
+            residual, res_n, res_root, gates, x_own, all_g,
+        ) = run_attend(
+            seqs, n_dp, layers, group_input, full_attn_gain[None], qkv, *tables, wo,
+            full_ffn_gain[None], router_wide, hits_wide, sent,
+        )
+        all_g = all_g.reshape((n_dev,) + sent.shape)
+        res_root, gates_dense, normed2 = res_root[:, :1], gates[:, :experts], x_own[:, :width]
+
         expert_sum, grad_sum, x_slots, g_slots, acts = run_experts(
-            x_own, all_g, table, w_gate, w_up, w_down, n_dp, experts, cap
+            x_own, all_g, near_g, w_gate, w_up, w_down, n_dp, experts, cap
         )
         grad_w_gate, grad_w_up, grad_w_down = run_weights(x_slots, g_slots, acts)
         output = (residual + expert_sum).astype(BF)
@@ -1352,45 +1816,34 @@
         grad_logits = (gates_dense * (gate_grads - weighted)).astype(BF)
 
         grad_n2 = grad_sum[:, :width] + ein("te,de->td", grad_logits, full_router)
-        grad_router = ein("td,te->de", normed2, grad_logits)
         grad_y = grad_out.astype(F32)
         grad_ffn_gain = jnp.sum(grad_n2 * res_n, axis=0)
         dn = grad_n2 * full_ffn_gain
         grad_residual = grad_y + res_root * (dn - res_n * jnp.mean(dn * res_n, -1, keepdims=True))
 
-        gao = layer_gather(grad_residual.astype(BF), n_dp).reshape(group * rows, width)
-        grad_wo = ein("td,te->de", mixed, gao)
-        grad_mixed = ein("te,de->td", gao, wo).astype(BF).reshape(by_head)
-        grad_values = ein("bhqk,bqhd->bkhd", probs_low, grad_mixed)
-        grad_probs = ein("bqhd,bkhd->bhqk", grad_mixed, values)
-        delta = jnp.sum(probs * grad_probs, axis=-1, keepdims=True)
-        grad_scores = (probs * (grad_probs - delta)).astype(BF)
-        grad_q_rot = ein("bhqk,bkhd->bqhd", grad_scores, k_rot) * scale
-        grad_k_rot = ein("bhqk,bqhd->bkhd", grad_scores, q_rot) * scale
-        gq, gk = rope_back(grad_q_rot), rope_back(grad_k_rot)
-        grad_q_gain, grad_k_gain = jnp.sum(gq * q_n, axis=0), jnp.sum(gk * k_n, axis=0)
-        gq, gk = gq * q_gain_own, gk * k_gain_own
-        inner = jnp.stack([jnp.sum(gq * q_n, -1), jnp.sum(gk * k_n, -1)])
-        inner = layer_stats(inner, n_dp) / width
-        gq = (q_root * (gq - q_n * inner[0][:, None])).astype(BF)
-        gk = (k_root * (gk - k_n * inner[1][:, None])).astype(BF)
-        gv = grad_values.reshape(-1, cols).astype(BF)
-        grad_normed = ein("te,de->td", gq, wq) + ein("te,de->td", gk, wk)
-        grad_normed = grad_normed + ein("te,de->td", gv, wv)
-        grad_attn_gain = jnp.sum(grad_normed * (group_input * group_root), axis=0)
-        grad_qkv = jnp.stack([ein("td,te->de", normed, part) for part in (gq, gk, gv)]).astype(BF)
+        gao = lax.all_gather(
+            grad_residual.astype(BF), AXES, axis=0, tiled=True, axis_index_groups=rows_of
+        )
+        grad_wo, gq, gk, gv, head_sums, inner = run_attend_back(
+            seqs, gao, wo, mixed, q_rot, k_rot, v_low, q_raw, k_raw, stats, *tables
+        )
+        inner = layer_stats(inner, n_dp)
+        part, grad_qkv, in_sums = run_project_back(
+            group, gq, gk, gv, q_raw, k_raw, stats, inner, qkv, normed, group_input
+        )
 
         def spread(part):
             return lax.dynamic_update_slice_in_dim(jnp.zeros((width,), F32), part, rank * cols, 0)
 
-        gain_grads = jnp.stack(
-            [grad_attn_gain, spread(grad_q_gain), spread(grad_k_gain), grad_ffn_gain], axis=1
-        )
         small_grads = jnp.concatenate(
-            [grad_router, gain_grads, jnp.zeros((width, 128 - experts - 4), F32)], axis=1
-        )
+            [
+                ein("te,td->ed", grad_logits, normed2),
+                in_sums[:1], spread(head_sums[0])[None], spread(head_sums[1])[None],
+                grad_ffn_gain[None], jnp.zeros((128 - experts - 4, width), F32),
+            ]
+        ).T
         grad_normed, grad_qkv, grad_o, small_grads = run_back(
-            grad_normed.astype(BF).reshape(group, rows, width), grad_qkv, grad_wo.astype(BF),
+            part, grad_qkv, grad_wo,
             small_grads.reshape(layers, group, own, 128), n_dp,
         )
         own_input = layer_input.astype(F32)

time: 969 us -> 744 us (0.77)
  Pallas kernels: 775 us -> 672 us
  matrix products: 62.4 us -> 4.26 us
  local copies, waits for them, and re-layouts: 67.6 us -> 15.4 us
  other arithmetic: 32.2 us -> 21.7 us
    pallas_call x1, Pallas kernels: 370 us -> 274 us  [run_experts(): pl.pallas_call(functools.partial(experts_kernel, n_dp, experts), out_shap...]
    pallas_call x2 -> x3, Pallas kernels: 47.6 us -> 140 us  [the longest x1 101 us: run_attend(): pl.pallas_call(functools.partial(attend_kernel, n_dp, layers, seqs), out_...]
    pallas_call x1, Pallas kernels: 179 us -> 99.1 us  [run_front(): pl.pallas_call(functools.partial(front_kernel, n_dp, layers), out_shape=(...]
    dot_general x15 -> x2, matrix products: 48.2 us -> 4.26 us  [ein(): return jnp.einsum(spec, left, right, preferred_element_type=F32)]
    pallas_call x1, Pallas kernels: 120 us -> 105 us  [run_back(): pl.pallas_call(functools.partial(back_kernel, n_dp, layers), out_shape=(s...]
    concatenate x7 -> x1, local copies, waits for them, and re-layouts: 14.3 us -> 2.2 us  [shards(): jnp.concatenate([ein('te,td->ed', grad_logits, normed2), in_sums[:1], spr...]
    unnamed x153 -> x56, local copies, waits for them, and re-layouts: 15.1 us -> 5.05 us
  transfers between devices with their start and end apart: 1 -> 1, of which waited for: 0 -> 0; matrix products, arithmetic and copies ran while one was open for 6% -> 0% of each run, Pallas kernels for 22% -> 7%
where the time goes in v4:
time: 744 us; the launch traced here: 729 us
  Pallas kernels  672 us (90%)
  other arithmetic  21.7 us (3%)
  local copies, waits for them, and re-layouts  15.4 us (2%)
  between operations  14.9 us (2%)
    pallas_call x1, Pallas kernels, run_experts(): pl.pallas_call(functools.partial(experts_kernel, n_dp, experts), out_shap...  274 us
    pallas_call x1, Pallas kernels, run_back(): pl.pallas_call(functools.partial(back_kernel, n_dp, layers), out_shape=(s...  105 us
    pallas_call x1, Pallas kernels, run_attend(): pl.pallas_call(functools.partial(attend_kernel, n_dp, layers, seqs), out_...  101 us
    pallas_call x1, Pallas kernels, run_front(): pl.pallas_call(functools.partial(front_kernel, n_dp, layers), out_shape=(...  99.1 us
    pallas_call x1, Pallas kernels, run_weights(): pl.pallas_call(weights_kernel, grid=(local, total // tile), out_shape=(ja...  48.3 us
    pallas_call x1, Pallas kernels, run_project_back(): pl.pallas_call(project_back_kernel, out_shape=(shape((group, total // gro...  22 us
    pallas_call x1, Pallas kernels, run_attend_back(): pl.pallas_call(functools.partial(attend_back_kernel, seqs), out_shape=(sh...  16.4 us
  transfers between devices with their start and end apart: 1, of which 0 were waited for; matrix products, arithmetic and copies ran while one was open for 0% of the time, Pallas kernels for 7%

profile of v4, /device:TPU:0, one launch (start us, length us, event | category | flops | bytes accessed | tf_op | source)
XLA Modules:
  0.0 728.7 jit_solution(1795995633372756680)
XLA Ops:
  10.7 1.4 maximum_maximum_fusion.small
  12.2 99.1 %shard_map.254 = (bf16[8,128,2048]{2,1,0:T(8,128)(2,1)}, bf16[3,4,512,256]{3,2,1,0:T(8,128)(2,1)}, bf16[4,64,2048]{2,1,0:T(8,128)(2,1)}, bf16[4,8,64,128]{3,2,1,...) custom-call(bf16[128,2048]{1,0:T(8,128)(2,1)} %x_own.1, bf16[64,2048]{1,0:T(8,128)(2,1)} %w_q.1, ...), custom_call_target="tpu_custom_call" | custom-call | tf_op jit(solution)/shard_map/pallas_call | solution.py:1168
  111.2 2.6 convert_reduce_fusion
  115.4 1.6 fusion.15
  117.1 1.9 broadcast_select_fusion.router
  119.0 1.4 pad_convert_fusion.hits
  123.0 1.0 pad_maximum_fusion
  124.0 101.4 %shard_map.255 = (bf16[1024,2048]{1,0:T(8,128)(2,1)}, f32[1024,256]{1,0:T(8,128)}, f32[1024,256]{1,0:T(8,128)}, bf16[1024,256]{1,0:T(8,128)(2,1)}, bf16[1024,256...) custom-call(bf16[1024,2048]{1,0:T(8,128)(2,1)} %bitcast.44, ...), custom_call_target="tpu_custom_call" | custom-call | tf_op jit(solution)/shard_map/pallas_call | solution.py:1611
  225.4 274.2 %shard_map.256 = (f32[128,2048]{1,0:T(8,128)}, f32[128,2176]{1,0:T(8,128)}, bf16[8,32,32,2048]{3,2,1,0:T(8,128)(2,1)}, bf16[8,32,32,2048]{3,2,1,0:T(8,128)(2,1)}...) custom-call(bf16[128,2176]{1,0:T(8,128)(2,1)} %get-tuple-element.59., ...), custom_call_target="tpu_custom_call" | custom-call | flops 51539607552 | bytes 209715200 | tf_op jit(solution)/shard_map/pallas_call | solution.py:592
  499.7 1.1 multiply_reduce_fusion.2
  500.8 2.3 multiply_reduce_fusion
  503.1 1.0 slice_reduce_fusion.2
  504.2 2.5 fusion.18
  506.9 2.0 fusion.10
  509.8 48.3 %shard_map.261 = (f32[8,2048,256]{2,1,0:T(8,128)}, f32[8,2048,256]{2,1,0:T(8,128)}, f32[8,256,2048]{2,1,0:T(8,128)}) custom-call(bf16[8,1024,2048]{2,1,0:T(8,128)(2,1)} %bitcast.64, bf16[8,1024,2048]{2,1,0:T(8,128)(2,1)} %bitcast.65, bf16[3,8,1024,256]{3,2,1,0:T(8,128)(2,1)} %get-tuple-element.90.acts), custom_call_target="tpu_custom_call" | custom-call | flops 25769803776 | bytes 136314880 | tf_op jit(solution)/shard_map/pallas_call | solution.py:665
  558.3 1.0 copy-done.6
  559.3 16.4 %shard_map.257 = (bf16[256,2048]{1,0:T(8,128)(2,1)S(1)}, f32[1024,256]{1,0:T(8,128)S(1)}, f32[1024,256]{1,0:T(8,128)}, bf16[1024,256]{1,0:T(8,128)(2,1)S(1)}, f3...) custom-call(bf16[1024,2048]{1,0:T(8,128)(2,1)} %all-gather.2.cloned.1.call-done.gao, bf16[256,2048]{1,0:T(8,128)(2,1)} %bitcast.53, ...), custom_call_target="tpu_custom_call" | custom-call | tf_op jit(solution)/shard_map/pallas_call | solution.py:1681
  575.7 1.0 copy-done.2
  577.5 6.4 shard_map.258
  584.5 22.0 %shard_map.259 = (bf16[8,128,2048]{2,1,0:T(8,128)(2,1)}, bf16[3,2048,256]{2,1,0:T(8,128)(2,1)}, f32[8,2048]{1,0:T(8,128)}) custom-call(f32[1024,256]{1,0:T(8,128)} %copy-done.2, f32[1024,256]{1,0:T(8,128)} %get-tuple-element.75.gk, bf16[1024,256]{1,0:T(8,128)(2,1)} %copy-done.7, f32[1024,256]{1,0:T(8,128)} %get-tuple-element.71.q_raw, ...), custom_call_target="tpu_custom_call" | custom-call | tf_op jit(solution)/shard_map/pallas_call | solution.py:1731
  608.3 2.2 concatenate.19
  610.9 104.5 %shard_map.260 = (f32[128,2048]{1,0:T(8,128)S(1)}, f32[3,64,2048]{2,1,0:T(8,128)S(1)}, f32[64,2048]{1,0:T(8,128)S(1)}, f32[64,128]{1,0:T(8,128)S(1)}) custom-call(bf16[8,128,2048]{2,1,0:T(8,128)(2,1)} %get-tuple-element.79.part, bf16[3,4,512,256]{3,2,1,0:T(8,128)(2,1)} %bitcast.54, bf16[4,64,2048]{2,1,0:T(8,128)(2,1)S(1)} %bitcast.38, ...), custom_call_target="tpu_custom_call" | custom-call | tf_op jit(solution)/shard_map/pallas_call | solution.py:1398
  715.4 1.2 slice_bitcast_fusion
  717.6 1.6 fusion.6
  (88 shorter events, 15.7 us)
Async XLA Ops:
  7.2 551.0 %all-gather.2.cloned.1.call-start = ((), (), s32[]{:S(2)}) async-start(), calls=%async_computation | async-start | bytes 4718592 | tf_op jit(solution)/shard_map/all_gather | solution.py:1824
  111.2 10.9 %copy-start.16 = (bf16[128,2048]{1,0:T(8,128)(2,1)S(1)}, bf16[128,2048]{1,0:T(8,128)(2,1)}, u32[]{:S(2)}) copy-start(bf16[128,2048]{1,0:T(8,128)(2,1)} %g_own.1) | copy-start | bytes 1572868
  499.6 7.1 copy-start.14
  499.6 7.3 copy-start.21
  499.6 7.3 copy-start.22
  499.6 7.3 copy-start.23
  499.6 9.2 %copy-start.19 = (f32[128,2048]{1,0:T(8,128)S(1)}, f32[128,2048]{1,0:T(8,128)}, u32[]{:S(2)}) copy-start(f32[128,2048]{1,0:T(8,128)} %get-tuple-element.58) | copy-start | bytes 3145732
  499.6 9.2 %copy-start.20 = (f32[128,2048]{1,0:T(8,128)S(1)}, f32[128,2048]{1,0:T(8,128)}, u32[]{:S(2)}) copy-start(f32[128,2048]{1,0:T(8,128)} %get-tuple-element.62) | copy-start | bytes 3145732
  509.8 48.4 %copy-start = (f32[512,128]{1,0:T(8,128)S(1)}, f32[512,128]{1,0:T(8,128)}, u32[]{:S(2)}) copy-start(f32[512,128]{1,0:T(8,128)} %get-tuple-element.111.cosine) | copy-start | bytes 786436
  509.8 48.4 %copy-start.1 = (f32[512,128]{1,0:T(8,128)S(1)}, f32[512,128]{1,0:T(8,128)}, u32[]{:S(2)}) copy-start(f32[512,128]{1,0:T(8,128)} %get-tuple-element.112.sine) | copy-start | bytes 786436
  509.8 48.4 %copy-start.3 = (bf16[1024,256]{1,0:T(8,128)(2,1)S(1)}, bf16[1024,256]{1,0:T(8,128)(2,1)}, u32[]{:S(2)}) copy-start(bf16[1024,256]{1,0:T(8,128)(2,1)} %get-tuple-element.70.v) | copy-start | bytes 1572868
  509.8 48.4 %copy-start.4 = (bf16[1024,256]{1,0:T(8,128)(2,1)S(1)}, bf16[1024,256]{1,0:T(8,128)(2,1)}, u32[]{:S(2)}) copy-start(bf16[1024,256]{1,0:T(8,128)(2,1)} %get-tuple-element.68.q_rot) | copy-start | bytes 1572868
  509.8 48.4 %copy-start.5 = (bf16[1024,256]{1,0:T(8,128)(2,1)S(1)}, bf16[1024,256]{1,0:T(8,128)(2,1)}, u32[]{:S(2)}) copy-start(bf16[1024,256]{1,0:T(8,128)(2,1)} %get-tuple-element.69.k_rot) | copy-start | bytes 1572868
  509.8 48.4 %copy-start.8 = (f32[8,1024]{1,0:T(8,128)S(1)}, f32[8,1024]{1,0:T(8,128)}, u32[]{:S(2)}) copy-start(f32[8,1024]{1,0:T(8,128)} %get-tuple-element.73.stats) | copy-start | bytes 98308
  509.8 48.4 %copy-start.9 = (f32[256]{0:T(256)S(1)}, f32[256]{0:T(256)}, u32[]{:S(2)}) copy-start(f32[256]{0:T(256)} %get-tuple-element.98) | copy-start | bytes 3076
  509.8 48.4 %copy-start.10 = (f32[256]{0:T(256)S(1)}, f32[256]{0:T(256)}, u32[]{:S(2)}) copy-start(f32[256]{0:T(256)} %get-tuple-element.99) | copy-start | bytes 3076
  558.3 1.0 copy-start.6
  584.5 23.8 %copy-start.18 = (f32[64,2048]{1,0:T(8,128)S(1)}, f32[64,2048]{1,0:T(8,128)}, u32[]{:S(2)}) copy-start(f32[64,2048]{1,0:T(8,128)} %fusion.10) | copy-start | bytes 1572868
  610.8 105.8 %copy-start.15 = (bf16[128,2048]{1,0:T(8,128)(2,1)S(1)}, bf16[128,2048]{1,0:T(8,128)(2,1)}, u32[]{:S(2)}) copy-start(bf16[128,2048]{1,0:T(8,128)(2,1)} %x_own.1) | copy-start | bytes 1572868
  610.9 105.8 %copy-start.26 = (f32[2048]{0:T(1024)S(1)}, f32[2048]{0:T(1024)}, u32[]{:S(2)}) copy-start(f32[2048]{0:T(1024)} %get-tuple-element.97) | copy-start | bytes 24580
  715.4 1.8 copy-start.11
  715.4 2.1 copy-start.13
  715.4 2.2 copy-start.17
  715.4 2.2 copy-start.24
  (4 other events, 3.6 us)
Sparse Core Ops, SparseCore 0:
  506.8 51.1 all-gather.1

commit v5 on v4

--- a/solution.py
+++ b/solution.py
@@ -941,43 +941,6 @@
     )
 
 
-def stats_kernel(n_dp, value, out, land, send, recv):
-    here = Place(n_dp)
-    group = 2 * n_dp
-    ranks = others(here, group)
-    greet([peer(here, rank) for rank in ranks])
-
-    def copy(k):
-        return remote(
-            value, land.at[k], send.at[k], recv.at[k], peer(here, ranks[k])
-        )
-
-    for k in range(group - 1):
-        copy(k).start()
-    total = value[...]
-    for k in range(group - 1):
-        copy(k).wait_recv()
-        total += land[k]
-    out[...] = total
-    for k in range(group - 1):
-        copy(k).wait_send()
-
-
-def layer_stats(value, n_dp):
-    dma = pltpu.SemaphoreType.DMA
-    peers = 2 * n_dp - 1
-    flat = value.reshape(-1, 128)
-    out = pl.pallas_call(
-        functools.partial(stats_kernel, n_dp),
-        out_shape=jax.ShapeDtypeStruct(flat.shape, F32),
-        in_specs=[VMEM],
-        out_specs=VMEM,
-        scratch_shapes=[pltpu.VMEM((peers,) + flat.shape, F32), dma((peers,)), dma((peers,))],
-        compiler_params=comm_params(4),
-    )(flat)
-    return out.reshape(value.shape)
-
-
 def front_kernel(
     n_dp, layers, x_own, w_q, w_k, w_v, w_o, small, g_own,
     x_all, qkv, wo, small_all, g_near, wo_col,
@@ -1195,230 +1158,6 @@
     )
 
 
-def back_kernel(
-    n_dp, layers, part, gw, go, small,
-    out, grad_w, grad_o, small_out,
-    acc, sib, one, two, load_sem, n_send, n_recv,
-    acc_w, acc_o, up_w, up_o, down_w, down_o, swapped, s_own, s_land, s_sum, s_far,
-    w_load, o_keep, o_send, o_recv, up_send, up_recv, down_send, down_recv,
-    a_keep, a_send, a_recv, s_keep, s_send, s_recv, t_send, t_recv,
-):
-    here = Place(n_dp)
-    group = 2 * n_dp
-    layer, rank = here.layer, here.rank
-    own = grad_w.shape[1]
-    cols = gw.shape[-1]
-    ranks = others(here, group)
-    away = [flip(layer, i, layers) for i in range(1, layers)]
-    greet([peer(here, r) for r in ranks] + [here.at_layer(z) for z in away])
-    job = LayerSum(here, part, acc, sib, one, two, load_sem, n_send, n_recv)
-
-    def bring():
-        return pltpu.make_async_copy(gw, acc_w, w_load.at[0])
-
-    def share(i):
-        number = rank * layers + i
-        z, target = number // group, number % group
-
-        def far():
-            return remote(
-                go.at[i], acc_o.at[z], o_send.at[i], o_recv.at[z], peer(here, target)
-            )
-
-        def near():
-            return pltpu.make_async_copy(go.at[i], acc_o.at[z], o_keep.at[z])
-
-        return target, far, near
-
-    def small_swap(k):
-        return remote(
-            small.at[:, ranks[k]], s_land.at[k], s_send.at[k], s_recv.at[k], peer(here, ranks[k])
-        )
-
-    def small_keep():
-        return pltpu.make_async_copy(small.at[:, rank], s_own, s_keep.at[0])
-
-    bring().start()
-    job.begin()
-    for i in range(layers):
-        target, far, near = share(i)
-
-        @pl.when(target != rank)
-        def _():
-            far().start()
-
-        @pl.when(target == rank)
-        def _():
-            near().start()
-    small_keep().start()
-    for k in range(group - 1):
-        small_swap(k).start()
-
-    def chain(which, up, z):
-        acc_ref = (acc_w.at[:, z], acc_o.at[z])[which]
-        land = ((up_w, up_o) if up else (down_w, down_o))[which].at[z]
-        sems = (up_send, up_recv) if up else (down_send, down_recv)
-        device = here.at_layer(layer + 1 if up else layer - 1)
-        return remote(acc_ref, land, sems[0].at[which, z], sems[1].at[which, z], device)
-
-    def take(which, up, z):
-        chain(which, up, z).wait_recv()
-        if which == 0:
-            land = up_w if up else down_w
-            for w in range(3):
-                total = acc_w[w, z].astype(F32) + land[z, w].astype(F32)
-                acc_w[w, z] = total.astype(BF)
-        else:
-            land = up_o if up else down_o
-            acc_o[z] = (acc_o[z].astype(F32) + land[z].astype(F32)).astype(BF)
-
-    def hop(which, d):
-        @pl.when(layer + d < layers)
-        def _():
-            @pl.when(layer > 0)
-            def _():
-                take(which, True, layer + d)
-            chain(which, True, layer + d).start()
-
-        @pl.when(layer - d >= 0)
-        def _():
-            @pl.when(layer + 1 < layers)
-            def _():
-                take(which, False, layer - d)
-            chain(which, False, layer - d).start()
-
-    bring().wait()
-    hop(0, layers - 1)
-    job.first()
-    for z in range(layers):
-        source = (z * group + rank) // layers
-
-        @pl.when(source != rank)
-        def _():
-            remote(
-                go.at[0], acc_o.at[z], o_send.at[0], o_recv.at[z], here.sibling
-            ).wait_recv()
-
-        @pl.when(source == rank)
-        def _():
-            pltpu.make_async_copy(go.at[0], acc_o.at[z], o_keep.at[z]).wait()
-    hop(1, layers - 1)
-    small_keep().wait()
-    total = s_own[...]
-    for k in range(group - 1):
-        small_swap(k).wait_recv()
-        total += s_land[k]
-    s_sum[...] = total
-
-    def small_far(i):
-        return remote(
-            s_sum.at[away[i]], s_far.at[i], t_send.at[i], t_recv.at[i], here.at_layer(away[i])
-        )
-
-    for i in range(layers - 1):
-        small_far(i).start()
-    job.second()
-    for d in range(layers - 2, 0, -1):
-        hop(0, d)
-        hop(1, d)
-    job.third(out)
-    total = s_sum[layer]
-    for i in range(layers - 1):
-        small_far(i).wait_recv()
-        total += s_far[i]
-    small_out[...] = total
-
-    for which in range(2):
-        @pl.when(layer > 0)
-        def _():
-            take(which, True, layer)
-
-        @pl.when(layer + 1 < layers)
-        def _():
-            take(which, False, layer)
-
-    def rows_at(index):
-        return pl.ds(pl.multiple_of(index * own, own), own)
-
-    def swap(k):
-        return remote(
-            acc_w.at[:, layer, rows_at(ranks[k])], swapped.at[rank],
-            a_send.at[k], a_recv.at[k], peer(here, ranks[k]),
-        )
-
-    def swap_own():
-        return pltpu.make_async_copy(
-            acc_w.at[:, layer, rows_at(rank)], swapped.at[rank], a_keep.at[0]
-        )
-
-    swap_own().start()
-    for k in range(group - 1):
-        swap(k).start()
-    grad_o[...] = acc_o[layer].astype(F32)
-    swap_own().wait()
-    for k in range(group - 1):
-        swap(k).wait_recv()
-    for r in range(group):
-        for w in range(3):
-            grad_w[w, :, r * cols : (r + 1) * cols] = swapped[r, w].astype(F32)
-
-    for k in range(group - 1):
-        swap(k).wait_send()
-        small_swap(k).wait_send()
-    for i in range(layers - 1):
-        small_far(i).wait_send()
-    for i in range(layers):
-        target, far, near = share(i)
-
-        @pl.when(target != rank)
-        def _():
-            far().wait_send()
-    for which in range(2):
-        for d in range(1, layers):
-            @pl.when(layer + d < layers)
-            def _():
-                chain(which, True, layer + d).wait_send()
-
-            @pl.when(layer - d >= 0)
-            def _():
-                chain(which, False, layer - d).wait_send()
-
-
-def run_back(part, gw, go, small, n_dp):
-    group, rows, width = part.shape
-    cols = gw.shape[-1]
-    layers = small.shape[0]
-    own = small.shape[2]
-    dma = pltpu.SemaphoreType.DMA
-    shape = jax.ShapeDtypeStruct
-    deep = pltpu.VMEM((layers, 3, group * own, cols), BF)
-    flat = pltpu.VMEM((layers, own, width), BF)
-    chain = dma((2, layers))
-    tiny = small.shape[2:]
-    return pl.pallas_call(
-        functools.partial(back_kernel, n_dp, layers),
-        out_shape=(
-            shape((rows, width), F32), shape((3, own, width), F32),
-            shape((own, width), F32), shape(tiny, F32),
-        ),
-        in_specs=[ANY] * 4,
-        out_specs=(VMEM,) * 4,
-        scratch_shapes=LayerSum.scratch(rows, width) + [
-            pltpu.VMEM((3, layers, group * own, cols), BF), flat, deep, flat, deep, flat,
-            pltpu.VMEM((group, 3, own, cols), BF),
-            pltpu.VMEM((layers,) + tiny, F32), pltpu.VMEM((group - 1, layers) + tiny, F32),
-            pltpu.VMEM((layers,) + tiny, F32), pltpu.VMEM((layers,) + tiny, F32),
-            dma((1,)), dma((layers,)), dma((layers,)), dma((layers,)),
-            chain, chain, chain, chain,
-            dma((1,)), dma((group - 1,)), dma((group - 1,)),
-            dma((1,)), dma((group - 1,)), dma((group - 1,)), dma((layers,)), dma((layers,)),
-        ],
-        compiler_params=comm_params(6),
-    )(
-        part, gw.reshape(3, layers, group * own, cols), go.reshape(layers, own, width), small
-    )
-
-
 class LayerTerms:
     def __init__(self, here, ranks, pick, land, send, recv):
         self.here, self.ranks, self.pick = here, ranks, pick
@@ -1443,6 +1182,33 @@
     def end(self):
         for k in range(len(self.ranks)):
             self.copy(k).wait_send()
+
+
+class ColumnTerms:
+    def __init__(self, here, layers, pick, land, send, recv):
+        self.here, self.pick = here, pick
+        self.away = [flip(here.layer, i, layers) for i in range(1, layers)]
+        self.land, self.send, self.recv = land, send, recv
+
+    def copy(self, i):
+        return remote(
+            self.pick(self.away[i]), self.land.at[i], self.send.at[i], self.recv.at[i],
+            self.here.at_layer(self.away[i]),
+        )
+
+    def begin(self):
+        for i in range(len(self.away)):
+            self.copy(i).start()
+
+    def total(self, own):
+        for i in range(len(self.away)):
+            self.copy(i).wait_recv()
+            own = own + self.land[i].astype(F32)
+        return own
+
+    def end(self):
+        for i in range(len(self.away)):
+            self.copy(i).wait_send()
 
 
 def as_row(column):
@@ -1632,19 +1398,140 @@
     return result
 
 
-def attend_back_kernel(
-    seqs, gao, wo, mixed, q_rot, k_rot, v, q_raw, k_raw, stats, q_gain, k_gain, cosine, sine,
-    grad_wo, gq, gk, gv, gains, inner, grad_mixed,
+def back_kernel(
+    n_dp, layers, seqs,
+    gao, wo, mixed, q_rot, k_rot, v, normed, q_raw, k_raw, stats, q_gain, k_gain, cosine, sine,
+    w, x, early,
+    out, grad_w, grad_o, small_out,
+    grad_mixed, gq, gk, low, inner, gains, rowmat, small, part,
+    acc, sib, one, two, load_sem, n_send, n_recv,
+    go, acc_w, acc_o, up_w, up_o, up_v, down_w, down_o, down_v, swapped, land, s_land, s_sum, s_far,
+    i_send, i_recv, o_keep, o_send, o_recv, up_send, up_recv, down_send, down_recv,
+    a_keep, a_send, a_recv, s_send, s_recv, t_send, t_recv,
 ):
+    here = Place(n_dp)
+    group = 2 * n_dp
+    layer, rank = here.layer, here.rank
     total, cols = q_raw.shape
     width = wo.shape[1]
+    own = grad_w.shape[1]
+    size = group * own
     length = total // seqs
     scale = HEAD_DIM ** (-0.5)
+    last = layers - 1
+    ranks = others(here, group)
+    greet(
+        [peer(here, r) for r in ranks]
+        + [here.at_layer(flip(layer, i, layers)) for i in range(1, layers)]
+    )
+    job = LayerSum(here, part, acc, sib, one, two, load_sem, n_send, n_recv)
+    terms = LayerTerms(here, ranks, lambda r: inner, land, i_send, i_recv)
+    small_terms = LayerTerms(here, ranks, lambda r: small.at[:, r], s_land, s_send, s_recv)
+    far_terms = ColumnTerms(here, layers, lambda z: s_sum.at[z], s_far, t_send, t_recv)
+
+    def share(i):
+        number = rank * layers + i
+        z, target = number // group, number % group
+
+        def far():
+            return remote(
+                go.at[i], acc_o.at[z], o_send.at[i], o_recv.at[z], peer(here, target)
+            )
+
+        def near():
+            return pltpu.make_async_copy(go.at[i], acc_o.at[z], o_keep.at[z])
+
+        return target, far, near
+
+    def shared(z):
+        source = (z * group + rank) // layers
+
+        @pl.when(source != rank)
+        def _():
+            remote(
+                go.at[0], acc_o.at[z], o_send.at[0], o_recv.at[z], here.sibling
+            ).wait_recv()
+
+        @pl.when(source == rank)
+        def _():
+            pltpu.make_async_copy(go.at[0], acc_o.at[z], o_keep.at[z]).wait()
+
+    def rows_of(z):
+        return pl.ds(pl.multiple_of(z * size, size), size)
+
+    def chain(which, up, z):
+        src = (acc_w.at[0:2, rows_of(z)], acc_o.at[z], acc_w.at[2, rows_of(z)])[which]
+        to = ((up_w, up_o, up_v) if up else (down_w, down_o, down_v))[which].at[z]
+        sems = (up_send, up_recv) if up else (down_send, down_recv)
+        device = here.at_layer(layer + 1 if up else layer - 1)
+        return remote(src, to, sems[0].at[which, z], sems[1].at[which, z], device)
+
+    def take(which, up, z):
+        chain(which, up, z).wait_recv()
+        if which == 0:
+            got = up_w if up else down_w
+            for i in range(2):
+                value = acc_w[i, rows_of(z)].astype(F32) + got[z, i].astype(F32)
+                acc_w[i, rows_of(z)] = value.astype(BF)
+        elif which == 1:
+            got = up_o if up else down_o
+            acc_o[z] = (acc_o[z].astype(F32) + got[z].astype(F32)).astype(BF)
+        else:
+            got = up_v if up else down_v
+            value = acc_w[2, rows_of(z)].astype(F32) + got[z].astype(F32)
+            acc_w[2, rows_of(z)] = value.astype(BF)
+
+    def launch(which):
+        for d in range(last, 0, -1):
+            @pl.when(layer == 0)
+            def _():
+                chain(which, True, layer + d).start()
+
+            @pl.when(layer == last)
+            def _():
+                chain(which, False, layer - d).start()
+
+    def relay(which, d):
+        @pl.when(jnp.logical_and(layer > 0, layer + d < layers))
+        def _():
+            take(which, True, layer + d)
+            chain(which, True, layer + d).start()
+
+        @pl.when(jnp.logical_and(layer < last, layer - d >= 0))
+        def _():
+            take(which, False, layer - d)
+            chain(which, False, layer - d).start()
+
+    def relay_all(which):
+        for d in range(last - 1, 0, -1):
+            relay(which, d)
+
+    def settle(which):
+        @pl.when(layer > 0)
+        def _():
+            take(which, True, layer)
+
+        @pl.when(layer < last)
+        def _():
+            take(which, False, layer)
+
     for n in range(0, width, STEP):
-        grad_wo[:, n : n + STEP] = tdot(mixed[...], gao[:, n : n + STEP]).astype(BF)
+        got = tdot(mixed[...], gao[:, n : n + STEP]).astype(BF)
+        go[:, :, n : n + STEP] = got.reshape(layers, own, STEP)
+    for i in range(layers):
+        target, far, near = share(i)
+
+        @pl.when(target != rank)
+        def _():
+            far().start()
+
+        @pl.when(target == rank)
+        def _():
+            near().start()
     grad_mixed[...] = dot_t(gao[...], wo[...]).astype(BF)
     inner[...] = jnp.zeros_like(inner)
     gains[...] = jnp.zeros_like(gains)
+
     for s in range(seqs):
         rows = slice(s * length, (s + 1) * length)
         roots = [
@@ -1656,11 +1543,11 @@
             q, k = q_rot[rows, head], k_rot[rows, head]
             probs = probabilities(q, k, scale)
             gm = grad_mixed[rows, head]
-            gv[rows, head] = tdot(probs.astype(BF), gm).astype(BF)
+            low[2, rows, head] = tdot(probs.astype(BF), gm).astype(BF)
             grad_probs = dot_t(gm, v[rows, head])
             delta = row_sum(probs * grad_probs)
             grad_scores = (probs * (grad_probs - delta)).astype(BF)
-            for i, (turned, raw, gain, out) in enumerate((
+            for i, (turned, raw, gain, to) in enumerate((
                 (dot(grad_scores, k) * scale, q_raw, q_gain, gq),
                 (tdot(grad_scores, q) * scale, k_raw, k_gain, gk),
             )):
@@ -1668,77 +1555,158 @@
                 unit = raw[rows, head] * roots[i]
                 gains[i : i + 1, head] += jnp.sum(back * unit, axis=0, keepdims=True)
                 back = back * gain[:, head]
-                out[rows, head] = back
+                to[rows, head] = back
                 inners[i] = inners[i] + row_sum(back * unit)
         for i in range(2):
             inner[i : i + 1, rows] = as_row(inners[i])
-
-
-def run_attend_back(seqs, gao, wo, mixed, q_rot, k_rot, v, q_raw, k_raw, stats, *rest):
-    total, cols = q_raw.shape
-    width = wo.shape[1]
-    shape = jax.ShapeDtypeStruct
-    return pl.pallas_call(
-        functools.partial(attend_back_kernel, seqs),
-        out_shape=(
-            shape((cols, width), BF), shape((total, cols), F32), shape((total, cols), F32),
-            shape((total, cols), BF), shape((8, cols), F32), shape((8, total), F32),
-        ),
-        in_specs=[VMEM] * 13,
-        out_specs=(VMEM,) * 6,
-        scratch_shapes=[pltpu.VMEM((total, cols), BF)],
-        compiler_params=pltpu.CompilerParams(vmem_limit_bytes=48 * 2**20),
-    )(gao, wo, mixed, q_rot, k_rot, v, q_raw, k_raw, stats, *rest)
-
-
-def project_back_kernel(
-    gq, gk, gv, q_raw, k_raw, stats, inner, w, normed, x, part, grad_w, gain, low,
-):
-    total, cols = gq.shape
-    group, rows, width = part.shape
+        if s == 0:
+            for z in range(layers):
+                shared(z)
+            launch(1)
+    terms.begin()
+
+    def weight_grads(i):
+        for n in range(0, width, STEP):
+            acc_w[i, n : n + STEP, :] = tdot(normed[:, n : n + STEP], low[i]).astype(BF)
+
+    weight_grads(2)
+    launch(2)
+    relay_all(1)
+    means = terms.total(inner[...]) / width
     for i, (grad, raw) in enumerate(((gq, q_raw), (gk, k_raw))):
         root = as_column(lax.rsqrt(stats[i : i + 1, :] / width + EPSILON))
-        mean = as_column(inner[i : i + 1, :] / width)
+        mean = as_column(means[i : i + 1, :])
         low[i] = (root * (grad[...] - raw[...] * root * mean)).astype(BF)
-    low[2] = gv[...]
-    gain[...] = jnp.zeros_like(gain)
-
-    def block(b, c):
-        at = pl.ds(pl.multiple_of(b * rows, rows), rows)
+        weight_grads(i)
+    launch(0)
+    rowmat[...] = early[...]
+
+    def project(b, c):
+        at = pl.ds(pl.multiple_of(b * part.shape[1], part.shape[1]), part.shape[1])
         value = x[at, :].astype(F32)
         root = lax.rsqrt(row_sum(value * value) / width + EPSILON)
         for n in range(0, width, STEP):
             cut = slice(n, n + STEP)
-            total = dot_t(low[0, at, :], w[0, cut, :]) + dot_t(low[1, at, :], w[1, cut, :])
-            total = total + dot_t(low[2, at, :], w[2, cut, :])
-            part[b, :, cut] = total.astype(BF)
+            got = dot_t(low[0, at, :], w[0, cut, :]) + dot_t(low[1, at, :], w[1, cut, :])
+            got = got + dot_t(low[2, at, :], w[2, cut, :])
+            part[b, :, cut] = got.astype(BF)
             unit = x[at, cut].astype(F32) * root
-            gain[0:1, cut] += jnp.sum(total * unit, axis=0, keepdims=True)
+            rowmat[64:65, cut] += jnp.sum(got * unit, axis=0, keepdims=True)
         return c
 
-    lax.fori_loop(0, group, block, 0)
-    for n in range(0, width, STEP):
-        cut = slice(n, n + STEP)
-        rows_t = normed[:, cut]
+    lax.fori_loop(0, group, project, 0)
+    job.begin()
+    head_cols = pl.ds(pl.multiple_of(rank * cols, cols), cols)
+    rowmat[65:66, head_cols] = gains[0:1, :]
+    rowmat[66:67, head_cols] = gains[1:2, :]
+    for n in range(0, width, 128):
+        turned = rowmat[:, n : n + 128].T
+        for i in range(128 // own):
+            number = n // own + i
+            small[number // group, number % group] = turned[i * own : (i + 1) * own]
+    relay_all(2)
+    job.first()
+    small_terms.begin()
+    for d in range(last - 1, 0, -1):
+        relay(0, d)
+        if d == last - 1:
+            job.second()
+    if last < 2:
+        job.second()
+    s_sum[...] = small_terms.total(small[:, rank])
+    far_terms.begin()
+    job.third(out)
+    settle(1)
+    settle(2)
+    grad_o[...] = acc_o[layer].astype(F32)
+    small_out[...] = far_terms.total(s_sum[layer])
+    settle(0)
+
+    def block(index):
+        return acc_w.at[:, pl.ds(pl.multiple_of(layer * size + index * own, own), own)]
+
+    def swap(k):
+        return remote(
+            block(ranks[k]), swapped.at[rank], a_send.at[k], a_recv.at[k], peer(here, ranks[k])
+        )
+
+    def swap_own():
+        return pltpu.make_async_copy(block(rank), swapped.at[rank], a_keep.at[0])
+
+    swap_own().start()
+    for k in range(group - 1):
+        swap(k).start()
+    swap_own().wait()
+    for k in range(group - 1):
+        swap(k).wait_recv()
+    for r in range(group):
         for i in range(3):
-            grad_w[i, cut, :] = tdot(rows_t, low[i]).astype(BF)
-
-
-def run_project_back(group, gq, gk, gv, q_raw, k_raw, stats, inner, w, normed, x):
-    total, cols = gq.shape
-    width = x.shape[1]
+            grad_w[i, :, r * cols : (r + 1) * cols] = swapped[r, i].astype(F32)
+
+    terms.end()
+    small_terms.end()
+    far_terms.end()
+    for k in range(group - 1):
+        swap(k).wait_send()
+    for i in range(layers):
+        target, far, near = share(i)
+
+        @pl.when(target != rank)
+        def _():
+            far().wait_send()
+    for which in range(3):
+        for d in range(1, layers):
+            @pl.when(layer + d < layers)
+            def _():
+                chain(which, True, layer + d).wait_send()
+
+            @pl.when(layer - d >= 0)
+            def _():
+                chain(which, False, layer - d).wait_send()
+
+
+def run_back(seqs, n_dp, layers, gao, wo, mixed, q_rot, k_rot, v, normed, q_raw, k_raw, *rest):
+    total, cols = q_raw.shape
+    width = wo.shape[1]
+    group = 2 * n_dp
+    rows = total // group
+    own = width // (layers * group)
+    size = group * own
+    dma = pltpu.SemaphoreType.DMA
     shape = jax.ShapeDtypeStruct
+    many, few = dma((3, layers)), dma((layers,))
+    near = dma((group - 1,))
+    tiny = (layers, own, 128)
     return pl.pallas_call(
-        project_back_kernel,
+        functools.partial(back_kernel, n_dp, layers, seqs),
         out_shape=(
-            shape((group, total // group, width), BF), shape((3, width, cols), BF),
-            shape((8, width), F32),
+            shape((rows, width), F32), shape((3, own, width), F32),
+            shape((own, width), F32), shape((own, 128), F32),
         ),
-        in_specs=[VMEM] * 10,
-        out_specs=(VMEM,) * 3,
-        scratch_shapes=[pltpu.VMEM((3, total, cols), BF)],
-        compiler_params=pltpu.CompilerParams(vmem_limit_bytes=56 * 2**20),
-    )(gq, gk, gv, q_raw, k_raw, stats, inner, w, normed, x)
+        in_specs=[VMEM] * 17,
+        out_specs=(VMEM,) * 4,
+        scratch_shapes=[
+            pltpu.VMEM((total, cols), BF), pltpu.VMEM((total, cols), F32),
+            pltpu.VMEM((total, cols), F32), pltpu.VMEM((3, total, cols), BF),
+            pltpu.VMEM((8, total), F32), pltpu.VMEM((8, cols), F32),
+            pltpu.VMEM((128, width), F32), pltpu.VMEM((layers, group, own, 128), F32),
+            pltpu.VMEM((group, rows, width), BF),
+        ] + LayerSum.scratch(rows, width) + [
+            pltpu.VMEM((layers, own, width), BF), pltpu.VMEM((3, width, cols), BF),
+            pltpu.VMEM((layers, own, width), BF),
+        ] + [
+            pltpu.VMEM((layers, 2, size, cols), BF), pltpu.VMEM((layers, own, width), BF),
+            pltpu.VMEM((layers, size, cols), BF),
+        ] * 2 + [
+            pltpu.VMEM((group, 3, own, cols), BF), pltpu.VMEM((group - 1, 8, total), F32),
+            pltpu.VMEM((group - 1,) + tiny, F32), pltpu.VMEM(tiny, F32), pltpu.VMEM(tiny, F32),
+            near, near, few, few, few, many, many, many, many,
+            dma((1,)), near, near, near, near, few, few,
+        ],
+        compiler_params=pltpu.CompilerParams(
+            collective_id=6, has_side_effects=True, vmem_limit_bytes=63 * 2**20
+        ),
+    )(gao, wo, mixed, q_rot, k_rot, v, normed, q_raw, k_raw, *rest)
 
 
 def ein(spec, left, right):
@@ -1824,27 +1792,15 @@
         gao = lax.all_gather(
             grad_residual.astype(BF), AXES, axis=0, tiled=True, axis_index_groups=rows_of
         )
-        grad_wo, gq, gk, gv, head_sums, inner = run_attend_back(
-            seqs, gao, wo, mixed, q_rot, k_rot, v_low, q_raw, k_raw, stats, *tables
-        )
-        inner = layer_stats(inner, n_dp)
-        part, grad_qkv, in_sums = run_project_back(
-            group, gq, gk, gv, q_raw, k_raw, stats, inner, qkv, normed, group_input
-        )
-
-        def spread(part):
-            return lax.dynamic_update_slice_in_dim(jnp.zeros((width,), F32), part, rank * cols, 0)
-
-        small_grads = jnp.concatenate(
+        early = jnp.concatenate(
             [
-                ein("te,td->ed", grad_logits, normed2),
-                in_sums[:1], spread(head_sums[0])[None], spread(head_sums[1])[None],
+                ein("te,td->ed", grad_logits, normed2), jnp.zeros((3, width), F32),
                 grad_ffn_gain[None], jnp.zeros((128 - experts - 4, width), F32),
             ]
-        ).T
+        )
         grad_normed, grad_qkv, grad_o, small_grads = run_back(
-            part, grad_qkv, grad_wo,
-            small_grads.reshape(layers, group, own, 128), n_dp,
+            seqs, n_dp, layers, gao, wo, mixed, q_rot, k_rot, v_low, normed, q_raw, k_raw, stats,
+            *tables, qkv, group_input, early,
         )
         own_input = layer_input.astype(F32)
         in_root = inv_rms(own_input)

time: 744 us -> 702 us (0.944)
  Pallas kernels: 672 us -> 641 us
    pallas_call x4 -> x1, Pallas kernels: 149 us -> 119 us  [run_back(): pl.pallas_call(functools.partial(back_kernel, n_dp, layers, seqs), out_sh...]
  transfers between devices with their start and end apart: 1 -> 1, of which waited for: 0 -> 0; matrix products, arithmetic and copies ran while one was open for 0% -> 1% of each run, Pallas kernels for 7% -> 7%
where the time goes in v5:
time: 702 us; the launch traced here: 693 us
  Pallas kernels  641 us (91%)
  other arithmetic  23.9 us (3%)
  between operations  14.8 us (2%)
  local copies, waits for them, and re-layouts  8.84 us (1%)
    pallas_call x1, Pallas kernels, run_experts(): pl.pallas_call(functools.partial(experts_kernel, n_dp, experts), out_shap...  274 us
    pallas_call x1, Pallas kernels, run_back(): pl.pallas_call(functools.partial(back_kernel, n_dp, layers, seqs), out_sh...  119 us
    pallas_call x1, Pallas kernels, run_attend(): pl.pallas_call(functools.partial(attend_kernel, n_dp, layers, seqs), out_...  101 us
    pallas_call x1, Pallas kernels, run_front(): pl.pallas_call(functools.partial(front_kernel, n_dp, layers), out_shape=(...  99.1 us
    pallas_call x1, Pallas kernels, run_weights(): pl.pallas_call(weights_kernel, grid=(local, total // tile), out_shape=(ja...  48 us
  transfers between devices with their start and end apart: 1, of which 0 were waited for; matrix products, arithmetic and copies ran while one was open for 1% of the time, Pallas kernels for 7%

profile of v5, /device:TPU:0, one launch (start us, length us, event | category | flops | bytes accessed | tf_op | source)
XLA Modules:
  0.0 692.7 jit_solution(12172001568442255876)
XLA Ops:
  10.0 1.8 fusion.15
  11.8 1.9 fusion.8.g_own
  13.7 1.4 maximum_maximum_fusion.1.small
  15.1 99.1 %shard_map.254 = (bf16[8,128,2048]{2,1,0:T(8,128)(2,1)}, bf16[3,4,512,256]{3,2,1,0:T(8,128)(2,1)}, bf16[4,64,2048]{2,1,0:T(8,128)(2,1)}, bf16[4,8,64,128]{3,2,1,...) custom-call(bf16[128,2048]{1,0:T(8,128)(2,1)} %x_own.1, bf16[64,2048]{1,0:T(8,128)(2,1)} %w_q.1, ...), custom_call_target="tpu_custom_call" | custom-call | tf_op jit(solution)/shard_map/pallas_call | solution.py:1131
  114.2 2.6 convert_reduce_fusion
  116.7 0.8 dynamic-slice_convert_fusion
  117.6 0.8 slice_reduce_fusion
  118.4 1.9 broadcast_select_fusion.router
  120.3 2.3 pad_maximum_fusion
  122.6 101.4 %shard_map.255 = (bf16[1024,2048]{1,0:T(8,128)(2,1)}, f32[1024,256]{1,0:T(8,128)}, f32[1024,256]{1,0:T(8,128)}, bf16[1024,256]{1,0:T(8,128)(2,1)}, bf16[1024,256...) custom-call(bf16[1024,2048]{1,0:T(8,128)(2,1)} %bitcast.33, ...), custom_call_target="tpu_custom_call" | custom-call | tf_op jit(solution)/shard_map/pallas_call | solution.py:1377
  224.0 1.5 slice_reduce_fusion.2
  225.5 274.1 %shard_map.256 = (f32[128,2048]{1,0:T(8,128)}, f32[128,2176]{1,0:T(8,128)}, bf16[8,32,32,2048]{3,2,1,0:T(8,128)(2,1)}, bf16[8,32,32,2048]{3,2,1,0:T(8,128)(2,1)}...) custom-call(bf16[128,2176]{1,0:T(8,128)(2,1)} %get-tuple-element.50., ...), custom_call_target="tpu_custom_call" | custom-call | flops 51539607552 | bytes 209715200 | tf_op jit(solution)/shard_map/pallas_call | solution.py:592
  499.6 1.0 multiply_reduce_fusion.2
  500.7 2.3 multiply_reduce_fusion
  503.0 1.0 copy-done.1
  504.0 2.5 fusion.18
  507.0 1.4 fusion.10
  508.4 1.2 maximum_maximum_fusion.early
  509.5 0.9 add_convert_fusion
  510.4 48.0 %shard_map.258 = (f32[8,2048,256]{2,1,0:T(8,128)}, f32[8,2048,256]{2,1,0:T(8,128)}, f32[8,256,2048]{2,1,0:T(8,128)}) custom-call(bf16[8,1024,2048]{2,1,0:T(8,128)(2,1)} %bitcast.56, bf16[8,1024,2048]{2,1,0:T(8,128)(2,1)} %bitcast.57, bf16[3,8,1024,256]{3,2,1,0:T(8,128)(2,1)} %get-tuple-element.72.acts), custom_call_target="tpu_custom_call" | custom-call | flops 25769803776 | bytes 136314880 | tf_op jit(solution)/shard_map/pallas_call | solution.py:665
  558.5 118.7 %shard_map.257 = (f32[128,2048]{1,0:T(8,128)}, f32[3,64,2048]{2,1,0:T(8,128)}, f32[64,2048]{1,0:T(8,128)}, f32[64,128]{1,0:T(8,128)}) custom-call(bf16[1024,2048]{1,0:T(8,128)(2,1)} %all-gather.2.cloned.1.call-done.gao, bf16[256,2048]{1,0:T(8,128)(2,1)} %bitcast.41, bf16[1024,256]{1,0:T(8,128)(2,1)} %get-tuple-element.58.mixed, ...), custom_call_target="tpu_custom_call" | custom-call | tf_op jit(solution)/shard_map/pallas_call | solution.py:1680
  677.3 2.7 slice_bitcast_fusion
  680.0 1.6 fusion.3
  681.6 1.6 fusion.6
  (58 shorter events, 5.4 us)
Async XLA Ops:
  7.2 551.3 %all-gather.2.cloned.1.call-start = ((), (), s32[]{:S(2)}) async-start(), calls=%async_computation | async-start | bytes 4718592 | tf_op jit(solution)/shard_map/all_gather | solution.py:1792
  8.1 1.3 copy-start.11
  499.6 7.1 %copy-start.3 = (bf16[128,2048]{1,0:T(8,128)(2,1)S(1)}, bf16[128,2048]{1,0:T(8,128)(2,1)}, u32[]{:S(2)}) copy-start(bf16[128,2048]{1,0:T(8,128)(2,1)} %x_own.1) | copy-start | bytes 1572868
  499.6 7.3 %copy-start.9 = (f32[128,128]{1,0:T(8,128)S(1)}, f32[128,128]{1,0:T(8,128)}, u32[]{:S(2)}) copy-start(f32[128,128]{1,0:T(8,128)} %get-tuple-element.56) | copy-start | bytes 196612
  499.6 7.3 %copy-start.12 = (pred[128,64]{1,0:T(32,128)(4,1)S(1)}, pred[128,64]{1,0:T(32,128)(4,1)}, u32[]{:S(2)}) copy-start(pred[128,64]{1,0:T(32,128)(4,1)} %copy-done.11) | copy-start | bytes 24580
  503.0 1.1 copy-start.1
  503.0 6.5 copy-start.6
  503.0 6.5 copy-start.7
  558.5 121.5 %copy-start.14 = (f32[2048]{0:T(1024)S(1)}, f32[2048]{0:T(1024)}, u32[]{:S(2)}) copy-start(f32[2048]{0:T(1024)} %get-tuple-element.79) | copy-start | bytes 24580
  677.2 4.4 copy-start
  677.2 4.4 copy-start.2
  677.2 4.4 copy-start.4
  677.3 4.4 copy-start.5
  677.3 4.4 copy-start.13
  677.3 4.3 copy-start.15
  680.0 3.3 copy-start.8
  680.0 4.0 copy-start.10
Sparse Core Ops, SparseCore 0:
  506.7 51.2 all-gather.1

commit v6 on v5

--- a/solution.py
+++ b/solution.py
@@ -2,6 +2,7 @@
 
 import jax
 import jax.numpy as jnp
+import numpy as np
 from jax import lax
 from jax.experimental import pallas as pl
 from jax.experimental.pallas import tpu as pltpu
@@ -1241,9 +1242,9 @@
 
 def attend_kernel(
     n_dp, layers, seqs,
-    x, gain, w, q_gain, k_gain, cosine, sine, wo, ffn_gain, router, hits, g_own,
+    x, small, w, cosine, sine, wo, hits, g_own,
     normed, q_raw, k_raw, v, q_rot, k_rot, mixed, stats,
-    residual, res_unit, res_root, gates, x_out, g_all,
+    residual, res_unit, res_root, gates, x_out, gain_rows, head_gains, g_all,
     part, squares, land, n_send, n_recv, out, p_send, p_recv,
     acc, sib, one, two, load_sem, l_send, l_recv, g_keep, gz_send, gz_recv, g_send, g_recv,
 ):
@@ -1270,6 +1271,14 @@
     for k in range(group - 1):
         seats(k).start()
 
+    experts = small.shape[1] // 2
+    for n in range(0, width, 128):
+        turned = small[n : n + 128, :].astype(F32).T
+        gain_rows[:, n : n + 128] = turned[experts : experts + 8]
+    head_cols = pl.ds(pl.multiple_of(here.rank * cols, cols), cols)
+    head_gains[...] = gain_rows[:, head_cols]
+    gain, ffn_gain = gain_rows[0:1, :], gain_rows[3:4, :]
+
     tile = 256
     squares[...] = jnp.zeros_like(squares)
 
@@ -1277,7 +1286,7 @@
         at = slice(t * tile, (t + 1) * tile)
         value = x[at, :].astype(F32)
         root = lax.rsqrt(row_sum(value * value) / width + EPSILON)
-        low = (value * root * gain[...]).astype(BF)
+        low = (value * root * gain).astype(BF)
         normed[at, :] = low
         q, k = dot(low, w[0]), dot(low, w[1])
         q_raw[at, :] = q
@@ -1303,9 +1312,10 @@
             head = slice(h, h + HEAD_DIM)
             turned = []
             for raw, root, scale, to in (
-                (q_raw, roots[0], q_gain, q_rot), (k_raw, roots[1], k_gain, k_rot),
+                (q_raw, roots[0], head_gains[1:2, head], q_rot),
+                (k_raw, roots[1], head_gains[2:3, head], k_rot),
             ):
-                value = raw[rows, head] * root * scale[:, head]
+                value = raw[rows, head] * root * scale
                 value = (value * cosine[...] + swap_halves(value) * sine[...]).astype(BF)
                 to[rows, head] = value
                 turned.append(value)
@@ -1344,9 +1354,9 @@
     unit = value * root
     res_unit[...] = unit
     res_root[...] = jnp.broadcast_to(root, res_root.shape)
-    low = (unit * ffn_gain[...]).astype(BF)
+    low = (unit * ffn_gain).astype(BF)
     x_out[:, :width] = low
-    logits = dot(low, router[...])
+    logits = dot(low, small[...])
     chosen = hits[...] > 0.0
     top_logit = jnp.max(jnp.where(chosen, logits, -1e30), axis=1, keepdims=True)
     grown = jnp.where(chosen, jnp.exp(jnp.minimum(logits - top_logit, 0.0)), 0.0)
@@ -1365,7 +1375,7 @@
         seats(k).wait()
 
 
-def run_attend(seqs, n_dp, layers, x, gain, w, *rest):
+def run_attend(seqs, n_dp, layers, x, small, w, *rest):
     g_own = rest[-1]
     total, width = x.shape
     cols = w.shape[-1]
@@ -1380,10 +1390,11 @@
             shape((total, width), BF), narrow_f, narrow_f, narrow, narrow, narrow, narrow,
             shape((8, total), F32), shape((rows, width), F32), shape((rows, width), F32),
             shape((rows, 128), F32), shape((rows, 128), F32), shape((rows, width + 128), BF),
+            shape((8, width), F32), shape((8, cols), F32),
             shape((layers, group) + g_own.shape, BF),
         ),
-        in_specs=[VMEM] * 11 + [ANY],
-        out_specs=(VMEM,) * 13 + (ANY,),
+        in_specs=[VMEM] * 7 + [ANY],
+        out_specs=(VMEM,) * 15 + (ANY,),
         scratch_shapes=[
             pltpu.VMEM((group, rows, width), BF), pltpu.VMEM((8, total), F32),
             pltpu.VMEM((group - 1, 8, total), F32), dma((group - 1,)), dma((group - 1,)),
@@ -1394,13 +1405,13 @@
         compiler_params=pltpu.CompilerParams(
             collective_id=2, has_side_effects=True, vmem_limit_bytes=56 * 2**20
         ),
-    )(x, gain, w, *rest)
+    )(x, small, w, *rest)
     return result
 
 
 def back_kernel(
     n_dp, layers, seqs,
-    gao, wo, mixed, q_rot, k_rot, v, normed, q_raw, k_raw, stats, q_gain, k_gain, cosine, sine,
+    gao, wo, mixed, q_rot, k_rot, v, normed, q_raw, k_raw, stats, head_gains, cosine, sine,
     w, x, early,
     out, grad_w, grad_o, small_out,
     grad_mixed, gq, gk, low, inner, gains, rowmat, small, part,
@@ -1548,13 +1559,13 @@
             delta = row_sum(probs * grad_probs)
             grad_scores = (probs * (grad_probs - delta)).astype(BF)
             for i, (turned, raw, gain, to) in enumerate((
-                (dot(grad_scores, k) * scale, q_raw, q_gain, gq),
-                (tdot(grad_scores, q) * scale, k_raw, k_gain, gk),
+                (dot(grad_scores, k) * scale, q_raw, head_gains[1:2, head], gq),
+                (tdot(grad_scores, q) * scale, k_raw, head_gains[2:3, head], gk),
             )):
                 back = turned * cosine[...] - swap_halves(turned) * sine[...]
                 unit = raw[rows, head] * roots[i]
                 gains[i : i + 1, head] += jnp.sum(back * unit, axis=0, keepdims=True)
-                back = back * gain[:, head]
+                back = back * gain
                 to[rows, head] = back
                 inners[i] = inners[i] + row_sum(back * unit)
         for i in range(2):
@@ -1683,7 +1694,7 @@
             shape((rows, width), F32), shape((3, own, width), F32),
             shape((own, width), F32), shape((own, 128), F32),
         ),
-        in_specs=[VMEM] * 17,
+        in_specs=[VMEM] * 16,
         out_specs=(VMEM,) * 4,
         scratch_shapes=[
             pltpu.VMEM((total, cols), BF), pltpu.VMEM((total, cols), F32),
@@ -1745,10 +1756,6 @@
             layer_input, w_q, w_k, w_v, w_o, small, grad_out, n_dp, n_dev
         )
         full_router = small[:, :experts]
-        full_attn_gain = small[:, experts].astype(F32)
-        full_ffn_gain = small[:, experts + 3].astype(F32)
-        head_gains = lax.dynamic_slice_in_dim(small, rank * cols, cols, 0).astype(F32)
-        q_gain_own, k_gain_own = head_gains[:, experts + 1], head_gains[:, experts + 2]
 
         picked = routes[:, :, None] == jnp.arange(experts, dtype=jnp.int32)
         hits = jnp.any(picked, axis=1)
@@ -1757,20 +1764,19 @@
         place = jnp.pad(place.T, ((0, rows - experts), (0, 0)))
         sent = jnp.concatenate([grad_out, place], axis=1)
         hits_wide = jnp.pad(hits.astype(F32), ((0, 0), (0, 128 - experts)))
-        router_wide = jnp.pad(full_router, ((0, 0), (0, 128 - experts)))
         half_dim = HEAD_DIM // 2
-        frequency = 10000.0 ** (-jnp.arange(half_dim, dtype=F32) * 2.0 / HEAD_DIM)
-        angle = jnp.arange(seq_len, dtype=F32)[:, None] * frequency[None, :]
-        cosine = jnp.concatenate([jnp.cos(angle)] * 2, axis=-1)
-        sine = jnp.concatenate([-jnp.sin(angle), jnp.sin(angle)], axis=-1)
-        tables = (q_gain_own[None], k_gain_own[None], cosine, sine)
+        frequency = 10000.0 ** (-np.arange(half_dim, dtype=np.float32) * 2.0 / HEAD_DIM)
+        angle = np.arange(seq_len, dtype=np.float32)[:, None] * frequency[None, :]
+        angle = angle.astype(np.float32)
+        cosine = jnp.asarray(np.concatenate([np.cos(angle)] * 2, axis=-1), F32)
+        sine = jnp.asarray(np.concatenate([-np.sin(angle), np.sin(angle)], axis=-1), F32)
         (
             normed, q_raw, k_raw, v_low, q_rot, k_rot, mixed, stats,
-            residual, res_n, res_root, gates, x_own, all_g,
+            residual, res_n, res_root, gates, x_own, gain_rows, head_gains, all_g,
         ) = run_attend(
-            seqs, n_dp, layers, group_input, full_attn_gain[None], qkv, *tables, wo,
-            full_ffn_gain[None], router_wide, hits_wide, sent,
-        )
+            seqs, n_dp, layers, group_input, small, qkv, cosine, sine, wo, hits_wide, sent
+        )
+        full_attn_gain, full_ffn_gain = gain_rows[0], gain_rows[3]
         all_g = all_g.reshape((n_dev,) + sent.shape)
         res_root, gates_dense, normed2 = res_root[:, :1], gates[:, :experts], x_own[:, :width]
 
@@ -1800,7 +1806,7 @@
         )
         grad_normed, grad_qkv, grad_o, small_grads = run_back(
             seqs, n_dp, layers, gao, wo, mixed, q_rot, k_rot, v_low, normed, q_raw, k_raw, stats,
-            *tables, qkv, group_input, early,
+            head_gains, cosine, sine, qkv, group_input, early,
         )
         own_input = layer_input.astype(F32)
         in_root = inv_rms(own_input)

time: 702 us -> 692 us (0.986)
  other arithmetic: 23.9 us -> 14.6 us
where the time goes in v6:
time: 692 us; the launch traced here: 684 us
  Pallas kernels  641 us (93%)
  between operations  14.8 us (2%)
  other arithmetic  14.6 us (2%)
  local copies, waits for them, and re-layouts  9.52 us (1%)
    pallas_call x1, Pallas kernels, run_experts(): pl.pallas_call(functools.partial(experts_kernel, n_dp, experts), out_shap...  274 us
    pallas_call x1, Pallas kernels, run_back(): pl.pallas_call(functools.partial(back_kernel, n_dp, layers, seqs), out_sh...  119 us
    pallas_call x1, Pallas kernels, run_attend(): pl.pallas_call(functools.partial(attend_kernel, n_dp, layers, seqs), out_...  101 us
    pallas_call x1, Pallas kernels, run_front(): pl.pallas_call(functools.partial(front_kernel, n_dp, layers), out_shape=(...  99.1 us
    pallas_call x1, Pallas kernels, run_weights(): pl.pallas_call(weights_kernel, grid=(local, total // tile), out_shape=(ja...  48 us
  transfers between devices with their start and end apart: 1, of which 0 were waited for; matrix products, arithmetic and copies ran while one was open for 1% of the time, Pallas kernels for 7%

profile of v6, /device:TPU:0, one launch (start us, length us, event | category | flops | bytes accessed | tf_op | source)
XLA Modules:
  0.0 684.1 jit_solution(2283552945780878626)
XLA Ops:
  7.2 0.7 fusion.12
  8.1 0.7 pad_maximum_fusion
  9.3 0.6 pad_convert_fusion.hits
  10.0 1.9 fusion.8.g_own
  11.9 1.4 maximum_maximum_fusion.1.small
  13.3 99.1 %shard_map.272 = (bf16[8,128,2048]{2,1,0:T(8,128)(2,1)}, bf16[3,4,512,256]{3,2,1,0:T(8,128)(2,1)}, bf16[4,64,2048]{2,1,0:T(8,128)(2,1)}, bf16[4,8,64,128]{3,2,1,...) custom-call(bf16[128,2048]{1,0:T(8,128)(2,1)} %x_own.1, bf16[64,2048]{1,0:T(8,128)(2,1)} %w_q.1, ...), custom_call_target="tpu_custom_call" | custom-call | tf_op jit(solution)/shard_map/pallas_call | solution.py:1132
  112.4 101.4 %shard_map.273 = (bf16[1024,2048]{1,0:T(8,128)(2,1)}, f32[1024,256]{1,0:T(8,128)}, f32[1024,256]{1,0:T(8,128)}, bf16[1024,256]{1,0:T(8,128)(2,1)}, bf16[1024,256...) custom-call(bf16[1024,2048]{1,0:T(8,128)(2,1)} %bitcast.30, ...), custom_call_target="tpu_custom_call" | custom-call | tf_op jit(solution)/shard_map/pallas_call | solution.py:1387
  213.8 1.5 slice_reduce_fusion
  215.3 1.5 fusion.16
  216.8 274.1 %shard_map.274 = (f32[128,2048]{1,0:T(8,128)}, f32[128,2176]{1,0:T(8,128)}, bf16[8,32,32,2048]{3,2,1,0:T(8,128)(2,1)}, bf16[8,32,32,2048]{3,2,1,0:T(8,128)(2,1)}...) custom-call(bf16[128,2176]{1,0:T(8,128)(2,1)} %get-tuple-element.52., ...), custom_call_target="tpu_custom_call" | custom-call | flops 51539607552 | bytes 209715200 | tf_op jit(solution)/shard_map/pallas_call | solution.py:593
  490.9 1.0 multiply_reduce_fusion.2
  492.0 2.3 multiply_reduce_fusion
  494.3 1.0 copy-done.1
  495.4 2.5 fusion.15
  498.3 1.4 fusion.10
  499.7 1.2 maximum_maximum_fusion.early
  500.8 0.9 add_convert_fusion
  501.7 48.0 %shard_map.276 = (f32[8,2048,256]{2,1,0:T(8,128)}, f32[8,2048,256]{2,1,0:T(8,128)}, f32[8,256,2048]{2,1,0:T(8,128)}) custom-call(bf16[8,1024,2048]{2,1,0:T(8,128)(2,1)} %bitcast.51, bf16[8,1024,2048]{2,1,0:T(8,128)(2,1)} %bitcast.52, bf16[3,8,1024,256]{3,2,1,0:T(8,128)(2,1)} %get-tuple-element.76.acts), custom_call_target="tpu_custom_call" | custom-call | flops 25769803776 | bytes 136314880 | tf_op jit(solution)/shard_map/pallas_call | solution.py:666
  549.8 118.8 %shard_map.275 = (f32[128,2048]{1,0:T(8,128)}, f32[3,64,2048]{2,1,0:T(8,128)}, f32[64,2048]{1,0:T(8,128)}, f32[64,128]{1,0:T(8,128)}) custom-call(bf16[1024,2048]{1,0:T(8,128)(2,1)} %all-gather.2.cloned.1.call-done.gao, bf16[256,2048]{1,0:T(8,128)(2,1)} %bitcast.35, bf16[1024,256]{1,0:T(8,128)(2,1)} %get-tuple-element.61.mixed, ...), custom_call_target="tpu_custom_call" | custom-call | tf_op jit(solution)/shard_map/pallas_call | solution.py:1691
  668.7 2.7 slice_bitcast_fusion
  671.4 1.6 fusion.3
  673.0 1.6 fusion.6
  674.6 0.7 slice_reduce_fusion.1
  675.4 0.8 copy.57
  (52 shorter events, 1.8 us)
Async XLA Ops:
  7.2 542.6 %all-gather.2.cloned.1.call-start = ((), (), s32[]{:S(2)}) async-start(), calls=%async_computation | async-start | bytes 4718592 | tf_op jit(solution)/shard_map/all_gather | solution.py:1798
  8.1 1.2 copy-start.11
  490.9 7.1 %copy-start.3 = (bf16[128,2048]{1,0:T(8,128)(2,1)S(1)}, bf16[128,2048]{1,0:T(8,128)(2,1)}, u32[]{:S(2)}) copy-start(bf16[128,2048]{1,0:T(8,128)(2,1)} %x_own.1) | copy-start | bytes 1572868
  490.9 7.3 %copy-start.9 = (f32[128,128]{1,0:T(8,128)S(1)}, f32[128,128]{1,0:T(8,128)}, u32[]{:S(2)}) copy-start(f32[128,128]{1,0:T(8,128)} %get-tuple-element.58) | copy-start | bytes 196612
  490.9 7.3 %copy-start.12 = (pred[128,64]{1,0:T(32,128)(4,1)S(1)}, pred[128,64]{1,0:T(32,128)(4,1)}, u32[]{:S(2)}) copy-start(pred[128,64]{1,0:T(32,128)(4,1)} %copy-done.11) | copy-start | bytes 24580
  494.3 1.1 copy-start.1
  494.3 6.5 copy-start.6
  494.3 6.5 copy-start.7
  549.8 121.6 %copy-start.14 = (f32[1,2048]{1,0:T(1,128)S(1)}, f32[1,2048]{1,0:T(1,128)}, u32[]{:S(2)}) copy-start(f32[1,2048]{1,0:T(1,128)} %get-tuple-element.89) | copy-start | bytes 24580
  668.6 4.4 copy-start
  668.6 4.4 copy-start.2
  668.6 4.4 copy-start.4
  668.6 4.3 copy-start.5
  668.6 4.3 copy-start.13
  668.7 4.3 copy-start.15
  671.3 3.3 copy-start.8
  671.4 4.0 copy-start.10
Sparse Core Ops, SparseCore 0:
  498.0 51.1 all-gather.1
